TPU v7x, 32 devices: a whole 2x2x4 slice. The times are simulated.
32 devices in a mesh: group: 2 (over y), area: 4 (over z), region: 2 (over x), scen: 2 (over core).
Axes of the slice: x: 2, y: 2, z: 4, core: 2. Of those that a mesh axis runs over, the one named last changes fastest.
Arguments:
- kkt_inverse: float32 [8, 256, 256], P(('area', 'region')), may hold values from -1 to 1
- scen_load: float32 [8, 256, 1024], P(('area', 'region'), None, ('group', 'scen')), parts along dimension 2, may hold values from -12 to 12
- capacity: float32 [8, 256], P(('area', 'region')), may hold values from 0.3 to 3
- pair_active: int32 [8, 6], P(('area', 'region')), may hold values from 0 to 1, as said below
- tie_counts: int32 [8, 6], P(('area', 'region')), may hold values from 64 to 384, as said below
- line_index: int32 [8, 6, 384], P(('area', 'region')), may hold values from 0 to 127
- area_zone: int32 [8], P(('area', 'region')), may hold values from 0 to 3
Outputs:
- injection: float32 [8, 256, 1024], P(('area', 'region'), None, ('group', 'scen')), parts along dimension 2
- tie_flow: float32 [8, 6, 384, 1024], P(('area', 'region'), None, None, ('group', 'scen')), parts along dimension 3
- zone_prices: float32 [8, 1024], P('region', ('group', 'scen')), parts along dimension 1
There are 2 independent parts, one for each index of `group`. A program takes and returns all parts, laid end to end along the dimension named above; an argument that names none is the same for every part. Nothing has to cross between parts.
Inputs may be any that keep to these rules, and one draw needn't show every extreme that they name: `pair_active`: for every area and slot, the neighbour that the slot points to holds the same value on the slot that points back; the pair with 384 lines and one with 64 lines are always present. `tie_counts`: equal on both ends of a pair, as for pair_active.
All inputs are finite; a program needn't handle non-finite values.
Results may differ from a plain program's by a relative error of at most 0.0001.
Values sent between devices are 32-bit elements; how exact they have to be, the bound alone decides.
No kernel may reach another device: no remote copies, remote signals or barrier semaphores. Data moves between devices by JAX's collectives and lax.ppermute only.
A program may use at most 64 MiB of HBM per device.

v0:
```python
import jax
import jax.numpy as jnp
from jax import lax
from jax.sharding import PartitionSpec as P

ZONES = 4
INNER = 24
ROUNDS = 2


PENALTY = 1.0
ZONE_GAIN = 0.004
SYSTEM_GAIN = 0.001
NEIGHBOURS = (
    ("area", 1, 1),
    ("area", -1, 0),
    ("area", 2, 3),
    ("area", -2, 2),
    ("region", 1, 5),
    ("region", -1, 4),
)


def shifted(shard, axis, by):
    length = lax.axis_size(axis)
    return lax.ppermute(shard, axis, [(i, (i + by) % length) for i in range(length)])


def fetch_area_lines(values, offset):
    return shifted(values, "area", offset)


def fetch_region_lines(values, offset):
    return shifted(values, "region", offset)


def body(kkt_inverse, scen_load, capacity, pair_active, tie_counts, line_index, area_zone):
    inverse = kkt_inverse[0]
    demand = scen_load[0]
    limits = capacity[0][:, None]
    bus_count, scen_count = demand.shape
    slot_count, line_most = (line_index.shape[1], line_index.shape[2])
    positions = jnp.arange(line_most, dtype=jnp.int32)
    live_mask = (
        (pair_active[0][:, None] > 0) & (positions[None, :] < tie_counts[0][:, None])
    ).astype(jnp.float32)[:, :, None]
    side_sign = jnp.array([1.0, -1.0, 1.0, -1.0, 1.0, -1.0], jnp.float32)[:, None, None]
    line_rows = line_index[0]
    flat_index = line_rows.reshape(-1)
    own_onehot = (jnp.arange(bus_count, dtype=jnp.int32)[:, None] == flat_index[None, :]).astype(
        jnp.float32
    )
    my_zone = area_zone[0]
    zone_ids = jnp.arange(ZONES, dtype=jnp.int32)[:, None]
    zone_price = jnp.zeros((ZONES, scen_count), jnp.float32)
    system_price = jnp.zeros((scen_count,), jnp.float32)
    tie_flow = jnp.zeros((slot_count, line_most, scen_count), jnp.float32)
    duals = jnp.zeros((slot_count, line_most, scen_count), jnp.float32)
    clipped = jnp.zeros((bus_count, scen_count), jnp.float32)
    scaled = jnp.zeros((bus_count, scen_count), jnp.float32)
    solution = jnp.zeros((bus_count, scen_count), jnp.float32)
    for round_index in range(ROUNDS):
        area_price = jnp.sum(jnp.where(zone_ids == my_zone, zone_price, 0.0), axis=0) + system_price
        coupling_term = (PENALTY * side_sign * (tie_flow - duals)).reshape(-1, scen_count)
        coupling = jnp.dot(
            own_onehot,
            coupling_term,
            precision=lax.Precision.HIGHEST,
            preferred_element_type=jnp.float32,
        )
        linear = demand - area_price[None, :] + coupling

        def box_sweep(step_index, state):
            solution, clipped, scaled = state
            solution = jnp.dot(
                inverse,
                linear + clipped - scaled,
                precision=lax.Precision.HIGHEST,
                preferred_element_type=jnp.float32,
            )
            clipped = jnp.clip(solution + scaled, -limits, limits)
            scaled = scaled + solution - clipped
            return (solution, clipped, scaled)

        solution, clipped, scaled = lax.fori_loop(0, INNER, box_sweep, (solution, clipped, scaled))
        picked = lax.dot_general(
            own_onehot,
            solution,
            (((0,), (0,)), ((), ())),
            precision=lax.Precision.HIGHEST,
            preferred_element_type=jnp.float32,
        )
        own_view = side_sign * picked.reshape(slot_count, line_most, scen_count)
        own_offer = own_view + duals
        received = []
        for axis_name, offset, reverse in NEIGHBOURS:
            if axis_name == "area":
                received.append(fetch_area_lines(own_offer[reverse], -offset))
            else:
                received.append(fetch_region_lines(own_offer[reverse], -offset))
        peer_offer = jnp.stack(received)
        tie_flow = live_mask * (0.5 * (own_offer + peer_offer))
        duals = live_mask * (own_offer - tie_flow)
        mismatch = jnp.sum(solution, axis=0) - jnp.sum(side_sign * tie_flow, axis=(0, 1))
        zone_terms = jnp.where(zone_ids == my_zone, mismatch[None, :], 0.0)
        zone_sum = lax.psum(zone_terms, "area")
        system_total = lax.psum(jnp.sum(zone_sum, axis=0), "region")
        zone_price = zone_price + ZONE_GAIN * zone_sum
        system_price = system_price + SYSTEM_GAIN * system_total
    return (solution[None], tie_flow[None], zone_price + system_price[None, :])


def solution(mesh):
    placed = (
        P(("area", "region"), None, None),
        P(("area", "region"), None, ("group", "scen")),
        P(("area", "region"), None),
        P(("area", "region"), None),
        P(("area", "region"), None),
        P(("area", "region"), None, None),
        P(("area", "region")),
    )
    return jax.shard_map(
        body,
        mesh=mesh,
        in_specs=placed,
        out_specs=(
            P(("area", "region"), None, ("group", "scen")),
            P(("area", "region"), None, None, ("group", "scen")),
            P("region", ("group", "scen")),
        ),
        check_vma=False,
    )
```

profile of v0, /device:TPU:0, one launch (start us, length us, event | category | flops | bytes accessed | tf_op | source)
XLA Modules:
  0.0 231.3 jit_solution(5499373148461394943)
XLA Ops:
  2.2 2.4 %fusion.32 = f32[256,256]{1,0:T(8,128)S(1)} fusion(f32[2304]{0:T(1024)S(1)} %mul.173, s32[2304]{0:T(1024)S(1)} %eq.33, f32[1,256,256]{2,1,0:T(8,128)} %param.13), kind=kOutput, calls=%fused_computation.42 | convolution fusion | flops 1812594688 | bytes 542720 | tf_op jit(solution)/shard_map/dot_general | solution.py:65
  4.7 28.2 %while.32 = (s32[]{:T(128)}, f32[256,256]{0,1:T(8,128)}, f32[256,256]{0,1:T(8,128)S(1)}, f32[256,256]{0,1:T(8,128)S(1)}, f32[256,256]{0,1:T(8,128)S(1)}, /*index...) while((s32[]{:T(128)}, f32[256,256]{0,1:T(8,128)}, ...), condition=%wide.region_1.2_spmd.clone, body=%wide.region_0.1_spmd.clone.sunk | while | flops 201916416 | bytes 2885743 | solution.py:85
  32.9 2.4 %fusion.20 = f32[2304,256]{1,0:T(8,128)S(1)} fusion(f32[256,256]{0,1:T(8,128)} %get-tuple-element.394, s32[2304]{0:T(1024)S(1)} %eq.33), kind=kOutput, calls=%fused_computation.32 | convolution fusion | flops 1813118976 | bytes 2630656 | tf_op jit(solution)/shard_map/dot_general | solution.py:86
  37.1 5.0 %collective-permute-start = (f32[384,256]{1,0:T(8,128)}, f32[384,256]{1,0:T(8,128)}, u32[]{:S(2)}, u32[]{:S(2)}) collective-permute-start(f32[384,256]{1,0:T(8,128)} %get-tuple-element.256), channel_id=1, source_target_pairs={{0,12},{4,0},{8,4},{12,8},{1,13},{5,1},{9,5},{13,9},{2,14},{6,2},{... | collective-permute-start | bytes 1179656 | tf_op jit(solution)/shard_map/ppermute | solution.py:26
  47.8 4.1 %collective-permute-done = f32[384,256]{1,0:T(8,128)} collective-permute-done((f32[384,256]{1,0:T(8,128)}, f32[384,256]{1,0:T(8,128)}, u32[]{:S(2)}, u32[]{:S(2)}) %collective-permute-start) | collective-permute-done | bytes 393248 | tf_op jit(solution)/shard_map/ppermute | solution.py:26
  54.5 6.9 %collective-permute-done.1 = f32[384,256]{1,0:T(8,128)} collective-permute-done((f32[384,256]{1,0:T(8,128)}, f32[384,256]{1,0:T(8,128)}, u32[]{:S(2)}, u32[]{:S(2)}) %collective-permute-start.1) | collective-permute-done | bytes 393248 | tf_op jit(solution)/shard_map/ppermute | solution.py:26
  62.4 23.1 %collective-permute-done.2 = f32[384,256]{1,0:T(8,128)} collective-permute-done((f32[384,256]{1,0:T(8,128)}, f32[384,256]{1,0:T(8,128)}, u32[]{:S(2)}, u32[]{:S(2)}) %collective-permute-start.2) | collective-permute-done | bytes 393248 | tf_op jit(solution)/shard_map/ppermute | solution.py:26
  86.6 6.3 %collective-permute-done.3 = f32[384,256]{1,0:T(8,128)} collective-permute-done((f32[384,256]{1,0:T(8,128)}, f32[384,256]{1,0:T(8,128)}, u32[]{:S(2)}, u32[]{:S(2)}) %collective-permute-start.3) | collective-permute-done | bytes 393248 | tf_op jit(solution)/shard_map/ppermute | solution.py:26
  95.7 2.3 multiply_reduce_fusion
  98.1 11.0 %psum.28 = f32[4,256]{1,0:T(4,128)S(1)} all-reduce(f32[4,256]{1,0:T(4,128)S(1)} %broadcast_select_fusion.1), channel_id=1, replica_groups=mesh['group'=2,'area'=4,'region'=2,'scen'=2] {'area'}, use_global_device_ids=true, to_apply=%region_4.5 | all-reduce | flops 1024 | bytes 8192 | tf_op jit(solution)/shard_map/psum | solution.py:106
  109.2 4.9 %psum.29 = f32[256]{0:T(256)S(1)} all-reduce(f32[256]{0:T(256)S(1)} %get-tuple-element.203), channel_id=1, replica_groups=mesh['group'=2,'area'=4,'region'=2,'scen'=2] {'region'}, use_global_device_ids=true, to_apply=%region_7.8 | all-reduce | flops 256 | bytes 2048 | tf_op jit(solution)/shard_map/psum | solution.py:107
  114.1 4.4 %fusion.29 = f32[256,256]{1,0:T(8,128)} fusion(f32[2304,256]{1,0:T(8,128)} %get-tuple-element.242, f32[2304,256]{1,0:T(8,128)S(1)} %fusion.20, f32[2304]{0:T(1024)S(1)} %and_convert_fusion, f32[2304]{0:T(1024)S(1)} %mul.176, s32[2304]{0:T(1024)S(1)} %eq.33, f32[1,256,256]{2,1,0:T(8,128)S(1)} %copy-done.16, f32[256]{0:T(256)S(1)} %multiply_add_fusion.2), kind=kOutput, calls=%fused_computation.41 | convolution fusion | flops 1815609344 | bytes 5271552 | tf_op jit(solution)/shard_map/dot_general | solution.py:65
  119.6 28.1 %while.31 = (s32[]{:T(128)}, f32[256,256]{0,1:T(8,128)}, f32[256,256]{0,1:T(8,128)S(1)}, f32[256,256]{0,1:T(8,128)S(1)}, f32[256,256]{0,1:T(8,128)S(1)}, /*index...) while((s32[]{:T(128)}, f32[256,256]{0,1:T(8,128)}, ...), condition=%wide.region_9.10_spmd, body=%wide.region_8.9_spmd.sunk | while | flops 201719808 | bytes 2885725 | solution.py:85
  147.7 3.9 %fusion.18 = f32[2304,256]{1,0:T(8,128)} fusion(f32[256,256]{0,1:T(8,128)} %get-tuple-element.144, s32[2304]{0:T(1024)S(1)} %eq.33), kind=kOutput, calls=%fused_computation.31 | convolution fusion | flops 1813118976 | bytes 2630656 | tf_op jit(solution)/shard_map/dot_general | solution.py:86
  153.1 2.7 %multiply_add_fusion = f32[6,384,256]{2,1,0:T(8,128)S(1)} fusion(f32[6,384,256]{2,1,0:T(8,128)} %copy-done.4, f32[6,384,256]{2,1,0:T(8,128)} %bitcast.132, f32[6,384]{1,0:T(8,128)S(1)} %fusion.36, f32[6,384]{1,0:T(8,128)S(1)} %fusion.37, f32[6]{0:T(128)S(1)} %copy-done.26, f32[6,384,256]{2,1,0:T(8,128)S(1)} %bitcast.130), kind=kLoop, calls=%fused_computation.22 | loop fusion | flops 4128768 | bytes 9455640 | tf_op jit(solution)/shard_map/add | solution.py:94
  156.1 2.0 collective-permute-start.7
  158.1 2.9 %collective-permute-start.9 = (f32[384,256]{1,0:T(8,128)S(1)}, f32[384,256]{1,0:T(8,128)S(1)}, u32[]{:S(2)}, u32[]{:S(2)}) collective-permute-start(f32[384,256]{1,0:T(8,128)S(1)} %get-tuple-element.247), channel_id=1, source_target_pairs={{0,8},{4,12},{8,0},{12,4},{1,9},{5,13},{9,1},{13,5},{2,10},{6,14},... | collective-permute-start | bytes 1179656 | tf_op jit(solution)/shard_map/ppermute | solution.py:26
  167.7 3.4 %collective-permute-done.6 = f32[384,256]{1,0:T(8,128)S(1)} collective-permute-done((f32[384,256]{1,0:T(8,128)S(1)}, f32[384,256]{1,0:T(8,128)S(1)}, u32[]{:S(2)}, u32[]{:S(2)}) %collective-permute-start.6) | collective-permute-done | bytes 393248 | tf_op jit(solution)/shard_map/ppermute | solution.py:26
  172.6 3.0 %collective-permute-done.7 = f32[384,256]{1,0:T(8,128)S(1)} collective-permute-done((f32[384,256]{1,0:T(8,128)S(1)}, f32[384,256]{1,0:T(8,128)S(1)}, u32[]{:S(2)}, u32[]{:S(2)}) %collective-permute-start.7) | collective-permute-done | bytes 393248 | tf_op jit(solution)/shard_map/ppermute | solution.py:26
  175.6 24.0 %collective-permute-done.8 = f32[384,256]{1,0:T(8,128)S(1)} collective-permute-done((f32[384,256]{1,0:T(8,128)S(1)}, f32[384,256]{1,0:T(8,128)S(1)}, u32[]{:S(2)}, u32[]{:S(2)}) %collective-permute-start.8) | collective-permute-done | bytes 393248 | tf_op jit(solution)/shard_map/ppermute | solution.py:26
  199.6 4.2 %collective-permute-done.9 = f32[384,256]{1,0:T(8,128)S(1)} collective-permute-done((f32[384,256]{1,0:T(8,128)S(1)}, f32[384,256]{1,0:T(8,128)S(1)}, u32[]{:S(2)}, u32[]{:S(2)}) %collective-permute-start.9) | collective-permute-done | bytes 393248 | tf_op jit(solution)/shard_map/ppermute | solution.py:26
  207.3 11.3 %psum.30 = f32[4,256]{1,0:T(4,128)S(1)} all-reduce(f32[4,256]{1,0:T(4,128)S(1)} %broadcast_select_fusion), channel_id=1, replica_groups=mesh['group'=2,'area'=4,'region'=2,'scen'=2] {'area'}, use_global_device_ids=true, to_apply=%region_12.13 | all-reduce | flops 1024 | bytes 8192 | tf_op jit(solution)/shard_map/psum | solution.py:106
  218.6 4.9 %psum.31 = f32[256]{0:T(256)S(1)} all-reduce(f32[256]{0:T(256)S(1)} %reduce_sum.73), channel_id=1, replica_groups=mesh['group'=2,'area'=4,'region'=2,'scen'=2] {'region'}, use_global_device_ids=true, to_apply=%region_14.15 | all-reduce | flops 256 | bytes 2048 | tf_op jit(solution)/shard_map/psum | solution.py:107
  228.4 2.8 %add_multiply_fusion = f32[1,6,384,256]{3,2,1,0:T(8,128)} fusion(f32[1,6,384,256]{3,2,1,0:T(8,128)S(1)} %bitcast_dynamic-update-slice_fusion.6, f32[1,6,384,256]{3,2,1,0:T(8,128)S(1)} %copy-done.8, f32[1,6,384,256]{3,2,1,0:T(8,128)S(1)} %bitcast.131, f32[1,6,384,256]{3,2,1,0:T(8,128)S(1)} %bitcast.133, f32[6,384]{1,0:T(8,128)S(1)} %copy-done.23, ...), kind=kLoop, calls=%fused_computation.21 | loop fusion | flops 5308416 | bytes 11814936 | tf_op jit(solution)/shard_map/mul | solution.py:102
  (289 shorter events, 90.9 us)
Async XLA Ops:
  37.1 14.9 %collective-permute-start = (f32[384,256]{1,0:T(8,128)}, f32[384,256]{1,0:T(8,128)}, u32[]{:S(2)}, u32[]{:S(2)}) collective-permute-start(f32[384,256]{1,0:T(8,128)} %get-tuple-element.256), channel_id=1, source_target_pairs={{0,12},{4,0},{8,4},{12,8},{1,13},{5,1},{9,5},{13,9},{2,14},{6,2},{... | collective-permute-start | bytes 1179656 | tf_op jit(solution)/shard_map/ppermute | solution.py:26
  42.1 19.3 %collective-permute-start.1 = (f32[384,256]{1,0:T(8,128)}, f32[384,256]{1,0:T(8,128)}, u32[]{:S(2)}, u32[]{:S(2)}) collective-permute-start(f32[384,256]{1,0:T(8,128)} %get-tuple-element.255), channel_id=1, source_target_pairs={{0,4},{4,8},{8,12},{12,0},{1,5},{5,9},{9,13},{13,1},{2,6},{6,10},{... | collective-permute-start | bytes 1179656 | tf_op jit(solution)/shard_map/ppermute | solution.py:26
  42.1 43.4 %collective-permute-start.2 = (f32[384,256]{1,0:T(8,128)}, f32[384,256]{1,0:T(8,128)}, u32[]{:S(2)}, u32[]{:S(2)}) collective-permute-start(f32[384,256]{1,0:T(8,128)} %get-tuple-element.254), channel_id=1, source_target_pairs={{0,8},{4,12},{8,0},{12,4},{1,9},{5,13},{9,1},{13,5},{2,10},{6,14},... | collective-permute-start | bytes 1179656 | tf_op jit(solution)/shard_map/ppermute | solution.py:26
  43.1 49.7 %collective-permute-start.3 = (f32[384,256]{1,0:T(8,128)}, f32[384,256]{1,0:T(8,128)}, u32[]{:S(2)}, u32[]{:S(2)}) collective-permute-start(f32[384,256]{1,0:T(8,128)} %get-tuple-element.253), channel_id=1, source_target_pairs={{0,8},{4,12},{8,0},{12,4},{1,9},{5,13},{9,1},{13,5},{2,10},{6,14},... | collective-permute-start | bytes 1179656 | tf_op jit(solution)/shard_map/ppermute | solution.py:26
  45.0 48.8 %collective-permute-start.4 = (f32[384,256]{1,0:T(8,128)}, f32[384,256]{1,0:T(8,128)}, u32[]{:S(2)}, u32[]{:S(2)}) collective-permute-start(f32[384,256]{1,0:T(8,128)} %get-tuple-element.252), channel_id=1, source_target_pairs={{0,2},{2,0},{1,3},{3,1},{4,6},{6,4},{5,7},{7,5},{8,10},{10,8},{9,1... | collective-permute-start | bytes 1179656 | tf_op jit(solution)/shard_map/ppermute | solution.py:26
  46.8 48.9 %copy-start.18 = (f32[2304]{0:T(1024)}, f32[2304]{0:T(1024)S(1)}, u32[]{:S(2)}) copy-start(f32[2304]{0:T(1024)S(1)} %and_select_fusion) | copy-start | bytes 27652
  46.8 67.3 %copy-start.20 = (f32[2304]{0:T(1024)}, f32[2304]{0:T(1024)S(1)}, u32[]{:S(2)}) copy-start(f32[2304]{0:T(1024)S(1)} %and_convert_fusion) | copy-start | bytes 27652
  46.9 106.2 %copy-start.22 = (f32[6,384]{1,0:T(8,128)}, f32[6,384]{1,0:T(8,128)S(1)}, u32[]{:S(2)}) copy-start(f32[6,384]{1,0:T(8,128)S(1)} %fusion.36) | copy-start | bytes 27652
  47.0 106.1 %copy-start.24 = (f32[6,384]{1,0:T(8,128)}, f32[6,384]{1,0:T(8,128)S(1)}, u32[]{:S(2)}) copy-start(f32[6,384]{1,0:T(8,128)S(1)} %fusion.37) | copy-start | bytes 27652
  47.8 61.3 %copy-start.28 = (pred[4]{0:T(512)(128)(4,1)}, pred[4]{0:T(512)(128)(4,1)S(1)}, u32[]{:S(2)}) copy-start(pred[4]{0:T(512)(128)(4,1)S(1)} %iota_compare_fusion.8) | copy-start | bytes 16
  51.9 42.9 %collective-permute-start.5 = (f32[384,256]{1,0:T(8,128)}, f32[384,256]{1,0:T(8,128)S(1)}, u32[]{:S(2)}, u32[]{:S(2)}) collective-permute-start(f32[384,256]{1,0:T(8,128)} %get-tuple-element.251), channel_id=1, source_target_pairs={{0,2},{2,0},{1,3},{3,1},{4,6},{6,4},{5,7},{7,5},{8,10},{10,8},{9,1... | collective-permute-start | bytes 1179656 | tf_op jit(solution)/shard_map/ppermute | solution.py:26
  95.7 18.4 %copy-start.16 = (f32[1,256,256]{2,1,0:T(8,128)S(1)}, f32[1,256,256]{2,1,0:T(8,128)}, u32[]{:S(2)}) copy-start(f32[1,256,256]{2,1,0:T(8,128)} %param.13) | copy-start | bytes 786436
  156.0 15.1 %collective-permute-start.6 = (f32[384,256]{1,0:T(8,128)S(1)}, f32[384,256]{1,0:T(8,128)S(1)}, u32[]{:S(2)}, u32[]{:S(2)}) collective-permute-start(f32[384,256]{1,0:T(8,128)S(1)} %get-tuple-element.250), channel_id=1, source_target_pairs={{0,12},{4,0},{8,4},{12,8},{1,13},{5,1},{9,5},{13,9},{2,14},{6,2},{... | collective-permute-start | bytes 1179656 | tf_op jit(solution)/shard_map/ppermute | solution.py:26
  156.1 19.5 %collective-permute-start.7 = (f32[384,256]{1,0:T(8,128)S(1)}, f32[384,256]{1,0:T(8,128)S(1)}, u32[]{:S(2)}, u32[]{:S(2)}) collective-permute-start(f32[384,256]{1,0:T(8,128)S(1)} %get-tuple-element.249), channel_id=1, source_target_pairs={{0,4},{4,8},{8,12},{12,0},{1,5},{5,9},{9,13},{13,1},{2,6},{6,10},{... | collective-permute-start | bytes 1179656 | tf_op jit(solution)/shard_map/ppermute | solution.py:26
  158.1 41.5 %collective-permute-start.8 = (f32[384,256]{1,0:T(8,128)S(1)}, f32[384,256]{1,0:T(8,128)S(1)}, u32[]{:S(2)}, u32[]{:S(2)}) collective-permute-start(f32[384,256]{1,0:T(8,128)S(1)} %get-tuple-element.248), channel_id=1, source_target_pairs={{0,8},{4,12},{8,0},{12,4},{1,9},{5,13},{9,1},{13,5},{2,10},{6,14},... | collective-permute-start | bytes 1179656 | tf_op jit(solution)/shard_map/ppermute | solution.py:26
  158.1 45.7 %collective-permute-start.9 = (f32[384,256]{1,0:T(8,128)S(1)}, f32[384,256]{1,0:T(8,128)S(1)}, u32[]{:S(2)}, u32[]{:S(2)}) collective-permute-start(f32[384,256]{1,0:T(8,128)S(1)} %get-tuple-element.247), channel_id=1, source_target_pairs={{0,8},{4,12},{8,0},{12,4},{1,9},{5,13},{9,1},{13,5},{2,10},{6,14},... | collective-permute-start | bytes 1179656 | tf_op jit(solution)/shard_map/ppermute | solution.py:26
  161.0 42.9 %collective-permute-start.10 = (f32[384,256]{1,0:T(8,128)S(1)}, f32[384,256]{1,0:T(8,128)S(1)}, u32[]{:S(2)}, u32[]{:S(2)}) collective-permute-start(f32[384,256]{1,0:T(8,128)S(1)} %get-tuple-element.246), channel_id=1, source_target_pairs={{0,2},{2,0},{1,3},{3,1},{4,6},{6,4},{5,7},{7,5},{8,10},{10,8},{9,1... | collective-permute-start | bytes 1179656 | tf_op jit(solution)/shard_map/ppermute | solution.py:26
  167.6 37.9 %copy-start.19 = (f32[2304]{0:T(1024)S(1)}, f32[2304]{0:T(1024)}, u32[]{:S(2)}) copy-start(f32[2304]{0:T(1024)} %copy-done.18) | copy-start | bytes 27652
  167.7 37.9 %copy-start.21 = (f32[2304]{0:T(1024)S(1)}, f32[2304]{0:T(1024)}, u32[]{:S(2)}) copy-start(f32[2304]{0:T(1024)} %copy-done.20) | copy-start | bytes 27652
  167.7 36.2 %copy-start.7 = (f32[1,6,384,256]{3,2,1,0:T(8,128)}, f32[1,6,384,256]{3,2,1,0:T(8,128)S(1)}, u32[]{:S(2)}) copy-start(f32[1,6,384,256]{3,2,1,0:T(8,128)S(1)} %bitcast_dynamic-update-slice_fusion.12) | copy-start | bytes 7077892
  171.1 34.5 %copy-start.3 = (f32[2304,256]{1,0:T(8,128)S(1)}, f32[2304,256]{1,0:T(8,128)}, u32[]{:S(2)}) copy-start(f32[2304,256]{1,0:T(8,128)} %get-tuple-element.242) | copy-start | bytes 7077892
  171.1 34.5 %copy-start = (f32[2304,256]{1,0:T(8,128)S(1)}, f32[2304,256]{1,0:T(8,128)}, u32[]{:S(2)}) copy-start(f32[2304,256]{1,0:T(8,128)} %fusion.18) | copy-start | bytes 7077892
  171.1 32.8 %collective-permute-start.11 = (f32[384,256]{1,0:T(8,128)S(1)}, f32[384,256]{1,0:T(8,128)S(1)}, u32[]{:S(2)}, u32[]{:S(2)}) collective-permute-start(f32[384,256]{1,0:T(8,128)S(1)} %get-tuple-element.245), channel_id=1, source_target_pairs={{0,2},{2,0},{1,3},{3,1},{4,6},{6,4},{5,7},{7,5},{8,10},{10,8},{9,1... | collective-permute-start | bytes 1179656 | tf_op jit(solution)/shard_map/ppermute | solution.py:26
  205.6 19.3 %copy-start.12 = (f32[384,256]{1,0:T(8,128)S(1)}, f32[384,256]{1,0:T(8,128)}, u32[]{:S(2)}) copy-start(f32[384,256]{1,0:T(8,128)} %copy-done.11) | copy-start | bytes 1179652
  (21 other events, 91.9 us)
where the time goes:
time: 232 us; the launch traced here: 231 us
  waiting for transfers between devices  75 us (32%)
  matrix products  66.9 us (29%)
  blocking collectives  32.1 us (14%)
  local copies, waits for them, and re-layouts  22.8 us (10%)
  starting transfers between devices  18.9 us (8%)
  other arithmetic  13 us (6%)
    ppermute x12, waiting for transfers between devices, shifted(): lax.ppermute(shard, axis, [(i, (i + by) % length) for i in range(length)])  75 us
    dot_general x48, matrix products, box_sweep(): jnp.dot(inverse, linear + clipped - scaled, precision=lax.Precision.HIGHE...  54 us
    psum x2, blocking collectives, body(): zone_sum = lax.psum(zone_terms, 'area')  22.3 us
    ppermute x12, starting transfers between devices, shifted(): lax.ppermute(shard, axis, [(i, (i + by) % length) for i in range(length)])  18.9 us
    unnamed x87, local copies, waits for them, and re-layouts  15.5 us
    psum x2, blocking collectives, body(): system_total = lax.psum(jnp.sum(zone_sum, axis=0), 'region')  9.85 us
    dot_general x2, matrix products, body(): jnp.dot(own_onehot, coupling_term, precision=lax.Precision.HIGHEST, prefe...  6.74 us
    dot_general x2, matrix products, body(): lax.dot_general(own_onehot, solution, (((0,), (0,)), ((), ())), precision...  6.23 us
  transfers between devices with their start and end apart: 12, of which 8 were waited for; matrix products, arithmetic and copies ran while one was open for 5% of the time, Pallas kernels for 0%

commit v1 on v0

v1 whole, which is shorter than its diff:
```python
import functools

import jax
import jax.numpy as jnp
from jax import lax
from jax.experimental import pallas as pl
from jax.experimental.pallas import tpu as pltpu
from jax.sharding import PartitionSpec as P

ZONES = 4
INNER = 24
BOUNDARY = 128
LANES = 128
ZONE_GAIN = 0.004
SYSTEM_GAIN = 0.001
SLOTS = (
    ("area", 1, 1),
    ("area", -1, 0),
    ("area", 2, 3),
    ("area", -2, 2),
    ("region", 1, 5),
    ("region", -1, 4),
)
SIGNS = (1.0, -1.0, 1.0, -1.0, 1.0, -1.0)
CHAIN_ROWS = 64

F32 = jnp.float32
BF16 = jnp.bfloat16
VMEM = pl.BlockSpec(memory_space=pltpu.VMEM)
SMEM = pl.BlockSpec(memory_space=pltpu.SMEM)
PARAMS = pltpu.CompilerParams(vmem_limit_bytes=40 * 2**20)


def dot(a, b):
    return jnp.dot(a, b, preferred_element_type=F32)


def dot_nt(a, b):
    return lax.dot_general(a, b, (((1,), (1,)), ((), ())), preferred_element_type=F32)


def halves(x):
    high = x.astype(BF16)
    return high, (x - high.astype(F32)).astype(BF16)


def thirds(x):
    high = x.astype(BF16)
    rest = x - high.astype(F32)
    middle = rest.astype(BF16)
    return high, middle, (rest - middle.astype(F32)).astype(BF16)


def product(x, kh_ref, kl_ref):
    high, low = halves(x)
    return dot(high, kh_ref[...]) + dot(low, kh_ref[...]) + dot(high, kl_ref[...])


def run_sweeps(states, lin_ref, limits, kh_ref, kl_ref, count):
    injections = [None] * len(states)
    for _ in range(count):
        for i in range(len(states)):
            lin = lin_ref[pl.ds(i * CHAIN_ROWS, CHAIN_ROWS), :]
            v = states[i]
            if v is None:
                injections[i] = product(lin, kh_ref, kl_ref)
                states[i] = injections[i]
                continue
            clipped = jnp.clip(v, -limits, limits)
            over = v - clipped
            injections[i] = product(lin + (clipped - over), kh_ref, kl_ref)
            states[i] = injections[i] + over
    return injections, states


def first_kernel(k_ref, load_ref, cap_ref, idx_ref, edge_ref, rest_ref, v_ref, lin_ref, kh_ref, kl_ref):
    scens = lin_ref.shape[0]
    high, low = halves(k_ref[0].T)
    kh_ref[...] = high
    kl_ref[...] = low
    lin_ref[...] = load_ref[0].T
    slots, lines = idx_ref.shape[1:]
    pieces = lines // LANES
    edge_ref[pl.ds(scens, edge_ref.shape[0] - scens), :] = jnp.zeros((edge_ref.shape[0] - scens, LANES), F32)
    for p in range(slots):
        for j in range(pieces):
            row = idx_ref[0, pl.ds(p, 1), pl.ds(j * LANES, LANES)]
            edge_ref[pl.ds(scens + p * pieces + j, 1), :] = row.astype(F32)
    injections, states = run_sweeps([None] * (scens // CHAIN_ROWS), lin_ref, cap_ref[...], kh_ref, kl_ref, INNER)
    for i, (x, v) in enumerate(zip(injections, states)):
        rows = pl.ds(i * CHAIN_ROWS, CHAIN_ROWS)
        edge_ref[rows, :] = x[:, :BOUNDARY]
        rest_ref[rows, :] = x[:, BOUNDARY:]
        v_ref[rows, :] = v


def live_lines(active_ref, count_ref, p):
    return jnp.where(active_ref[0, p] > 0, count_ref[0, p], 0)


def peer_ident(p, areas, regions):
    axis, move, _ = SLOTS[p]
    a = lax.axis_index("area")
    r = lax.axis_index("region")
    if axis == "area":
        a = lax.rem(a + (move % areas), areas)
    else:
        r = lax.rem(r + (move % regions), regions)
    return a * regions + r


def weighted_sums(weights, edge, rest):
    wh, wl = halves(weights)
    eh, em, el = thirds(edge)
    out = dot_nt(wh[:, :BOUNDARY], eh) + dot_nt(wh[:, :BOUNDARY], em) + dot_nt(wh[:, :BOUNDARY], el)
    out = out + dot_nt(wl[:, :BOUNDARY], eh) + dot_nt(wl[:, :BOUNDARY], em)
    for part in thirds(rest):
        out = out + dot_nt(wh[:, BOUNDARY:], part)
    return out


def share_kernel(
    areas, regions, active_ref, count_ref, zone_ref, edge_ref, rest_ref, idx_ref, share_ref, own_ref, weight_ref
):
    total = areas * regions
    rows = share_ref.shape[0]
    scens = rest_ref.shape[0]
    slots, lines = idx_ref.shape[1:]
    me = lax.axis_index("area") * regions + lax.axis_index("region")
    row_id = lax.broadcasted_iota(jnp.int32, (rows, lines), 0)
    line_id = lax.broadcasted_iota(jnp.int32, (1, lines), 1)
    bus_id = lax.broadcasted_iota(jnp.int32, (BOUNDARY, lines), 0)
    weights = jnp.zeros((rows, BOUNDARY), F32)
    for p in range(slots):
        live = line_id < live_lines(active_ref, count_ref, p)
        onehot = jnp.where((bus_id == idx_ref[0, pl.ds(p, 1), :]) & live, 1.0, 0.0).astype(BF16)
        own_ref[:, pl.ds(p * lines, lines)] = onehot
        peer = peer_ident(p, areas, regions)
        coefficient = jnp.where(row_id == peer, 0.5, 0.0) - jnp.where(row_id == me, 0.5, 0.0)
        weights = weights + dot_nt(coefficient.astype(BF16), onehot)
    mine = jnp.where(lax.broadcasted_iota(jnp.int32, (rows, BOUNDARY), 0) == me, 1.0, 0.0)
    weights = jnp.concatenate([weights + mine, mine], axis=1)
    weight_ref[...] = weights
    sums = weighted_sums(weights, edge_ref[pl.ds(0, scens), :], rest_ref[...])
    scen_row = lax.broadcasted_iota(jnp.int32, (rows, scens), 0)
    zone = zone_ref[0].astype(F32)
    share_ref[...] = sums + jnp.where(scen_row == total + me, zone, 0.0)


def prices(shares, zones, total, regions, zone):
    ids = lax.broadcasted_iota(jnp.int32, shares.shape, 0)
    in_region = lax.rem(ids, regions) == lax.axis_index("region")
    gain = jnp.where(in_region & (zones == zone), ZONE_GAIN, 0.0) + SYSTEM_GAIN
    return jnp.sum(gain * shares, axis=0, keepdims=True)


def second_kernel(
    total, regions, buffer_of, zone_ref, lin_ref, v_ref, kh_ref, kl_ref, cap_ref, own_ref, shares_ref, *refs
):
    buffers = max(buffer_of) + 1
    got = refs[:buffers]
    edge_ref, rest_ref, lin2_ref = refs[buffers:]
    scens = lin_ref.shape[0]
    slots = len(buffer_of)
    lines = own_ref.shape[1] // slots
    pieces = lines // LANES
    bus_id = lax.broadcasted_iota(jnp.int32, (BOUNDARY, LANES), 0).astype(F32)
    counts = [None] * buffers
    for p in range(slots):
        b = buffer_of[p]
        for j in range(pieces):
            row = got[b][pl.ds(scens + SLOTS[p][2] * pieces + j, 1), :]
            there = jnp.where(bus_id == row, 1.0, 0.0).astype(BF16)
            met = dot_nt(own_ref[:, pl.ds(p * lines + j * LANES, LANES)], there)
            counts[b] = met if counts[b] is None else counts[b] + met
    counts_high, counts_low = halves(jnp.concatenate(counts, axis=1))
    high, low = halves(jnp.concatenate([g[pl.ds(0, scens), :] for g in got], axis=1))
    coupling = dot_nt(high, counts_high) + dot_nt(low, counts_high) + dot_nt(high, counts_low)
    shares = shares_ref[pl.ds(0, total), :]
    zones = shares_ref[pl.ds(total, total), :]
    price = prices(shares, zones, total, regions, zone_ref[0].astype(F32))
    price = jnp.broadcast_to(price, (8, scens)).T[:, 0:1]
    lin2_ref[:, pl.ds(0, BOUNDARY)] = lin_ref[:, pl.ds(0, BOUNDARY)] - price - coupling
    lin2_ref[:, pl.ds(BOUNDARY, BOUNDARY)] = lin_ref[:, pl.ds(BOUNDARY, BOUNDARY)] - price
    chains = scens // CHAIN_ROWS
    states = [v_ref[pl.ds(i * CHAIN_ROWS, CHAIN_ROWS), :] for i in range(chains)]
    injections, _ = run_sweeps(states, lin2_ref, cap_ref[...], kh_ref, kl_ref, INNER)
    for i, x in enumerate(injections):
        rows = pl.ds(i * CHAIN_ROWS, CHAIN_ROWS)
        edge_ref[rows, :] = x[:, :BOUNDARY]
        rest_ref[rows, :] = x[:, BOUNDARY:]


def again_kernel(weight_ref, edge_ref, rest_ref, share_ref, injection_ref):
    share_ref[...] = weighted_sums(weight_ref[...], edge_ref[...], rest_ref[...])
    injection_ref[0, pl.ds(0, BOUNDARY), :] = edge_ref[...].T
    injection_ref[0, pl.ds(BOUNDARY, BOUNDARY), :] = rest_ref[...].T


def table_kernel(buffer_of, scens, active_ref, count_ref, own_ref, *refs):
    got = refs[:-1]
    table_ref = refs[-1]
    slots, lines = table_ref.shape[:2]
    pieces = lines // LANES
    extra = own_ref.shape[0] - scens
    mine = own_ref[pl.ds(scens, extra), :].T
    theirs = [g[pl.ds(scens, extra), :].T for g in got]
    bus_id = lax.broadcasted_iota(jnp.int32, (LANES, BOUNDARY), 1).astype(F32)
    line_id = lax.broadcasted_iota(jnp.int32, (LANES, BOUNDARY), 0)
    for p in range(slots):
        number = live_lines(active_ref, count_ref, p)
        other = theirs[buffer_of[p]]
        half = 0.5 * SIGNS[p]
        for j in range(pieces):
            live = jnp.where(line_id + j * LANES < number, half, 0.0)
            at = p * pieces + j
            back = SLOTS[p][2] * pieces + j
            left = jnp.where(bus_id == mine[:, at : at + 1], live, 0.0)
            right = jnp.where(bus_id == other[:, back : back + 1], -live, 0.0)
            rows = pl.ds(j * LANES, LANES)
            table_ref[p, rows, pl.ds(0, BOUNDARY)] = left.astype(BF16)
            table_ref[p, rows, pl.ds(BOUNDARY, BOUNDARY)] = right.astype(BF16)


def final_kernel(total, regions, buffer_of, table_ref, shares1_ref, shares2_ref, own_ref, *refs):
    buffers = max(buffer_of) + 1
    got = refs[:buffers]
    flow_ref, price_ref, high_ref, low_ref = refs[buffers:]
    slot = pl.program_id(0)

    @pl.when(slot == 0)
    def _():
        for b in range(buffers):
            both = jnp.concatenate([own_ref[...], got[b][...]], axis=1)
            high, low = halves(both)
            high_ref[b] = high
            low_ref[b] = low
        shares = shares1_ref[pl.ds(0, total), :] + shares2_ref[pl.ds(0, total), :]
        zones = shares1_ref[pl.ds(total, total), :]
        for z in range(ZONES):
            price_ref[pl.ds(z, 1), :] = prices(shares, zones, total, regions, float(z))

    for p in range(len(buffer_of)):

        @pl.when(slot == p)
        def _(p=p):
            b = buffer_of[p]
            flow_ref[0, 0] = dot_nt(table_ref[0], high_ref[b]) + dot_nt(table_ref[0], low_ref[b])


def moved(x, axis, by):
    length = lax.axis_size(axis)
    return lax.ppermute(x, axis, [(i, (i + by) % length) for i in range(length)])


def body(kkt_inverse, scen_load, capacity, pair_active, tie_counts, line_index, area_zone):
    areas = lax.axis_size("area")
    regions = lax.axis_size("region")
    total = areas * regions
    _, buses, scens = scen_load.shape
    _, slots, lines = line_index.shape
    rest = buses - BOUNDARY
    index_rows = -(-slots * (lines // LANES) // 8) * 8
    share_rows = -(-2 * total // 16) * 16

    sources = []
    buffer_of = []
    for axis, move, _ in SLOTS:
        source = (axis, move % lax.axis_size(axis))
        if source not in sources:
            sources.append(source)
        buffer_of.append(sources.index(source))
    buffer_of = tuple(buffer_of)

    def f32(*shape):
        return jax.ShapeDtypeStruct(shape, F32)

    def bf16(*shape):
        return jax.ShapeDtypeStruct(shape, BF16)

    def exchange(x):
        return [moved(x, axis, -move) for axis, move in sources]

    def reduce_shares(shares):
        if (areas, regions) != (4, 2):
            return lax.psum(shares, ("area", "region"))
        shares = shares + moved(shares, "region", 1)
        return (shares + moved(shares, "area", 2)) + (moved(shares, "area", 1) + moved(shares, "area", -1))

    edge1, rest1, state, lin, kh, kl = pl.pallas_call(
        first_kernel,
        out_shape=(
            f32(scens + index_rows, BOUNDARY),
            f32(scens, rest),
            f32(scens, buses),
            f32(scens, buses),
            bf16(buses, buses),
            bf16(buses, buses),
        ),
        in_specs=[VMEM] * 4,
        out_specs=[VMEM] * 6,
        compiler_params=PARAMS,
        name="first_round",
    )(kkt_inverse, scen_load, capacity, line_index)
    got1 = exchange(edge1)
    share1, own, weights = pl.pallas_call(
        functools.partial(share_kernel, areas, regions),
        out_shape=(f32(share_rows, scens), bf16(BOUNDARY, slots * lines), f32(share_rows, buses)),
        in_specs=[SMEM] * 3 + [VMEM] * 3,
        out_specs=[VMEM] * 3,
        compiler_params=PARAMS,
        name="mismatch_shares",
    )(pair_active, tie_counts, area_zone, edge1, rest1, line_index)
    shares1 = reduce_shares(share1)
    edge2, rest2 = pl.pallas_call(
        functools.partial(second_kernel, total, regions, buffer_of),
        out_shape=(f32(scens, BOUNDARY), f32(scens, rest)),
        in_specs=[SMEM] + [VMEM] * (7 + len(got1)),
        out_specs=[VMEM] * 2,
        scratch_shapes=[pltpu.VMEM((scens, buses), F32)],
        compiler_params=PARAMS,
        name="second_round",
    )(area_zone, lin, state, kh, kl, capacity, own, shares1, *got1)
    got2 = exchange(edge2)
    share2, injection = pl.pallas_call(
        again_kernel,
        out_shape=(f32(share_rows, scens), f32(1, buses, scens)),
        in_specs=[VMEM] * 3,
        out_specs=[VMEM] * 2,
        compiler_params=PARAMS,
        name="mismatch_shares_again",
    )(weights, edge2, rest2)
    shares2 = reduce_shares(share2)
    table = pl.pallas_call(
        functools.partial(table_kernel, buffer_of, scens),
        out_shape=bf16(slots, lines, 2 * BOUNDARY),
        in_specs=[SMEM] * 2 + [VMEM] * (1 + len(got1)),
        out_specs=VMEM,
        compiler_params=PARAMS,
        name="line_table",
    )(pair_active, tie_counts, edge1, *got1)
    flow, price = pl.pallas_call(
        functools.partial(final_kernel, total, regions, buffer_of),
        out_shape=(f32(1, slots, lines, scens), f32(ZONES, scens)),
        grid=(slots,),
        in_specs=[pl.BlockSpec((1, lines, 2 * BOUNDARY), lambda p: (p, 0, 0))]
        + [pl.BlockSpec((share_rows, scens), lambda p: (0, 0))] * 2
        + [pl.BlockSpec((scens, BOUNDARY), lambda p: (0, 0))] * (1 + len(got2)),
        out_specs=(
            pl.BlockSpec((1, 1, lines, scens), lambda p: (0, p, 0, 0)),
            pl.BlockSpec((ZONES, scens), lambda p: (0, 0)),
        ),
        scratch_shapes=[pltpu.VMEM((len(got2), scens, 2 * BOUNDARY), BF16)] * 2,
        compiler_params=PARAMS,
        name="tie_flows",
    )(table, shares1, shares2, edge2, *got2)
    return injection, flow, price


def solution(mesh):
    placed = (
        P(("area", "region"), None, None),
        P(("area", "region"), None, ("group", "scen")),
        P(("area", "region"), None),
        P(("area", "region"), None),
        P(("area", "region"), None),
        P(("area", "region"), None, None),
        P(("area", "region")),
    )
    return jax.shard_map(
        body,
        mesh=mesh,
        in_specs=placed,
        out_specs=(
            P(("area", "region"), None, ("group", "scen")),
            P(("area", "region"), None, None, ("group", "scen")),
            P("region", ("group", "scen")),
        ),
        check_vma=False,
    )
```

time: 232 us -> 69.2 us (0.30)
  matrix products: 66.9 us -> 0 us
  waiting for transfers between devices: 75 us -> 16.7 us
  blocking collectives: 32.1 us -> 0 us
  Pallas kernels: 0 us -> 20 us
  local copies, waits for them, and re-layouts: 22.8 us -> 4.6 us
  other arithmetic: 13 us -> 0.02 us
  starting transfers between devices: 18.9 us -> 26.2 us
    dot_general x52 -> x0, matrix products: 66.9 us -> none  [the longest x48 54 us: box_sweep(): jnp.dot(inverse, linear + clipped - scaled, precision=lax.Precision.HIGHE...]
    ppermute x12 -> x16, waiting for transfers between devices: 75 us -> 16.7 us  [moved(): lax.ppermute(x, axis, [(i, (i + by) % length) for i in range(length)])]
    psum x4 -> x0, blocking collectives: 32.1 us -> none  [the longest x2 22.3 us: body(): zone_sum = lax.psum(zone_terms, 'area')]
    pallas_call x0 -> x6, Pallas kernels: none -> 20 us  [the longest x1 7.24 us: body(): pl.pallas_call(functools.partial(second_kernel, total, regions, buffer_of...]
    unnamed x87 -> x15, local copies, waits for them, and re-layouts: 15.5 us -> 4.6 us
    ppermute x12 -> x16, starting transfers between devices: 18.9 us -> 26.2 us  [moved(): lax.ppermute(x, axis, [(i, (i + by) % length) for i in range(length)])]
    reduce_sum x6 -> x0, other arithmetic: 4.79 us -> none  [the longest x2 3.9 us: body(): jnp.sum(side_sign * tie_flow, axis=(0, 1))]
    add x4, other arithmetic: 4.01 us -> 0.02 us  [the longest x2 0.01 us: reduce_shares(): shares + moved(shares, 'area', 2) + (moved(shares, 'area', 1) + moved(sha...]
  transfers between devices with their start and end apart: 12 -> 16, of which waited for: 8 -> 5; matrix products, arithmetic and copies ran while one was open for 5% -> 0% of each run, Pallas kernels for 0% -> 2%
where the time goes in v1:
time: 69.2 us; the launch traced here: 68.9 us
  starting transfers between devices  26.2 us (38%)
  Pallas kernels  20 us (29%)
  waiting for transfers between devices  16.7 us (24%)
  local copies, waits for them, and re-layouts  4.6 us (7%)
  between operations  1.39 us (2%)
    ppermute x16, starting transfers between devices, moved(): lax.ppermute(x, axis, [(i, (i + by) % length) for i in range(length)])  26.2 us
    ppermute x16, waiting for transfers between devices, moved(): lax.ppermute(x, axis, [(i, (i + by) % length) for i in range(length)])  16.7 us
    pallas_call x1, Pallas kernels, body(): pl.pallas_call(functools.partial(second_kernel, total, regions, buffer_of...  7.24 us
    pallas_call x1, Pallas kernels, body(): pl.pallas_call(first_kernel, out_shape=(f32(scens + index_rows, BOUNDARY)...  5.4 us
    unnamed x15, local copies, waits for them, and re-layouts  4.6 us
    pallas_call x1, Pallas kernels, body(): pl.pallas_call(functools.partial(final_kernel, total, regions, buffer_of)...  3.66 us
    pallas_call x1, Pallas kernels, body(): pl.pallas_call(functools.partial(table_kernel, buffer_of, scens), out_sha...  1.41 us
  transfers between devices with their start and end apart: 16, of which 5 were waited for; matrix products, arithmetic and copies ran while one was open for 0% of the time, Pallas kernels for 2%

profile of v1, /device:TPU:0, one launch (start us, length us, event | category | flops | bytes accessed | tf_op | source)
XLA Modules:
  0.0 68.9 jit_solution(12066974417611671088)
XLA Ops:
  2.0 0.9 %copy-done = f32[1,256,256]{2,1,0:T(8,128)S(1)} copy-done((f32[1,256,256]{2,1,0:T(8,128)S(1)}, f32[1,256,256]{2,1,0:T(8,128)}, u32[]{:S(2)}) %copy-start) | copy-done | bytes 262168
  3.0 0.9 %copy-done.1 = f32[1,256,256]{2,1,0:T(8,128)S(1)} copy-done((f32[1,256,256]{2,1,0:T(8,128)S(1)}, f32[1,256,256]{2,1,0:T(8,128)}, u32[]{:S(2)}) %copy-start.1) | copy-done | bytes 262168
  4.6 5.4 %first_round.1 = (f32[280,128]{1,0:T(8,128)S(1)}, f32[256,128]{1,0:T(8,128)S(1)}, f32[256,256]{1,0:T(8,128)S(1)}, f32[256,256]{1,0:T(8,128)S(1)}, bf16[256,256]{...) custom-call(f32[1,256,256]{2,1,0:T(8,128)S(1)} %copy-done, f32[1,256,256]{2,1,0:T(8,128)S(1)} %copy-done.1, ...), custom_call_target="tpu_custom_call" | custom-call | tf_op jit(solution)/shard_map/first_round/pallas_call | solution.py:290
  11.3 1.3 %mismatch_shares.1 = (f32[16,256]{1,0:T(8,128)S(1)}, bf16[128,2304]{1,0:T(8,128)(2,1)S(1)}, f32[16,256]{1,0:T(8,128)S(1)}) custom-call(s32[1,6]{1,0:T(1,128)S(1)} %copy-done.3, s32[1,6]{1,0:T(1,128)S(1)} %copy-done.5, s32[1]{0:T(128)S(6)} %copy.12.zone_ref, f32[280,128]{1,0:T(8,128)S(1)} %get-tuple-element.18.edge_ref.own_ref, ...), custom_call_target="tpu_custom_call" | custom-call | tf_op jit(solution)/shard_map/mismatch_shares/pallas_call | solution.py:306
  12.7 3.0 %collective-permute-start = (f32[16,256]{1,0:T(8,128)S(1)}, f32[16,256]{1,0:T(8,128)S(1)}, u32[]{:S(2)}, u32[]{:S(2)}) collective-permute-start(f32[16,256]{1,0:T(8,128)S(1)} %get-tuple-element.26), channel_id=1, source_target_pairs={{0,2},{2,0},{1,3},{3,1},{4,6},{6,4},{5,7},{7,5},{8,10},{10,8},{9,1... | collective-permute-start | bytes 49160 | tf_op jit(solution)/shard_map/ppermute | solution.py:253
  15.6 1.7 %collective-permute-done = f32[16,256]{1,0:T(8,128)S(1)} collective-permute-done((f32[16,256]{1,0:T(8,128)S(1)}, f32[16,256]{1,0:T(8,128)S(1)}, u32[]{:S(2)}, u32[]{:S(2)}) %collective-permute-start) | collective-permute-done | bytes 16416 | tf_op jit(solution)/shard_map/ppermute | solution.py:253
  17.4 4.1 %collective-permute-start.3 = (f32[16,256]{1,0:T(8,128)S(1)}, f32[16,256]{1,0:T(8,128)S(1)}, u32[]{:S(2)}, u32[]{:S(2)}) collective-permute-start(f32[16,256]{1,0:T(8,128)S(1)} %add.24), channel_id=1, source_target_pairs={{0,12},{4,0},{8,4},{12,8},{1,13},{5,1},{9,5},{13,9},{2,14},{6,2},{... | collective-permute-start | bytes 49160 | tf_op jit(solution)/shard_map/ppermute | solution.py:253
  21.5 1.0 %collective-permute-start.1 = (f32[16,256]{1,0:T(8,128)S(1)}, f32[16,256]{1,0:T(8,128)S(1)}, u32[]{:S(2)}, u32[]{:S(2)}) collective-permute-start(f32[16,256]{1,0:T(8,128)S(1)} %add.24), channel_id=1, source_target_pairs={{0,8},{4,12},{8,0},{12,4},{1,9},{5,13},{9,1},{13,5},{2,10},{6,14},... | collective-permute-start | bytes 49160 | tf_op jit(solution)/shard_map/ppermute | solution.py:253
  22.5 1.5 %collective-permute-start.7 = (f32[280,128]{1,0:T(8,128)S(1)}, f32[280,128]{1,0:T(8,128)S(1)}, u32[]{:S(2)}, u32[]{:S(2)}) collective-permute-start(f32[280,128]{1,0:T(8,128)S(1)} %get-tuple-element.18.edge_ref.own_ref), channel_id=1, source_target_pairs={{0,2},{2,0},{1,3},{3,1},{4,6},{6,4},{5,7},{7,5},{8,10},{10,8},{9,1... | collective-permute-start | bytes 430088 | tf_op jit(solution)/shard_map/ppermute | solution.py:253
  24.0 1.9 %collective-permute-start.6 = (f32[280,128]{1,0:T(8,128)S(1)}, f32[280,128]{1,0:T(8,128)S(1)}, u32[]{:S(2)}, u32[]{:S(2)}) collective-permute-start(f32[280,128]{1,0:T(8,128)S(1)} %get-tuple-element.18.edge_ref.own_ref), channel_id=1, source_target_pairs={{0,8},{4,12},{8,0},{12,4},{1,9},{5,13},{9,1},{13,5},{2,10},{6,14},... | collective-permute-start | bytes 430088 | tf_op jit(solution)/shard_map/ppermute | solution.py:253
  25.9 1.5 %collective-permute-start.5 = (f32[280,128]{1,0:T(8,128)S(1)}, f32[280,128]{1,0:T(8,128)S(1)}, u32[]{:S(2)}, u32[]{:S(2)}) collective-permute-start(f32[280,128]{1,0:T(8,128)S(1)} %get-tuple-element.18.edge_ref.own_ref), channel_id=1, source_target_pairs={{0,4},{4,8},{8,12},{12,0},{1,5},{5,9},{9,13},{13,1},{2,6},{6,10},{... | collective-permute-start | bytes 430088 | tf_op jit(solution)/shard_map/ppermute | solution.py:253
  27.4 2.6 %collective-permute-start.4 = (f32[280,128]{1,0:T(8,128)S(1)}, f32[280,128]{1,0:T(8,128)S(1)}, u32[]{:S(2)}, u32[]{:S(2)}) collective-permute-start(f32[280,128]{1,0:T(8,128)S(1)} %get-tuple-element.18.edge_ref.own_ref), channel_id=1, source_target_pairs={{0,12},{4,0},{8,4},{12,8},{1,13},{5,1},{9,5},{13,9},{2,14},{6,2},{... | collective-permute-start | bytes 430088 | tf_op jit(solution)/shard_map/ppermute | solution.py:253
  30.0 7.1 %collective-permute-done.6.refs_2_ = f32[280,128]{1,0:T(8,128)S(1)} collective-permute-done((f32[280,128]{1,0:T(8,128)S(1)}, f32[280,128]{1,0:T(8,128)S(1)}, u32[]{:S(2)}, u32[]{:S(2)}) %collective-permute-start.6) | collective-permute-done | bytes 143392 | tf_op jit(solution)/shard_map/ppermute | solution.py:253
  37.1 7.2 %second_round.1 = (f32[256,128]{1,0:T(8,128)S(1)}, f32[256,128]{1,0:T(8,128)S(1)}) custom-call(s32[1]{0:T(128)S(6)} %copy.12.zone_ref, f32[256,256]{1,0:T(8,128)S(1)} %get-tuple-element.21.lin_ref, f32[256,256]{1,0:T(8,128)S(1)} %get-tuple-element.22.v_ref, bf16[256,256]{1,0:T(8,128)(2,1)S(1)} %get-tuple-element.23.kh_ref, ...), custom_call_target="tpu_custom_call" | custom-call | tf_op jit(solution)/shard_map/second_round/pallas_call | solution.py:315
  44.3 0.9 %mismatch_shares_again.1 = (f32[16,256]{1,0:T(8,128)S(1)}, f32[1,256,256]{2,1,0:T(8,128)}) custom-call(f32[16,256]{1,0:T(8,128)S(1)} %get-tuple-element.20.weight_ref, f32[256,128]{1,0:T(8,128)S(1)} %get-tuple-element.27.edge_ref.own_ref, f32[256,128]{1,0:T(8,128)S(1)} %get-tuple-element.28.rest_ref), custom_call_target="tpu_custom_call" | custom-call | tf_op jit(solution)/shard_map/mismatch_shares_again/pallas_call | solution.py:325
  45.2 0.8 %collective-permute-start.8 = (f32[16,256]{1,0:T(8,128)S(1)}, f32[16,256]{1,0:T(8,128)S(1)}, u32[]{:S(2)}, u32[]{:S(2)}) collective-permute-start(f32[16,256]{1,0:T(8,128)S(1)} %get-tuple-element.30), channel_id=1, source_target_pairs={{0,2},{2,0},{1,3},{3,1},{4,6},{6,4},{5,7},{7,5},{8,10},{10,8},{9,1... | collective-permute-start | bytes 49160 | tf_op jit(solution)/shard_map/ppermute | solution.py:253
  46.1 2.9 %collective-permute-done.8 = f32[16,256]{1,0:T(8,128)S(1)} collective-permute-done((f32[16,256]{1,0:T(8,128)S(1)}, f32[16,256]{1,0:T(8,128)S(1)}, u32[]{:S(2)}, u32[]{:S(2)}) %collective-permute-start.8) | collective-permute-done | bytes 16416 | tf_op jit(solution)/shard_map/ppermute | solution.py:253
  49.0 1.9 %collective-permute-start.11 = (f32[16,256]{1,0:T(8,128)S(1)}, f32[16,256]{1,0:T(8,128)S(1)}, u32[]{:S(2)}, u32[]{:S(2)}) collective-permute-start(f32[16,256]{1,0:T(8,128)S(1)} %add.28), channel_id=1, source_target_pairs={{0,12},{4,0},{8,4},{12,8},{1,13},{5,1},{9,5},{13,9},{2,14},{6,2},{... | collective-permute-start | bytes 49160 | tf_op jit(solution)/shard_map/ppermute | solution.py:253
  51.1 2.6 %collective-permute-start.9 = (f32[16,256]{1,0:T(8,128)S(1)}, f32[16,256]{1,0:T(8,128)S(1)}, u32[]{:S(2)}, u32[]{:S(2)}) collective-permute-start(f32[16,256]{1,0:T(8,128)S(1)} %add.28), channel_id=1, source_target_pairs={{0,8},{4,12},{8,0},{12,4},{1,9},{5,13},{9,1},{13,5},{2,10},{6,14},... | collective-permute-start | bytes 49160 | tf_op jit(solution)/shard_map/ppermute | solution.py:253
  54.9 1.4 %line_table.1.table_ref = bf16[6,384,256]{2,1,0:T(8,128)(2,1)S(1)} custom-call(s32[1,6]{1,0:T(1,128)S(1)} %copy-done.4, s32[1,6]{1,0:T(1,128)S(1)} %copy-done.6, f32[280,128]{1,0:T(8,128)S(1)} %get-tuple-element.18.edge_ref.own_ref, f32[280,128]{1,0:T(8,128)S(1)} %collective-permute-done.4.refs_0_, f32[280,128]{1,0:T(8,128)S(1)} %collective-permute-done.5.refs_1_, ...), custom_call_target="tpu_custom_call" | custom-call | tf_op jit(solution)/shard_map/line_table/pallas_call | solution.py:334
  56.3 2.0 %collective-permute-start.13 = (f32[256,128]{1,0:T(8,128)S(1)}, f32[256,128]{1,0:T(8,128)S(1)}, u32[]{:S(2)}, u32[]{:S(2)}) collective-permute-start(f32[256,128]{1,0:T(8,128)S(1)} %get-tuple-element.27.edge_ref.own_ref), channel_id=1, source_target_pairs={{0,4},{4,8},{8,12},{12,0},{1,5},{5,9},{9,13},{13,1},{2,6},{6,10},{... | collective-permute-start | bytes 393224 | tf_op jit(solution)/shard_map/ppermute | solution.py:253
  58.3 1.9 %collective-permute-start.12 = (f32[256,128]{1,0:T(8,128)S(1)}, f32[256,128]{1,0:T(8,128)S(1)}, u32[]{:S(2)}, u32[]{:S(2)}) collective-permute-start(f32[256,128]{1,0:T(8,128)S(1)} %get-tuple-element.27.edge_ref.own_ref), channel_id=1, source_target_pairs={{0,12},{4,0},{8,4},{12,8},{1,13},{5,1},{9,5},{13,9},{2,14},{6,2},{... | collective-permute-start | bytes 393224 | tf_op jit(solution)/shard_map/ppermute | solution.py:253
  60.2 4.3 %collective-permute-done.14.refs_2_ = f32[256,128]{1,0:T(8,128)S(1)} collective-permute-done((f32[256,128]{1,0:T(8,128)S(1)}, f32[256,128]{1,0:T(8,128)S(1)}, u32[]{:S(2)}, u32[]{:S(2)}) %collective-permute-start.14) | collective-permute-done | bytes 131104 | tf_op jit(solution)/shard_map/ppermute | solution.py:253
  65.3 3.7 %tie_flows.1 = (f32[1,6,384,256]{3,2,1,0:T(8,128)}, f32[4,256]{1,0:T(4,128)}) custom-call(bf16[6,384,256]{2,1,0:T(8,128)(2,1)S(1)} %line_table.1.table_ref, f32[16,256]{1,0:T(8,128)S(1)} %add_add_fusion.1.shares_ref.shares1_ref, f32[16,256]{1,0:T(8,128)S(1)} %add_add_fusion.shares2_ref, f32[256,128]{1,0:T(8,128)S(1)} %get-tuple-element.27.edge_ref.own_ref, ...), custom_call_target="tpu_custom_call" | custom-call | tf_op jit(solution)/shard_map/tie_flows/pallas_call | solution.py:342
  (33 shorter events, 4.9 us)
Async XLA Ops:
  0.6 54.3 %copy-start.6 = (s32[1,6]{1,0:T(1,128)S(1)}, s32[1,6]{1,0:T(1,128)}, u32[]{:S(2)}) copy-start(s32[1,6]{1,0:T(1,128)} %count_ref.3) | copy-start | bytes 76
  0.6 54.3 %copy-start.4 = (s32[1,6]{1,0:T(1,128)S(1)}, s32[1,6]{1,0:T(1,128)}, u32[]{:S(2)}) copy-start(s32[1,6]{1,0:T(1,128)} %active_ref.3) | copy-start | bytes 76
  2.0 0.9 %copy-start = (f32[1,256,256]{2,1,0:T(8,128)S(1)}, f32[1,256,256]{2,1,0:T(8,128)}, u32[]{:S(2)}) copy-start(f32[1,256,256]{2,1,0:T(8,128)} %k_ref.1) | copy-start | bytes 786436
  3.0 0.9 %copy-start.1 = (f32[1,256,256]{2,1,0:T(8,128)S(1)}, f32[1,256,256]{2,1,0:T(8,128)}, u32[]{:S(2)}) copy-start(f32[1,256,256]{2,1,0:T(8,128)} %load_ref.1) | copy-start | bytes 786436
  3.9 0.7 copy-start.2
  10.0 0.7 copy-start.3
  10.7 0.7 copy-start.5
  12.7 4.7 %collective-permute-start = (f32[16,256]{1,0:T(8,128)S(1)}, f32[16,256]{1,0:T(8,128)S(1)}, u32[]{:S(2)}, u32[]{:S(2)}) collective-permute-start(f32[16,256]{1,0:T(8,128)S(1)} %get-tuple-element.26), channel_id=1, source_target_pairs={{0,2},{2,0},{1,3},{3,1},{4,6},{6,4},{5,7},{7,5},{8,10},{10,8},{9,1... | collective-permute-start | bytes 49160 | tf_op jit(solution)/shard_map/ppermute | solution.py:253
  17.4 8.6 %collective-permute-start.3 = (f32[16,256]{1,0:T(8,128)S(1)}, f32[16,256]{1,0:T(8,128)S(1)}, u32[]{:S(2)}, u32[]{:S(2)}) collective-permute-start(f32[16,256]{1,0:T(8,128)S(1)} %add.24), channel_id=1, source_target_pairs={{0,12},{4,0},{8,4},{12,8},{1,13},{5,1},{9,5},{13,9},{2,14},{6,2},{... | collective-permute-start | bytes 49160 | tf_op jit(solution)/shard_map/ppermute | solution.py:253
  21.5 5.9 %collective-permute-start.2 = (f32[16,256]{1,0:T(8,128)S(1)}, f32[16,256]{1,0:T(8,128)S(1)}, u32[]{:S(2)}, u32[]{:S(2)}) collective-permute-start(f32[16,256]{1,0:T(8,128)S(1)} %add.24), channel_id=1, source_target_pairs={{0,4},{4,8},{8,12},{12,0},{1,5},{5,9},{9,13},{13,1},{2,6},{6,10},{... | collective-permute-start | bytes 49160 | tf_op jit(solution)/shard_map/ppermute | solution.py:253
  21.5 8.5 %collective-permute-start.1 = (f32[16,256]{1,0:T(8,128)S(1)}, f32[16,256]{1,0:T(8,128)S(1)}, u32[]{:S(2)}, u32[]{:S(2)}) collective-permute-start(f32[16,256]{1,0:T(8,128)S(1)} %add.24), channel_id=1, source_target_pairs={{0,8},{4,12},{8,0},{12,4},{1,9},{5,13},{9,1},{13,5},{2,10},{6,14},... | collective-permute-start | bytes 49160 | tf_op jit(solution)/shard_map/ppermute | solution.py:253
  22.5 7.5 %collective-permute-start.7 = (f32[280,128]{1,0:T(8,128)S(1)}, f32[280,128]{1,0:T(8,128)S(1)}, u32[]{:S(2)}, u32[]{:S(2)}) collective-permute-start(f32[280,128]{1,0:T(8,128)S(1)} %get-tuple-element.18.edge_ref.own_ref), channel_id=1, source_target_pairs={{0,2},{2,0},{1,3},{3,1},{4,6},{6,4},{5,7},{7,5},{8,10},{10,8},{9,1... | collective-permute-start | bytes 430088 | tf_op jit(solution)/shard_map/ppermute | solution.py:253
  24.0 13.1 %collective-permute-start.6 = (f32[280,128]{1,0:T(8,128)S(1)}, f32[280,128]{1,0:T(8,128)S(1)}, u32[]{:S(2)}, u32[]{:S(2)}) collective-permute-start(f32[280,128]{1,0:T(8,128)S(1)} %get-tuple-element.18.edge_ref.own_ref), channel_id=1, source_target_pairs={{0,8},{4,12},{8,0},{12,4},{1,9},{5,13},{9,1},{13,5},{2,10},{6,14},... | collective-permute-start | bytes 430088 | tf_op jit(solution)/shard_map/ppermute | solution.py:253
  25.9 11.2 %collective-permute-start.5 = (f32[280,128]{1,0:T(8,128)S(1)}, f32[280,128]{1,0:T(8,128)S(1)}, u32[]{:S(2)}, u32[]{:S(2)}) collective-permute-start(f32[280,128]{1,0:T(8,128)S(1)} %get-tuple-element.18.edge_ref.own_ref), channel_id=1, source_target_pairs={{0,4},{4,8},{8,12},{12,0},{1,5},{5,9},{9,13},{13,1},{2,6},{6,10},{... | collective-permute-start | bytes 430088 | tf_op jit(solution)/shard_map/ppermute | solution.py:253
  27.4 9.7 %collective-permute-start.4 = (f32[280,128]{1,0:T(8,128)S(1)}, f32[280,128]{1,0:T(8,128)S(1)}, u32[]{:S(2)}, u32[]{:S(2)}) collective-permute-start(f32[280,128]{1,0:T(8,128)S(1)} %get-tuple-element.18.edge_ref.own_ref), channel_id=1, source_target_pairs={{0,12},{4,0},{8,4},{12,8},{1,13},{5,1},{9,5},{13,9},{2,14},{6,2},{... | collective-permute-start | bytes 430088 | tf_op jit(solution)/shard_map/ppermute | solution.py:253
  45.2 3.7 %collective-permute-start.8 = (f32[16,256]{1,0:T(8,128)S(1)}, f32[16,256]{1,0:T(8,128)S(1)}, u32[]{:S(2)}, u32[]{:S(2)}) collective-permute-start(f32[16,256]{1,0:T(8,128)S(1)} %get-tuple-element.30), channel_id=1, source_target_pairs={{0,2},{2,0},{1,3},{3,1},{4,6},{6,4},{5,7},{7,5},{8,10},{10,8},{9,1... | collective-permute-start | bytes 49160 | tf_op jit(solution)/shard_map/ppermute | solution.py:253
  49.0 7.3 %collective-permute-start.11 = (f32[16,256]{1,0:T(8,128)S(1)}, f32[16,256]{1,0:T(8,128)S(1)}, u32[]{:S(2)}, u32[]{:S(2)}) collective-permute-start(f32[16,256]{1,0:T(8,128)S(1)} %add.28), channel_id=1, source_target_pairs={{0,12},{4,0},{8,4},{12,8},{1,13},{5,1},{9,5},{13,9},{2,14},{6,2},{... | collective-permute-start | bytes 49160 | tf_op jit(solution)/shard_map/ppermute | solution.py:253
  50.9 7.4 %collective-permute-start.10 = (f32[16,256]{1,0:T(8,128)S(1)}, f32[16,256]{1,0:T(8,128)S(1)}, u32[]{:S(2)}, u32[]{:S(2)}) collective-permute-start(f32[16,256]{1,0:T(8,128)S(1)} %add.28), channel_id=1, source_target_pairs={{0,4},{4,8},{8,12},{12,0},{1,5},{5,9},{9,13},{13,1},{2,6},{6,10},{... | collective-permute-start | bytes 49160 | tf_op jit(solution)/shard_map/ppermute | solution.py:253
  51.1 9.1 %collective-permute-start.9 = (f32[16,256]{1,0:T(8,128)S(1)}, f32[16,256]{1,0:T(8,128)S(1)}, u32[]{:S(2)}, u32[]{:S(2)}) collective-permute-start(f32[16,256]{1,0:T(8,128)S(1)} %add.28), channel_id=1, source_target_pairs={{0,8},{4,12},{8,0},{12,4},{1,9},{5,13},{9,1},{13,5},{2,10},{6,14},... | collective-permute-start | bytes 49160 | tf_op jit(solution)/shard_map/ppermute | solution.py:253
  53.7 6.5 %collective-permute-start.15 = (f32[256,128]{1,0:T(8,128)S(1)}, f32[256,128]{1,0:T(8,128)S(1)}, u32[]{:S(2)}, u32[]{:S(2)}) collective-permute-start(f32[256,128]{1,0:T(8,128)S(1)} %get-tuple-element.27.edge_ref.own_ref), channel_id=1, source_target_pairs={{0,2},{2,0},{1,3},{3,1},{4,6},{6,4},{5,7},{7,5},{8,10},{10,8},{9,1... | collective-permute-start | bytes 393224 | tf_op jit(solution)/shard_map/ppermute | solution.py:253
  54.4 10.1 %collective-permute-start.14 = (f32[256,128]{1,0:T(8,128)S(1)}, f32[256,128]{1,0:T(8,128)S(1)}, u32[]{:S(2)}, u32[]{:S(2)}) collective-permute-start(f32[256,128]{1,0:T(8,128)S(1)} %get-tuple-element.27.edge_ref.own_ref), channel_id=1, source_target_pairs={{0,8},{4,12},{8,0},{12,4},{1,9},{5,13},{9,1},{13,5},{2,10},{6,14},... | collective-permute-start | bytes 393224 | tf_op jit(solution)/shard_map/ppermute | solution.py:253
  56.3 8.2 %collective-permute-start.13 = (f32[256,128]{1,0:T(8,128)S(1)}, f32[256,128]{1,0:T(8,128)S(1)}, u32[]{:S(2)}, u32[]{:S(2)}) collective-permute-start(f32[256,128]{1,0:T(8,128)S(1)} %get-tuple-element.27.edge_ref.own_ref), channel_id=1, source_target_pairs={{0,4},{4,8},{8,12},{12,0},{1,5},{5,9},{9,13},{13,1},{2,6},{6,10},{... | collective-permute-start | bytes 393224 | tf_op jit(solution)/shard_map/ppermute | solution.py:253
  58.3 6.9 %collective-permute-start.12 = (f32[256,128]{1,0:T(8,128)S(1)}, f32[256,128]{1,0:T(8,128)S(1)}, u32[]{:S(2)}, u32[]{:S(2)}) collective-permute-start(f32[256,128]{1,0:T(8,128)S(1)} %get-tuple-element.27.edge_ref.own_ref), channel_id=1, source_target_pairs={{0,12},{4,0},{8,4},{12,8},{1,13},{5,1},{9,5},{13,9},{2,14},{6,2},{... | collective-permute-start | bytes 393224 | tf_op jit(solution)/shard_map/ppermute | solution.py:253

commit v2 on v0

v2 whole, which is shorter than its diff:
```python
import functools

import jax
import jax.numpy as jnp
from jax import lax
from jax.experimental import pallas as pl
from jax.experimental.pallas import tpu as pltpu
from jax.sharding import PartitionSpec as P

ZONES = 4
INNER = 24
BOUNDARY = 128
LANES = 128
ZONE_GAIN = 0.004
SYSTEM_GAIN = 0.001
SLOTS = (
    ("area", 1, 1),
    ("area", -1, 0),
    ("area", 2, 3),
    ("area", -2, 2),
    ("region", 1, 5),
    ("region", -1, 4),
)
SIGNS = (1.0, -1.0, 1.0, -1.0, 1.0, -1.0)
CHAIN_ROWS = 32
UNROLL = 4
BIG = 10**11
SMALL = 10**9

F32 = jnp.float32
BF16 = jnp.bfloat16
VMEM = pl.BlockSpec(memory_space=pltpu.VMEM)
HBM = pl.BlockSpec(memory_space=pltpu.HBM)
FIRST_VMEM = 56 * 2**20
PARAMS = pltpu.CompilerParams(vmem_limit_bytes=40 * 2**20)


def dot(a, b):
    return jnp.dot(a, b, preferred_element_type=F32)


def dot_nt(a, b):
    return lax.dot_general(a, b, (((1,), (1,)), ((), ())), preferred_element_type=F32)


def halves(x):
    high = x.astype(BF16)
    return high, (x - high.astype(F32)).astype(BF16)


def thirds(x):
    high = x.astype(BF16)
    rest = x - high.astype(F32)
    middle = rest.astype(BF16)
    return high, middle, (rest - middle.astype(F32)).astype(BF16)


def clipping(v, limits):
    clipped = jnp.clip(v, -limits, limits)
    return clipped, v - clipped


def run_sweeps(start, finish, lin_ref, over_ref, limits, kh_ref, kl_ref, count):
    scens, buses = lin_ref.shape
    chains = scens // CHAIN_ROWS

    def scoped(*accumulators):
        highs, lows = accumulators[:chains], accumulators[chains:]
        pltpu.matmul_push_rhs(kh_ref[...], 0, 0)
        pltpu.matmul_push_rhs(kl_ref[...], 0, 1)

        def issue(i, x, load=None):
            high, low = halves(x)
            pltpu.matmul_acc_lhs(highs[i], high, load)
            pltpu.matmul_acc_lhs(highs[i], low)
            pltpu.matmul_acc_lhs(lows[i], high, load)

        def rows_of(i):
            return pl.ds(i * CHAIN_ROWS, CHAIN_ROWS)

        def taken(i):
            return pltpu.matmul_pop(highs[i]) + pltpu.matmul_pop(lows[i])

        for i in range(chains):
            x, over = start(rows_of(i))
            over_ref[rows_of(i), :] = over
            issue(i, x, 0 if i == 0 else None)

        def sweep(_, carry):
            for i in range(chains):
                rows = rows_of(i)
                clipped, over = clipping(taken(i) + over_ref[rows, :], limits)
                over_ref[rows, :] = over
                issue(i, lin_ref[rows, :] + (clipped - over))
            return carry

        lax.fori_loop(0, count - 1, sweep, 0, unroll=UNROLL)
        for i in range(chains):
            finish(rows_of(i), taken(i), over_ref[rows_of(i), :])

    pl.run_scoped(
        scoped,
        *[pltpu.ACC(0)((CHAIN_ROWS, buses), F32)] * chains,
        *[pltpu.ACC(1)((CHAIN_ROWS, buses), F32)] * chains,
    )


def line_tables(areas, regions, slots, pieces, near, idx_row, number, own_ref, rows):
    me_area, me_region = lax.axis_index("area"), lax.axis_index("region")
    here = me_area if near else me_area * regions + me_region
    width = -(-rows // LANES) * LANES
    row_id = lax.broadcasted_iota(jnp.int32, (1, width), 1)
    line_id = lax.broadcasted_iota(jnp.int32, (1, LANES), 1).astype(F32)
    bus_id = lax.broadcasted_iota(jnp.int32, (BOUNDARY, LANES), 0).astype(F32)
    weights = jnp.zeros((BOUNDARY, width), F32)
    for p in range(slots):
        axis, move, _ = SLOTS[p]
        if axis == "area":
            other = lax.rem(me_area + move % areas, areas)
            there = other if near else other * regions + me_region
        else:
            there = areas + 1 if near else me_area * regions + lax.rem(me_region + move % regions, regions)
        coefficient = jnp.where(row_id == there, 0.5, 0.0) - jnp.where(row_id == here, 0.5, 0.0)
        met = None
        for j in range(pieces):
            row = jnp.where(line_id + float(j * LANES) < number(p), idx_row(p, j), -1.0)
            onehot = jnp.where(bus_id == row, 1.0, 0.0)
            own_ref[:, pl.ds((p * pieces + j) * LANES, LANES)] = onehot.astype(BF16)
            met = onehot if met is None else met + onehot
        weights = weights + jnp.sum(met, axis=1, keepdims=True) * coefficient
    last = areas if near else areas * regions
    mine = jnp.where((row_id == here) | (row_id == last), 1.0, 0.0)
    weights = jnp.concatenate([weights + mine, jnp.broadcast_to(mine, (BOUNDARY, width))], axis=0)
    return weights.T[0:rows, :]


def weighted_sums(weights, x):
    wh, wl = halves(weights)
    xh, xm, xl = thirds(x)
    return dot_nt(wh, xh) + (dot_nt(wh, xm) + dot_nt(wl, xh)) + (dot_nt(wh, xl) + dot_nt(wl, xm))


def store_shares(areas, near, sums, share_refs):
    share_refs[0][...] = sums[0 : share_refs[0].shape[0], :]
    if near:
        row_id = lax.broadcasted_iota(jnp.int32, (8, sums.shape[1]), 0)
        across = jnp.where(row_id == lax.axis_index("area"), sums[areas + 1 : areas + 2, :], 0.0)
        share_refs[1][...] = jnp.where(row_id == areas, sums[areas : areas + 1, :], across)


def first_kernel(
    areas, regions, near, base,
    k_hbm, load_hbm, cap_hbm, idx_hbm, active_hbm, count_hbm, zone_hbm,
    edge_ref, rest_ref, v_ref, lin_hbm, kh_hbm, kl_hbm, own_hbm, cap_out_ref, weight_ref,
    k_ref, load_ref, cap_ref, idx_ref, active_ref, count_ref, zone_ref,
    lin_ref, kh_ref, kl_ref, own_ref, over_ref, sems, out_sems,
):
    pairs = (
        (k_hbm, k_ref),
        (load_hbm, load_ref),
        (cap_hbm, cap_ref),
        (idx_hbm, idx_ref),
        (active_hbm, active_ref),
        (count_hbm, count_ref),
        (zone_hbm, zone_ref),
    )
    copies = [pltpu.make_async_copy(src, dst, sems.at[i]) for i, (src, dst) in enumerate(pairs)]
    for copy in copies:
        copy.start()
    pairs = ((kh_ref, kh_hbm), (kl_ref, kl_hbm), (lin_ref, lin_hbm), (own_ref, own_hbm))
    results = [pltpu.make_async_copy(src, dst, out_sems.at[i]) for i, (src, dst) in enumerate(pairs)]
    scens = lin_ref.shape[0]
    slots, _, lines = idx_ref.shape
    pieces = lines // LANES
    for copy in copies[3:]:
        copy.wait()
    numbers = jnp.where(active_ref[...] > 0, count_ref[...], 0).astype(F32)

    def idx_row(p, j):
        return idx_ref[p, :, pl.ds(j * LANES, LANES)].astype(F32)

    edge_ref[pl.ds(base, edge_ref.shape[0] - base), :] = jnp.zeros((edge_ref.shape[0] - base, LANES), F32)
    for p in range(slots):
        for j in range(pieces):
            edge_ref[pl.ds(base + p * pieces + j, 1), :] = idx_row(p, j)
    edge_ref[pl.ds(base + slots * pieces, 1), pl.ds(0, slots)] = numbers
    zone = zone_ref[0].astype(F32)
    edge_ref[pl.ds(base + slots * pieces + 1, 1), :] = jnp.full((1, LANES), zone)
    weight_ref[...] = line_tables(
        areas, regions, slots, pieces, near, idx_row, lambda p: numbers[:, p : p + 1], own_ref, weight_ref.shape[0]
    )
    copies[0].wait()
    high, low = halves(k_ref[0].T)
    kh_ref[...] = high
    kl_ref[...] = low
    copies[1].wait()
    lin_ref[...] = load_ref[0].T
    copies[2].wait()
    cap_out_ref[...] = cap_ref[...]
    for copy in results:
        copy.start()
    limits = cap_ref[...]

    def start(rows):
        return lin_ref[rows, :], jnp.zeros((CHAIN_ROWS, lin_ref.shape[1]), F32)

    def finish(rows, x, over):
        edge_ref[rows, :] = x[:, :BOUNDARY]
        rest_ref[rows, :] = x[:, BOUNDARY:]
        v_ref[rows, :] = x + over

    run_sweeps(start, finish, lin_ref, over_ref, limits, kh_ref, kl_ref, INNER)
    for copy in results:
        copy.wait()


def share_kernel(areas, regions, near, zone_at, weight_ref, edge_ref, rest_ref, *share_refs):
    scens = rest_ref.shape[0]
    x = jnp.concatenate([edge_ref[pl.ds(0, scens), :], rest_ref[...]], axis=1)
    sums = weighted_sums(weight_ref[...], x)
    if zone_at is not None:
        me = lax.axis_index("area") * regions + lax.axis_index("region")
        zone = edge_ref[pl.ds(zone_at, 1), pl.ds(0, 1)]
        row_id = lax.broadcasted_iota(jnp.int32, sums.shape, 0)
        sums = sums + jnp.where(row_id == areas * regions + 1 + me, zone, 0.0)
    store_shares(areas, near, sums, share_refs)


def live_lines(edge_ref, base, slots, pieces, p):
    return edge_ref[pl.ds(base + slots * pieces, 1), pl.ds(p, 1)]


def by_area(values):
    me = lax.axis_index("area")
    out = []
    for k in range(4):
        mask = jnp.bitwise_xor(me, k)
        low = jnp.where(jnp.bitwise_and(mask, 1) == 0, values[0], values[1])
        high = jnp.where(jnp.bitwise_and(mask, 1) == 0, values[2], values[3])
        out.append(jnp.where(mask < 2, low, high))
    return out


def near_zones(at, own_ref, got):
    return by_area([ref[pl.ds(at, 1), pl.ds(0, 1)] for ref in (own_ref, got[2], got[1], got[0])])


def near_prices(sums, zones, zone):
    price = sums[4:5, :] * SYSTEM_GAIN
    for k in range(4):
        price = price + jnp.where(zones[k] == zone, ZONE_GAIN, 0.0) * sums[k : k + 1, :]
    return price


def prices(shares, zones, total, regions, zone):
    ids = lax.broadcasted_iota(jnp.int32, zones.shape, 0)
    in_region = lax.rem(ids, regions) == lax.axis_index("region")
    gain = jnp.where(in_region & (zones == zone), ZONE_GAIN, 0.0) + SYSTEM_GAIN
    return jnp.sum(gain * shares[0:total, :], axis=0, keepdims=True)


class Mask(int):
    pass


def by_slot(buffer_of, got):
    even = lax.rem(lax.axis_index("area"), 2) == 0

    def read(p, rows):
        choice = buffer_of[p]
        if isinstance(choice, int):
            return got[choice][rows, :]
        return jnp.where(even, got[choice[0]][rows, :], got[choice[1]][rows, :])

    return read


def coupling_kernel(slots_of, scens, base, pieces, own_ref, *refs):
    got = refs[: len(slots_of)]
    coupling_ref = refs[-1]
    before = refs[len(slots_of) : -1]
    even = lax.rem(lax.axis_index("area"), 2) == 0
    lines = pieces * LANES
    bus_id = lax.broadcasted_iota(jnp.int32, (BOUNDARY, LANES), 0).astype(F32)
    counts = []
    for g, served in zip(got, slots_of):
        met = jnp.zeros((BOUNDARY, BOUNDARY), F32)
        for pair in served:
            for j in range(pieces):
                if isinstance(pair, int):
                    mine = own_ref[:, pl.ds(pair * lines + j * LANES, LANES)]
                    row = g[pl.ds(base + SLOTS[pair][2] * pieces + j, 1), :]
                else:
                    mine, row = [], []
                    for p in pair:
                        mine.append(own_ref[:, pl.ds(p * lines + j * LANES, LANES)])
                        row.append(g[pl.ds(base + SLOTS[p][2] * pieces + j, 1), :])
                    mine = jnp.where(even, *mine)
                    row = jnp.where(even, *row)
                there = jnp.where(bus_id == row, 1.0, 0.0).astype(BF16)
                met = met + dot_nt(mine, there)
        counts.append(met)
    counts_high, counts_low = halves(jnp.concatenate(counts, axis=1))
    high, low = halves(jnp.concatenate([g[pl.ds(0, scens), :] for g in got], axis=1))
    out = dot_nt(high, counts_high) + dot_nt(low, counts_high) + dot_nt(high, counts_low)
    for ref in before:
        out = out + ref[...]
    coupling_ref[...] = out


def second_kernel(
    areas, regions, near, info, lin_ref, coupling_ref, v_ref, kh_ref, kl_ref, cap_ref, edge1_ref, *refs
):
    edge_ref, rest_ref, sums_ref, lin2_ref, over_ref = refs[-5:]
    refs = refs[:-5]
    scens = lin_ref.shape[0]
    zone = edge1_ref[pl.ds(info + 1, 1), pl.ds(0, 1)]
    if near:
        sums = refs[0][...] + refs[1][...]
        zones = near_zones(info + 1, edge1_ref, refs[2:])
        price = near_prices(sums, zones, zone)
        sums_ref[pl.ds(0, 8), :] = sums
        sums_ref[pl.ds(8, 8), :] = jnp.zeros((8, scens), F32)
        for k in range(4):
            sums_ref[pl.ds(8 + k, 1), :] = jnp.broadcast_to(zones[k], (1, scens))
    else:
        total = areas * regions
        sums = refs[0][...]
        sums_ref[...] = sums
        price = prices(sums, sums[total + 1 : 2 * total + 1, :], total, regions, zone)
    price = jnp.broadcast_to(price, (8, scens)).T[:, 0:1]
    lin2_ref[:, pl.ds(0, BOUNDARY)] = lin_ref[:, pl.ds(0, BOUNDARY)] - price - coupling_ref[...]
    lin2_ref[:, pl.ds(BOUNDARY, BOUNDARY)] = lin_ref[:, pl.ds(BOUNDARY, BOUNDARY)] - price
    limits = cap_ref[...]

    def start(rows):
        clipped, over = clipping(v_ref[rows, :], limits)
        return lin2_ref[rows, :] + (clipped - over), over

    def finish(rows, x, over):
        edge_ref[rows, :] = x[:, :BOUNDARY]
        rest_ref[rows, :] = x[:, BOUNDARY:]

    run_sweeps(start, finish, lin2_ref, over_ref, limits, kh_ref, kl_ref, INNER)


def injection_kernel(edge_ref, rest_ref, injection_ref):
    scens = rest_ref.shape[0]
    injection_ref[0, pl.ds(0, BOUNDARY), :] = edge_ref[pl.ds(0, scens), :].T
    injection_ref[0, pl.ds(BOUNDARY, BOUNDARY), :] = rest_ref[...].T


def table_kernel(buffer_of, base, own_ref, *refs):
    got = refs[:-2]
    mine_ref, theirs_ref = refs[-2:]
    slots, lines = mine_ref.shape[:2]
    pieces = lines // LANES
    extra = own_ref.shape[0] - base
    read = by_slot(buffer_of, got)
    mine = own_ref[pl.ds(base, extra), :].T
    bus_id = lax.broadcasted_iota(jnp.int32, (LANES, BOUNDARY), 1).astype(F32)
    line_id = lax.broadcasted_iota(jnp.int32, (LANES, BOUNDARY), 0).astype(F32)
    for p in range(slots):
        number = live_lines(own_ref, base, slots, pieces, p)
        other = read(p, pl.ds(base, extra)).T
        half = 0.5 * SIGNS[p]
        for j in range(pieces):
            live = jnp.where(line_id + float(j * LANES) < number, half, 0.0)
            at = p * pieces + j
            back = SLOTS[p][2] * pieces + j
            rows = pl.ds(j * LANES, LANES)
            mine_ref[p, rows, :] = jnp.where(bus_id == mine[:, at : at + 1], live, 0.0).astype(BF16)
            theirs_ref[p, rows, :] = jnp.where(bus_id == other[:, back : back + 1], -live, 0.0).astype(BF16)


def twice(x):
    return jnp.concatenate([x, x], axis=1)


def own_kernel(table_ref, edge_ref, flow_ref):
    scens = flow_ref.shape[2]
    parts = jnp.concatenate(halves(edge_ref[pl.ds(0, scens), :]), axis=1)
    for p in range(table_ref.shape[0]):
        flow_ref[p] = dot_nt(twice(table_ref[p]), parts)


def parts_kernel(*refs):
    buffers = len(refs) // 2
    for b in range(buffers):
        refs[buffers + b][...] = jnp.concatenate(halves(refs[b][...]), axis=1)


def final_kernel(areas, regions, near, buffer_of, buffers, ready, table_ref, own_ref, sums_ref, *refs):
    flow_hbm, price_ref, flow_ref, late_ref, sems = refs[-5:]
    parts = list(refs[:ready])
    for i, ref in enumerate(refs[ready:buffers]):
        late_ref[i] = jnp.concatenate(halves(ref[...]), axis=1)
        parts.append(late_ref.at[i])
    read = by_slot(buffer_of, parts)
    scens = flow_ref.shape[2]
    copies = []
    for p in range(len(buffer_of)):
        flow_ref[p] = own_ref[p] + dot_nt(twice(table_ref[p]), read(p, pl.ds(0, scens)))
        copies.append(pltpu.make_async_copy(flow_ref.at[p], flow_hbm.at[0, p], sems.at[p]))
        copies[-1].start()
    rest = refs[buffers:-5]
    if near:
        sums = sums_ref[pl.ds(0, 8), :] + (rest[0][...] + rest[1][...])
        zones = [sums_ref[pl.ds(8 + k, 1), :] for k in range(4)]
        for z in range(ZONES):
            price_ref[pl.ds(z, 1), :] = near_prices(sums, zones, float(z))
    else:
        total = areas * regions
        first = sums_ref[...]
        zones = first[total + 1 : 2 * total + 1, :]
        for z in range(ZONES):
            price_ref[pl.ds(z, 1), :] = prices(first + rest[0][...], zones, total, regions, float(z))
    for copy in copies:
        copy.wait()


def moved(x, axis, by):
    length = lax.axis_size(axis)
    if isinstance(by, Mask):
        return lax.ppermute(x, axis, [(i, i ^ by) for i in range(length)])
    return lax.ppermute(x, axis, [((i + by) % length, i) for i in range(length)])


def body(kkt_inverse, scen_load, capacity, pair_active, tie_counts, line_index, area_zone):
    areas = lax.axis_size("area")
    regions = lax.axis_size("region")
    total = areas * regions
    _, buses, scens = scen_load.shape
    _, slots, lines = line_index.shape
    rest = buses - BOUNDARY
    pieces = lines // LANES
    near = (areas, regions) == (4, 2)
    base = scens
    info = base + slots * pieces
    edge1_rows = -(-(info + 2) // 8) * 8
    share_rows = 8 if near else -(-(2 * total + 1) // 8) * 8
    weight_rows = -(-share_rows // 16) * 16

    if areas == 4:
        sources = [("area", Mask(3)), ("area", Mask(2)), ("area", Mask(1))]
        buffer_of = [(2, 0), (0, 2), 1, 1]
        slots_of = [((1, 0),), (2, 3), ((0, 1),)]
        ready = 2
    else:
        sources = [("area", move) for _, move, _ in SLOTS[:4]]
        buffer_of = [0, 1, 2, 3]
        slots_of = [(0,), (1,), (2,), (3,)]
        ready = 4
    for p, (axis, move, _) in enumerate(SLOTS[4:], 4):
        source = (axis, move % regions)
        if source not in sources:
            sources.append(source)
            slots_of.append(())
        buffer_of.append(sources.index(source))
        slots_of[-1] += (p,)
    buffer_of = tuple(buffer_of)

    def f32(*shape):
        return jax.ShapeDtypeStruct(shape, F32)

    def bf16(*shape):
        return jax.ShapeDtypeStruct(shape, BF16)

    def exchange(x):
        return [moved(x, axis, move) for axis, move in sources[::-1]][::-1]

    def reduce_shares(shares):
        if not near:
            return [lax.psum(shares[0], ("area", "region"))]
        sums = shares[0] + moved(shares[1], "region", 1)
        sums = sums + moved(sums, "area", Mask(1))
        return [sums, moved(sums, "area", Mask(2))]

    def cost(flops):
        return pl.CostEstimate(flops=flops, bytes_accessed=0, transcendentals=0)

    edge1, rest1, state, lin, kh, kl, own, limits, weights = pl.pallas_call(
        functools.partial(first_kernel, areas, regions, near, base),
        out_shape=[
            f32(edge1_rows, BOUNDARY),
            f32(scens, rest),
            f32(scens, buses),
            f32(scens, buses),
            bf16(buses, buses),
            bf16(buses, buses),
            bf16(BOUNDARY, slots * lines),
            f32(1, buses),
            f32(weight_rows, buses),
        ],
        in_specs=[HBM] * 7,
        out_specs=[VMEM] * 3 + [HBM] * 4 + [VMEM] * 2,
        scratch_shapes=[
            pltpu.VMEM((1, buses, buses), F32),
            pltpu.VMEM((1, buses, scens), F32),
            pltpu.VMEM((1, buses), F32),
            pltpu.VMEM((slots, 1, lines), jnp.int32),
            pltpu.VMEM((1, slots), jnp.int32),
            pltpu.VMEM((1, slots), jnp.int32),
            pltpu.SMEM((1,), jnp.int32),
            pltpu.VMEM((scens, buses), F32),
            pltpu.VMEM((buses, buses), BF16),
            pltpu.VMEM((buses, buses), BF16),
            pltpu.VMEM((BOUNDARY, slots * lines), BF16),
            pltpu.VMEM((scens, buses), F32),
            pltpu.SemaphoreType.DMA((7,)),
            pltpu.SemaphoreType.DMA((4,)),
        ],
        compiler_params=pltpu.CompilerParams(vmem_limit_bytes=FIRST_VMEM),
        name="first_round",
    )(kkt_inverse, scen_load, capacity, line_index.reshape(slots, 1, lines), pair_active, tie_counts, area_zone)

    def make_shares(edge, rest, zone_at):
        return pl.pallas_call(
            functools.partial(share_kernel, areas, regions, near, zone_at),
            out_shape=[f32(share_rows, scens)] * (2 if near else 1),
            in_specs=[VMEM] * 3,
            out_specs=[VMEM] * (2 if near else 1),
            compiler_params=PARAMS,
            name="mismatch_shares",
        )(weights, edge, rest)

    sums1 = reduce_shares(make_shares(edge1, rest1, None if near else info + 1))
    got1 = exchange(edge1)
    coupling = ()
    for which, estimate in ((slice(0, ready), BIG), (slice(ready, None), SMALL)):
        coupling = pl.pallas_call(
            functools.partial(coupling_kernel, slots_of[which], scens, base, pieces),
            out_shape=(f32(scens, BOUNDARY),),
            in_specs=[VMEM] * (1 + len(got1[which]) + len(coupling)),
            out_specs=(VMEM,),
            compiler_params=PARAMS,
            cost_estimate=cost(estimate),
            name="coupling",
        )(own, *got1[which], *coupling)
    sources1 = [*sums1, *got1] if near else sums1
    edge2, rest2, first = pl.pallas_call(
        functools.partial(second_kernel, areas, regions, near, info),
        out_shape=[
            f32(scens, BOUNDARY),
            f32(scens, rest),
            f32(16 if near else share_rows, scens),
        ],
        in_specs=[VMEM] * (7 + len(sources1)),
        out_specs=[VMEM] * 3,
        scratch_shapes=[pltpu.VMEM((scens, buses), F32)] * 2,
        compiler_params=PARAMS,
        name="second_round",
    )(lin, *coupling, state, kh, kl, limits, edge1, *sources1)
    sums2 = reduce_shares(make_shares(edge2, rest2, None))
    got2 = exchange(edge2)
    injection = pl.pallas_call(
        injection_kernel,
        out_shape=f32(1, buses, scens),
        in_specs=[VMEM] * 2,
        out_specs=VMEM,
        compiler_params=PARAMS,
        name="injection",
    )(edge2, rest2)
    mine, theirs = pl.pallas_call(
        functools.partial(table_kernel, buffer_of, base),
        out_shape=(bf16(slots, lines, BOUNDARY),) * 2,
        in_specs=[VMEM] * (1 + len(got1)),
        out_specs=[VMEM] * 2,
        compiler_params=PARAMS,
        name="line_table",
    )(edge1, *got1)
    own_flow = pl.pallas_call(
        own_kernel,
        out_shape=f32(slots, lines, scens),
        in_specs=[VMEM] * 2,
        out_specs=VMEM,
        compiler_params=PARAMS,
        name="own_flows",
    )(mine, edge2)
    parts = pl.pallas_call(
        parts_kernel,
        out_shape=[bf16(scens, 2 * BOUNDARY)] * ready,
        in_specs=[VMEM] * ready,
        out_specs=[VMEM] * ready,
        compiler_params=PARAMS,
        cost_estimate=cost(BIG),
        name="injection_parts",
    )(*got2[:ready])
    flow, price = pl.pallas_call(
        functools.partial(final_kernel, areas, regions, near, buffer_of, len(got2), ready),
        out_shape=(f32(1, slots, lines, scens), f32(ZONES, scens)),
        in_specs=[VMEM] * (3 + len(got2) + len(sums2)),
        out_specs=(HBM, VMEM),
        scratch_shapes=[
            pltpu.VMEM((slots, lines, scens), F32),
            pltpu.VMEM((len(got2) - ready, scens, 2 * BOUNDARY), BF16),
            pltpu.SemaphoreType.DMA((slots,)),
        ],
        compiler_params=PARAMS,
        name="tie_flows",
    )(theirs, own_flow, first, *parts, *got2[ready:], *sums2)
    return injection, flow, price


def solution(mesh):
    placed = (
        P(("area", "region"), None, None),
        P(("area", "region"), None, ("group", "scen")),
        P(("area", "region"), None),
        P(("area", "region"), None),
        P(("area", "region"), None),
        P(("area", "region"), None, None),
        P(("area", "region")),
    )
    return jax.shard_map(
        body,
        mesh=mesh,
        in_specs=placed,
        out_specs=(
            P(("area", "region"), None, ("group", "scen")),
            P(("area", "region"), None, None, ("group", "scen")),
            P("region", ("group", "scen")),
        ),
        check_vma=False,
    )
```

time: 232 us -> 54.7 us (0.24)
  matrix products: 66.9 us -> 0 us
  waiting for transfers between devices: 75 us -> 8.45 us
  blocking collectives: 32.1 us -> 0 us
  local copies, waits for them, and re-layouts: 22.8 us -> 2.71 us
  Pallas kernels: 0 us -> 19.6 us
  other arithmetic: 13 us -> 0.01 us
  starting transfers between devices: 18.9 us -> 22.1 us
    dot_general x52 -> x0, matrix products: 66.9 us -> none  [the longest x48 54 us: box_sweep(): jnp.dot(inverse, linear + clipped - scaled, precision=lax.Precision.HIGHE...]
    ppermute x12 -> x14, waiting for transfers between devices: 75 us -> 8.45 us  [the longest x4 4.68 us: moved(): lax.ppermute(x, axis, [((i + by) % length, i) for i in range(length)])]
    psum x4 -> x0, blocking collectives: 32.1 us -> none  [the longest x2 22.3 us: body(): zone_sum = lax.psum(zone_terms, 'area')]
    pallas_call x0 -> x11, Pallas kernels: none -> 19.6 us  [the longest x1 6.46 us: body(): pl.pallas_call(functools.partial(first_kernel, areas, regions, near, base...]
    unnamed x87 -> x18, local copies, waits for them, and re-layouts: 15.5 us -> 2.71 us
    reduce_sum x6 -> x0, other arithmetic: 4.79 us -> none  [the longest x2 3.9 us: body(): jnp.sum(side_sign * tie_flow, axis=(0, 1))]
    add x4, other arithmetic: 4.01 us -> 0.01 us  [the longest x2 0.01 us: reduce_shares(): sums = sums + moved(sums, 'area', Mask(1))]
    while x98 -> x0, local copies, waits for them, and re-layouts: 3.68 us -> none  [the longest x2 1.91 us: body(): lax.fori_loop(0, INNER, box_sweep, (solution, clipped, scaled))]
  transfers between devices with their start and end apart: 12 -> 14, of which waited for: 8 -> 5; matrix products, arithmetic and copies ran while one was open for 5% -> 0% of each run, Pallas kernels for 0% -> 11%
where the time goes in v2:
time: 54.7 us; the launch traced here: 54.3 us
  starting transfers between devices  22.1 us (40%)
  Pallas kernels  19.6 us (36%)
  waiting for transfers between devices  8.45 us (15%)
  local copies, waits for them, and re-layouts  2.71 us (5%)
  between operations  1.44 us (3%)
    ppermute x10, starting transfers between devices, moved(): return lax.ppermute(x, axis, [(i, i ^ by) for i in range(length)])  16.7 us
    pallas_call x1, Pallas kernels, body(): pl.pallas_call(functools.partial(first_kernel, areas, regions, near, base...  6.46 us
    ppermute x4, starting transfers between devices, moved(): lax.ppermute(x, axis, [((i + by) % length, i) for i in range(length)])  5.38 us
    pallas_call x1, Pallas kernels, body(): pl.pallas_call(functools.partial(second_kernel, areas, regions, near, inf...  4.82 us
    ppermute x4, waiting for transfers between devices, moved(): lax.ppermute(x, axis, [((i + by) % length, i) for i in range(length)])  4.68 us
    ppermute x10, waiting for transfers between devices, moved(): return lax.ppermute(x, axis, [(i, i ^ by) for i in range(length)])  3.77 us
    unnamed x18, local copies, waits for them, and re-layouts  2.71 us
    pallas_call x1, Pallas kernels, body(): pl.pallas_call(functools.partial(final_kernel, areas, regions, near, buff...  2.37 us
  transfers between devices with their start and end apart: 14, of which 5 were waited for; matrix products, arithmetic and copies ran while one was open for 0% of the time, Pallas kernels for 11%

profile of v2, /device:TPU:0, one launch (start us, length us, event | category | flops | bytes accessed | tf_op | source)
XLA Modules:
  0.0 54.3 jit_solution(2512537322866465634)
XLA Ops:
  1.3 6.5 %first_round.1 = (f32[280,128]{1,0:T(8,128)}, f32[256,128]{1,0:T(8,128)}, f32[256,256]{1,0:T(8,128)}, f32[256,256]{1,0:T(8,128)}, bf16[256,256]{1,0:T(8,128)(2,1...) custom-call(f32[1,256,256]{2,1,0:T(8,128)} %k_hbm.1, ...), custom_call_target="tpu_custom_call" | custom-call | tf_op jit(solution)/shard_map/first_round/pallas_call | solution.py:482
  7.7 4.1 %collective-permute-start.3 = (f32[280,128]{1,0:T(8,128)}, f32[280,128]{1,0:T(8,128)S(1)}, u32[]{:S(2)}, u32[]{:S(2)}) collective-permute-start(f32[280,128]{1,0:T(8,128)} %get-tuple-element.27.edge_ref.edge1_ref.own_ref), channel_id=1, source_target_pairs={{0,8},{4,12},{8,0},{12,4},{1,9},{5,13},{9,1},{13,5},{2,10},{6,14},... | collective-permute-start | bytes 430088 | tf_op jit(solution)/shard_map/ppermute | solution.py:425
  11.8 1.3 %collective-permute-start.2 = (f32[280,128]{1,0:T(8,128)}, f32[280,128]{1,0:T(8,128)S(1)}, u32[]{:S(2)}, u32[]{:S(2)}) collective-permute-start(f32[280,128]{1,0:T(8,128)} %get-tuple-element.27.edge_ref.edge1_ref.own_ref), channel_id=1, source_target_pairs={{0,12},{4,8},{8,4},{12,0},{1,13},{5,9},{9,5},{13,1},{2,14},{6,10},... | collective-permute-start | bytes 430088 | tf_op jit(solution)/shard_map/ppermute | solution.py:425
  13.2 0.9 %copy-done.4 = f32[256,128]{1,0:T(8,128)S(1)} copy-done((f32[256,128]{1,0:T(8,128)S(1)}, f32[256,128]{1,0:T(8,128)}, u32[]{:S(2)}) %copy-start.4) | copy-done | bytes 131096
  14.1 0.7 %copy-done.5 = f32[16,256]{1,0:T(8,128)S(1)} copy-done((f32[16,256]{1,0:T(8,128)S(1)}, f32[16,256]{1,0:T(8,128)}, u32[]{:S(2)}) %copy-start.5) | copy-done | bytes 16408
  14.8 1.2 %mismatch_shares.2 = (f32[8,256]{1,0:T(8,128)S(1)}, f32[8,256]{1,0:T(8,128)S(1)}) custom-call(f32[16,256]{1,0:T(8,128)S(1)} %copy-done.5, f32[280,128]{1,0:T(8,128)} %get-tuple-element.27.edge_ref.edge1_ref.own_ref, f32[256,128]{1,0:T(8,128)S(1)} %copy-done.4), custom_call_target="tpu_custom_call" | custom-call | tf_op jit(solution)/shard_map/mismatch_shares/pallas_call | solution.py:518
  16.0 1.6 %collective-permute-start.4 = (f32[8,256]{1,0:T(8,128)S(1)}, f32[8,256]{1,0:T(8,128)S(1)}, u32[]{:S(2)}, u32[]{:S(2)}) collective-permute-start(f32[8,256]{1,0:T(8,128)S(1)} %get-tuple-element.35), channel_id=1, source_target_pairs={{2,0},{0,2},{3,1},{1,3},{6,4},{4,6},{7,5},{5,7},{10,8},{8,10},{11,... | collective-permute-start | bytes 24584 | tf_op jit(solution)/shard_map/ppermute | solution.py:426
  17.5 2.2 %collective-permute-done.4 = f32[8,256]{1,0:T(8,128)S(1)} collective-permute-done((f32[8,256]{1,0:T(8,128)S(1)}, f32[8,256]{1,0:T(8,128)S(1)}, u32[]{:S(2)}, u32[]{:S(2)}) %collective-permute-start.4) | collective-permute-done | bytes 8224 | tf_op jit(solution)/shard_map/ppermute | solution.py:426
  19.9 1.5 %collective-permute-start.1 = (f32[280,128]{1,0:T(8,128)}, f32[280,128]{1,0:T(8,128)S(1)}, u32[]{:S(2)}, u32[]{:S(2)}) collective-permute-start(f32[280,128]{1,0:T(8,128)} %get-tuple-element.27.edge_ref.edge1_ref.own_ref), channel_id=1, source_target_pairs={{2,0},{0,2},{3,1},{1,3},{6,4},{4,6},{7,5},{5,7},{10,8},{8,10},{11,... | collective-permute-start | bytes 430088 | tf_op jit(solution)/shard_map/ppermute | solution.py:426
  21.4 1.8 %collective-permute-start = (f32[280,128]{1,0:T(8,128)}, f32[280,128]{1,0:T(8,128)S(1)}, u32[]{:S(2)}, u32[]{:S(2)}) collective-permute-start(f32[280,128]{1,0:T(8,128)} %get-tuple-element.27.edge_ref.edge1_ref.own_ref), channel_id=1, source_target_pairs={{0,4},{4,0},{8,12},{12,8},{1,5},{5,1},{9,13},{13,9},{2,6},{6,2},{1... | collective-permute-start | bytes 430088 | tf_op jit(solution)/shard_map/ppermute | solution.py:425
  23.4 1.7 %collective-permute-start.6 = (f32[8,256]{1,0:T(8,128)S(1)}, f32[8,256]{1,0:T(8,128)S(1)}, u32[]{:S(2)}, u32[]{:S(2)}) collective-permute-start(f32[8,256]{1,0:T(8,128)S(1)} %add.13.refs_0_), channel_id=1, source_target_pairs={{0,8},{4,12},{8,0},{12,4},{1,9},{5,13},{9,1},{13,5},{2,10},{6,14},... | collective-permute-start | bytes 24584 | tf_op jit(solution)/shard_map/ppermute | solution.py:425
  25.1 1.1 %copy-done.8 = bf16[128,2304]{1,0:T(8,128)(2,1)S(1)} copy-done((bf16[128,2304]{1,0:T(8,128)(2,1)S(1)}, bf16[128,2304]{1,0:T(8,128)(2,1)}, u32[]{:S(2)}) %copy-start.8) | copy-done | bytes 589848
  28.0 4.8 %second_round.1 = (f32[256,128]{1,0:T(8,128)S(1)}, f32[256,128]{1,0:T(8,128)S(1)}, f32[16,256]{1,0:T(8,128)S(1)}) custom-call(f32[256,256]{1,0:T(8,128)S(1)} %copy-done.1, f32[256,128]{1,0:T(8,128)S(1)} %coupling.3.coupling_ref, f32[256,256]{1,0:T(8,128)S(1)} %copy-done, bf16[256,256]{1,0:T(8,128)(2,1)S(1)} %copy-done.2, bf16[256,256]{1,0:T(8,128)(2,1)S(1)} %copy-done.3, ...), custom_call_target="tpu_custom_call" | custom-call | tf_op jit(solution)/shard_map/second_round/pallas_call | solution.py:541
  32.9 2.7 %collective-permute-start.8 = (f32[256,128]{1,0:T(8,128)S(1)}, f32[256,128]{1,0:T(8,128)S(1)}, u32[]{:S(2)}, u32[]{:S(2)}) collective-permute-start(f32[256,128]{1,0:T(8,128)S(1)} %get-tuple-element.36.edge_ref), channel_id=1, source_target_pairs={{0,8},{4,12},{8,0},{12,4},{1,9},{5,13},{9,1},{13,5},{2,10},{6,14},... | collective-permute-start | bytes 393224 | tf_op jit(solution)/shard_map/ppermute | solution.py:425
  35.6 1.3 %collective-permute-start.7 = (f32[256,128]{1,0:T(8,128)S(1)}, f32[256,128]{1,0:T(8,128)S(1)}, u32[]{:S(2)}, u32[]{:S(2)}) collective-permute-start(f32[256,128]{1,0:T(8,128)S(1)} %get-tuple-element.36.edge_ref), channel_id=1, source_target_pairs={{0,12},{4,8},{8,4},{12,0},{1,13},{5,9},{9,5},{13,1},{2,14},{6,10},... | collective-permute-start | bytes 393224 | tf_op jit(solution)/shard_map/ppermute | solution.py:425
  37.2 1.2 %collective-permute-start.11 = (f32[8,256]{1,0:T(8,128)S(1)}, f32[8,256]{1,0:T(8,128)S(1)}, u32[]{:S(2)}, u32[]{:S(2)}) collective-permute-start(f32[8,256]{1,0:T(8,128)S(1)} %get-tuple-element.44), channel_id=1, source_target_pairs={{2,0},{0,2},{3,1},{1,3},{6,4},{4,6},{7,5},{5,7},{10,8},{8,10},{11,... | collective-permute-start | bytes 24584 | tf_op jit(solution)/shard_map/ppermute | solution.py:426
  38.4 2.5 %collective-permute-done.11 = f32[8,256]{1,0:T(8,128)S(1)} collective-permute-done((f32[8,256]{1,0:T(8,128)S(1)}, f32[8,256]{1,0:T(8,128)S(1)}, u32[]{:S(2)}, u32[]{:S(2)}) %collective-permute-start.11) | collective-permute-done | bytes 8224 | tf_op jit(solution)/shard_map/ppermute | solution.py:426
  40.9 0.8 %injection.1 = f32[1,256,256]{2,1,0:T(8,128)} custom-call(f32[256,128]{1,0:T(8,128)S(1)} %get-tuple-element.36.edge_ref, f32[256,128]{1,0:T(8,128)S(1)} %get-tuple-element.37.rest_ref), custom_call_target="tpu_custom_call" | custom-call | tf_op jit(solution)/shard_map/injection/pallas_call | solution.py:556
  41.7 1.1 %collective-permute-start.10 = (f32[256,128]{1,0:T(8,128)S(1)}, f32[256,128]{1,0:T(8,128)S(1)}, u32[]{:S(2)}, u32[]{:S(2)}) collective-permute-start(f32[256,128]{1,0:T(8,128)S(1)} %get-tuple-element.36.edge_ref), channel_id=1, source_target_pairs={{2,0},{0,2},{3,1},{1,3},{6,4},{4,6},{7,5},{5,7},{10,8},{8,10},{11,... | collective-permute-start | bytes 393224 | tf_op jit(solution)/shard_map/ppermute | solution.py:426
  42.9 2.0 %collective-permute-start.9 = (f32[256,128]{1,0:T(8,128)S(1)}, f32[256,128]{1,0:T(8,128)S(1)}, u32[]{:S(2)}, u32[]{:S(2)}) collective-permute-start(f32[256,128]{1,0:T(8,128)S(1)} %get-tuple-element.36.edge_ref), channel_id=1, source_target_pairs={{0,4},{4,0},{8,12},{12,8},{1,5},{5,1},{9,13},{13,9},{2,6},{6,2},{1... | collective-permute-start | bytes 393224 | tf_op jit(solution)/shard_map/ppermute | solution.py:425
  44.9 1.9 %line_table.1 = (bf16[6,384,128]{2,1,0:T(8,128)(2,1)S(1)}, bf16[6,384,128]{2,1,0:T(8,128)(2,1)S(1)}) custom-call(f32[280,128]{1,0:T(8,128)} %get-tuple-element.27.edge_ref.edge1_ref.own_ref, f32[280,128]{1,0:T(8,128)S(1)} %collective-permute-done.2.refs_0_.refs_2_, f32[280,128]{1,0:T(8,128)S(1)} %collective-permute-done.3.refs_1_.refs_3_, ...), custom_call_target="tpu_custom_call" | custom-call | tf_op jit(solution)/shard_map/line_table/pallas_call | solution.py:564
  47.3 1.5 %collective-permute-start.13 = (f32[8,256]{1,0:T(8,128)S(1)}, f32[8,256]{1,0:T(8,128)S(1)}, u32[]{:S(2)}, u32[]{:S(2)}) collective-permute-start(f32[8,256]{1,0:T(8,128)S(1)} %add.15.refs_4_), channel_id=1, source_target_pairs={{0,8},{4,12},{8,0},{12,4},{1,9},{5,13},{9,1},{13,5},{2,10},{6,14},... | collective-permute-start | bytes 24584 | tf_op jit(solution)/shard_map/ppermute | solution.py:425
  48.9 3.1 %collective-permute-done.13.refs_5_ = f32[8,256]{1,0:T(8,128)S(1)} collective-permute-done((f32[8,256]{1,0:T(8,128)S(1)}, f32[8,256]{1,0:T(8,128)S(1)}, u32[]{:S(2)}, u32[]{:S(2)}) %collective-permute-start.13) | collective-permute-done | bytes 8224 | tf_op jit(solution)/shard_map/ppermute | solution.py:425
  52.0 2.4 %tie_flows.1 = (f32[1,6,384,256]{3,2,1,0:T(8,128)}, f32[4,256]{1,0:T(4,128)}) custom-call(bf16[6,384,128]{2,1,0:T(8,128)(2,1)S(1)} %get-tuple-element.38.table_ref, f32[6,384,256]{2,1,0:T(8,128)S(1)} %own_flows.1.own_ref, f32[16,256]{1,0:T(8,128)S(1)} %get-tuple-element.40.sums_ref, bf16[256,256]{1,0:T(8,128)(2,1)S(1)} %get-tuple-element.41.refs_0_, ...), custom_call_target="tpu_custom_call" | custom-call | tf_op jit(solution)/shard_map/tie_flows/pallas_call | solution.py:589
  (37 shorter events, 3.0 us)
Async XLA Ops:
  7.7 17.4 %collective-permute-start.3 = (f32[280,128]{1,0:T(8,128)}, f32[280,128]{1,0:T(8,128)S(1)}, u32[]{:S(2)}, u32[]{:S(2)}) collective-permute-start(f32[280,128]{1,0:T(8,128)} %get-tuple-element.27.edge_ref.edge1_ref.own_ref), channel_id=1, source_target_pairs={{0,8},{4,12},{8,0},{12,4},{1,9},{5,13},{9,1},{13,5},{2,10},{6,14},... | collective-permute-start | bytes 430088 | tf_op jit(solution)/shard_map/ppermute | solution.py:425
  11.8 13.3 %collective-permute-start.2 = (f32[280,128]{1,0:T(8,128)}, f32[280,128]{1,0:T(8,128)S(1)}, u32[]{:S(2)}, u32[]{:S(2)}) collective-permute-start(f32[280,128]{1,0:T(8,128)} %get-tuple-element.27.edge_ref.edge1_ref.own_ref), channel_id=1, source_target_pairs={{0,12},{4,8},{8,4},{12,0},{1,13},{5,9},{9,5},{13,1},{2,14},{6,10},... | collective-permute-start | bytes 430088 | tf_op jit(solution)/shard_map/ppermute | solution.py:425
  13.2 0.9 %copy-start.4 = (f32[256,128]{1,0:T(8,128)S(1)}, f32[256,128]{1,0:T(8,128)}, u32[]{:S(2)}) copy-start(f32[256,128]{1,0:T(8,128)} %get-tuple-element.33.rest_ref) | copy-start | bytes 393220
  14.1 0.7 %copy-start.5 = (f32[16,256]{1,0:T(8,128)S(1)}, f32[16,256]{1,0:T(8,128)}, u32[]{:S(2)}) copy-start(f32[16,256]{1,0:T(8,128)} %get-tuple-element.32.weight_ref) | copy-start | bytes 49156
  16.0 3.7 %collective-permute-start.4 = (f32[8,256]{1,0:T(8,128)S(1)}, f32[8,256]{1,0:T(8,128)S(1)}, u32[]{:S(2)}, u32[]{:S(2)}) collective-permute-start(f32[8,256]{1,0:T(8,128)S(1)} %get-tuple-element.35), channel_id=1, source_target_pairs={{2,0},{0,2},{3,1},{1,3},{6,4},{4,6},{7,5},{5,7},{10,8},{8,10},{11,... | collective-permute-start | bytes 24584 | tf_op jit(solution)/shard_map/ppermute | solution.py:426
  19.7 3.7 %collective-permute-start.5 = (f32[8,256]{1,0:T(8,128)S(1)}, f32[8,256]{1,0:T(8,128)S(1)}, u32[]{:S(2)}, u32[]{:S(2)}) collective-permute-start(f32[8,256]{1,0:T(8,128)S(1)} %add.12), channel_id=1, source_target_pairs={{0,4},{4,0},{8,12},{12,8},{1,5},{5,1},{9,13},{13,9},{2,6},{6,2},{1... | collective-permute-start | bytes 24584 | tf_op jit(solution)/shard_map/ppermute | solution.py:425
  19.9 7.0 %collective-permute-start.1 = (f32[280,128]{1,0:T(8,128)}, f32[280,128]{1,0:T(8,128)S(1)}, u32[]{:S(2)}, u32[]{:S(2)}) collective-permute-start(f32[280,128]{1,0:T(8,128)} %get-tuple-element.27.edge_ref.edge1_ref.own_ref), channel_id=1, source_target_pairs={{2,0},{0,2},{3,1},{1,3},{6,4},{4,6},{7,5},{5,7},{10,8},{8,10},{11,... | collective-permute-start | bytes 430088 | tf_op jit(solution)/shard_map/ppermute | solution.py:426
  21.4 5.5 %collective-permute-start = (f32[280,128]{1,0:T(8,128)}, f32[280,128]{1,0:T(8,128)S(1)}, u32[]{:S(2)}, u32[]{:S(2)}) collective-permute-start(f32[280,128]{1,0:T(8,128)} %get-tuple-element.27.edge_ref.edge1_ref.own_ref), channel_id=1, source_target_pairs={{0,4},{4,0},{8,12},{12,8},{1,5},{5,1},{9,13},{13,9},{2,6},{6,2},{1... | collective-permute-start | bytes 430088 | tf_op jit(solution)/shard_map/ppermute | solution.py:425
  23.4 4.5 %collective-permute-start.6 = (f32[8,256]{1,0:T(8,128)S(1)}, f32[8,256]{1,0:T(8,128)S(1)}, u32[]{:S(2)}, u32[]{:S(2)}) collective-permute-start(f32[8,256]{1,0:T(8,128)S(1)} %add.13.refs_0_), channel_id=1, source_target_pairs={{0,8},{4,12},{8,0},{12,4},{1,9},{5,13},{9,1},{13,5},{2,10},{6,14},... | collective-permute-start | bytes 24584 | tf_op jit(solution)/shard_map/ppermute | solution.py:425
  25.1 1.1 %copy-start.8 = (bf16[128,2304]{1,0:T(8,128)(2,1)S(1)}, bf16[128,2304]{1,0:T(8,128)(2,1)}, u32[]{:S(2)}) copy-start(bf16[128,2304]{1,0:T(8,128)(2,1)} %get-tuple-element.26.own_ref) | copy-start | bytes 1769476
  26.9 1.1 %copy-start = (f32[256,256]{1,0:T(8,128)S(1)}, f32[256,256]{1,0:T(8,128)}, u32[]{:S(2)}) copy-start(f32[256,256]{1,0:T(8,128)} %get-tuple-element.28.v_ref) | copy-start | bytes 786436
  26.9 1.1 %copy-start.1 = (f32[256,256]{1,0:T(8,128)S(1)}, f32[256,256]{1,0:T(8,128)}, u32[]{:S(2)}) copy-start(f32[256,256]{1,0:T(8,128)} %get-tuple-element.25.lin_ref) | copy-start | bytes 786436
  26.9 1.1 %copy-start.2 = (bf16[256,256]{1,0:T(8,128)(2,1)S(1)}, bf16[256,256]{1,0:T(8,128)(2,1)}, u32[]{:S(2)}) copy-start(bf16[256,256]{1,0:T(8,128)(2,1)} %get-tuple-element.29.kh_ref) | copy-start | bytes 393220
  26.9 1.1 %copy-start.3 = (bf16[256,256]{1,0:T(8,128)(2,1)S(1)}, bf16[256,256]{1,0:T(8,128)(2,1)}, u32[]{:S(2)}) copy-start(bf16[256,256]{1,0:T(8,128)(2,1)} %get-tuple-element.30.kl_ref) | copy-start | bytes 393220
  26.9 1.1 %copy-start.7 = (f32[1,256]{1,0:T(1,128)S(1)}, f32[1,256]{1,0:T(1,128)}, u32[]{:S(2)}) copy-start(f32[1,256]{1,0:T(1,128)} %get-tuple-element.31.cap_ref) | copy-start | bytes 3076
  26.9 10.0 %copy-start.6 = (f32[16,256]{1,0:T(8,128)S(1)}, f32[16,256]{1,0:T(8,128)}, u32[]{:S(2)}) copy-start(f32[16,256]{1,0:T(8,128)} %get-tuple-element.32.weight_ref) | copy-start | bytes 49156
  32.9 16.0 %collective-permute-start.8 = (f32[256,128]{1,0:T(8,128)S(1)}, f32[256,128]{1,0:T(8,128)S(1)}, u32[]{:S(2)}, u32[]{:S(2)}) collective-permute-start(f32[256,128]{1,0:T(8,128)S(1)} %get-tuple-element.36.edge_ref), channel_id=1, source_target_pairs={{0,8},{4,12},{8,0},{12,4},{1,9},{5,13},{9,1},{13,5},{2,10},{6,14},... | collective-permute-start | bytes 393224 | tf_op jit(solution)/shard_map/ppermute | solution.py:425
  35.6 13.2 %collective-permute-start.7 = (f32[256,128]{1,0:T(8,128)S(1)}, f32[256,128]{1,0:T(8,128)S(1)}, u32[]{:S(2)}, u32[]{:S(2)}) collective-permute-start(f32[256,128]{1,0:T(8,128)S(1)} %get-tuple-element.36.edge_ref), channel_id=1, source_target_pairs={{0,12},{4,8},{8,4},{12,0},{1,13},{5,9},{9,5},{13,1},{2,14},{6,10},... | collective-permute-start | bytes 393224 | tf_op jit(solution)/shard_map/ppermute | solution.py:425
  37.2 3.7 %collective-permute-start.11 = (f32[8,256]{1,0:T(8,128)S(1)}, f32[8,256]{1,0:T(8,128)S(1)}, u32[]{:S(2)}, u32[]{:S(2)}) collective-permute-start(f32[8,256]{1,0:T(8,128)S(1)} %get-tuple-element.44), channel_id=1, source_target_pairs={{2,0},{0,2},{3,1},{1,3},{6,4},{4,6},{7,5},{5,7},{10,8},{8,10},{11,... | collective-permute-start | bytes 24584 | tf_op jit(solution)/shard_map/ppermute | solution.py:426
  40.9 6.4 %collective-permute-start.12 = (f32[8,256]{1,0:T(8,128)S(1)}, f32[8,256]{1,0:T(8,128)S(1)}, u32[]{:S(2)}, u32[]{:S(2)}) collective-permute-start(f32[8,256]{1,0:T(8,128)S(1)} %add.14), channel_id=1, source_target_pairs={{0,4},{4,0},{8,12},{12,8},{1,5},{5,1},{9,13},{13,9},{2,6},{6,2},{1... | collective-permute-start | bytes 24584 | tf_op jit(solution)/shard_map/ppermute | solution.py:425
  41.7 10.2 %collective-permute-start.10 = (f32[256,128]{1,0:T(8,128)S(1)}, f32[256,128]{1,0:T(8,128)S(1)}, u32[]{:S(2)}, u32[]{:S(2)}) collective-permute-start(f32[256,128]{1,0:T(8,128)S(1)} %get-tuple-element.36.edge_ref), channel_id=1, source_target_pairs={{2,0},{0,2},{3,1},{1,3},{6,4},{4,6},{7,5},{5,7},{10,8},{8,10},{11,... | collective-permute-start | bytes 393224 | tf_op jit(solution)/shard_map/ppermute | solution.py:426
  42.9 9.1 %collective-permute-start.9 = (f32[256,128]{1,0:T(8,128)S(1)}, f32[256,128]{1,0:T(8,128)S(1)}, u32[]{:S(2)}, u32[]{:S(2)}) collective-permute-start(f32[256,128]{1,0:T(8,128)S(1)} %get-tuple-element.36.edge_ref), channel_id=1, source_target_pairs={{0,4},{4,0},{8,12},{12,8},{1,5},{5,1},{9,13},{13,9},{2,6},{6,2},{1... | collective-permute-start | bytes 393224 | tf_op jit(solution)/shard_map/ppermute | solution.py:425
  47.3 4.6 %collective-permute-start.13 = (f32[8,256]{1,0:T(8,128)S(1)}, f32[8,256]{1,0:T(8,128)S(1)}, u32[]{:S(2)}, u32[]{:S(2)}) collective-permute-start(f32[8,256]{1,0:T(8,128)S(1)} %add.15.refs_4_), channel_id=1, source_target_pairs={{0,8},{4,12},{8,0},{12,4},{1,9},{5,13},{9,1},{13,5},{2,10},{6,14},... | collective-permute-start | bytes 24584 | tf_op jit(solution)/shard_map/ppermute | solution.py:425

commit v3 on v2

v3 whole, which is shorter than its diff:
```python
import functools

import jax
import jax.numpy as jnp
from jax import lax
from jax.experimental import pallas as pl
from jax.experimental.pallas import tpu as pltpu
from jax.sharding import PartitionSpec as P

ZONES = 4
INNER = 24
BOUNDARY = 128
LANES = 128
ZONE_GAIN = 0.004
SYSTEM_GAIN = 0.001
SLOTS = (
    ("area", 1, 1),
    ("area", -1, 0),
    ("area", 2, 3),
    ("area", -2, 2),
    ("region", 1, 5),
    ("region", -1, 4),
)
SIGNS = (1.0, -1.0, 1.0, -1.0, 1.0, -1.0)
CHAIN_ROWS = 32
UNROLL = 4
BIG = 4 * 10**9
OPENING = 10**11

F32 = jnp.float32
BF16 = jnp.bfloat16
VMEM = pl.BlockSpec(memory_space=pltpu.VMEM)
SMEM = pl.BlockSpec(memory_space=pltpu.SMEM)
HBM = pl.BlockSpec(memory_space=pltpu.HBM)
PARAMS = pltpu.CompilerParams(vmem_limit_bytes=40 * 2**20)


def dot(a, b):
    return jnp.dot(a, b, preferred_element_type=F32)


def dot_nt(a, b):
    return lax.dot_general(a, b, (((1,), (1,)), ((), ())), preferred_element_type=F32)


def halves(x):
    high = x.astype(BF16)
    return high, (x - high.astype(F32)).astype(BF16)


def thirds(x):
    high = x.astype(BF16)
    rest = x - high.astype(F32)
    middle = rest.astype(BF16)
    return high, middle, (rest - middle.astype(F32)).astype(BF16)


def clipping(v, limits):
    clipped = jnp.clip(v, -limits, limits)
    return clipped, v - clipped


def run_sweeps(start, finish, lin_ref, over_ref, limits, kh_ref, kl_ref, count):
    scens, buses = lin_ref.shape
    chains = scens // CHAIN_ROWS

    def scoped(*accumulators):
        highs, lows = accumulators[:chains], accumulators[chains:]
        pltpu.matmul_push_rhs(kh_ref[...], 0, 0)
        pltpu.matmul_push_rhs(kl_ref[...], 0, 1)

        def issue(i, x, load=None):
            high, low = halves(x)
            pltpu.matmul_acc_lhs(highs[i], high, load)
            pltpu.matmul_acc_lhs(highs[i], low)
            pltpu.matmul_acc_lhs(lows[i], high, load)

        def rows_of(i):
            return pl.ds(i * CHAIN_ROWS, CHAIN_ROWS)

        def taken(i):
            return pltpu.matmul_pop(highs[i]) + pltpu.matmul_pop(lows[i])

        for i in range(chains):
            x, over = start(rows_of(i))
            over_ref[rows_of(i), :] = over
            issue(i, x, 0 if i == 0 else None)

        def sweep(_, carry):
            for i in range(chains):
                rows = rows_of(i)
                clipped, over = clipping(taken(i) + over_ref[rows, :], limits)
                over_ref[rows, :] = over
                issue(i, lin_ref[rows, :] + (clipped - over))
            return carry

        lax.fori_loop(0, count - 1, sweep, 0, unroll=UNROLL)
        for i in range(chains):
            finish(rows_of(i), taken(i), over_ref[rows_of(i), :])

    pl.run_scoped(
        scoped,
        *[pltpu.ACC(0)((CHAIN_ROWS, buses), F32)] * chains,
        *[pltpu.ACC(1)((CHAIN_ROWS, buses), F32)] * chains,
    )


def line_tables(areas, regions, slots, pieces, near, idx_row, number, own_ref, rows):
    me_area, me_region = lax.axis_index("area"), lax.axis_index("region")
    here = me_area if near else me_area * regions + me_region
    width = -(-rows // LANES) * LANES
    row_id = lax.broadcasted_iota(jnp.int32, (1, width), 1)
    line_id = lax.broadcasted_iota(jnp.int32, (1, LANES), 1).astype(F32)
    bus_id = lax.broadcasted_iota(jnp.int32, (BOUNDARY, LANES), 0).astype(F32)
    weights = jnp.zeros((BOUNDARY, width), F32)
    for p in range(slots):
        axis, move, _ = SLOTS[p]
        if axis == "area":
            other = lax.rem(me_area + move % areas, areas)
            there = other if near else other * regions + me_region
        else:
            there = areas + 1 if near else me_area * regions + lax.rem(me_region + move % regions, regions)
        coefficient = jnp.where(row_id == there, 0.5, 0.0) - jnp.where(row_id == here, 0.5, 0.0)
        met = None
        for j in range(pieces):
            row = jnp.where(line_id + float(j * LANES) < number(p), idx_row(p, j), -1.0)
            onehot = jnp.where(bus_id == row, 1.0, 0.0)
            own_ref[:, pl.ds((p * pieces + j) * LANES, LANES)] = onehot.astype(BF16)
            met = onehot if met is None else met + onehot
        weights = weights + jnp.sum(met, axis=1, keepdims=True) * coefficient
    last = areas if near else areas * regions
    mine = jnp.where((row_id == here) | (row_id == last), 1.0, 0.0)
    weights = jnp.concatenate([weights + mine, jnp.broadcast_to(mine, (BOUNDARY, width))], axis=0)
    return weights.T[0:rows, :]


def weighted_sums(weights, x):
    wh, wl = halves(weights)
    xh, xm, xl = thirds(x)
    return dot_nt(wh, xh) + (dot_nt(wh, xm) + dot_nt(wl, xh)) + (dot_nt(wh, xl) + dot_nt(wl, xm))


def folded(x):
    return jnp.concatenate([x[:, j : j + LANES] for j in range(0, x.shape[1], LANES)], axis=0)


def unfolded(x):
    return jnp.concatenate([x[j : j + 8, :] for j in range(0, x.shape[0], 8)], axis=1)


def opening_kernel(zeros_ref):
    zeros_ref[...] = jnp.zeros(zeros_ref.shape, F32)


def first_kernel(
    areas, regions, near, zeros_ref, k_ref, load_ref, cap_ref, idx_ref, active_ref, count_ref, zone_ref, *refs
):
    edge_ref, *lean_refs = refs[:-8]
    rest_ref, v_ref, lin_ref, kh_ref, kl_ref, own_ref, weight_ref, over_ref = refs[-8:]
    scens = lin_ref.shape[0]
    slots, _, lines = idx_ref.shape
    pieces = lines // LANES
    numbers = jnp.where(active_ref[...] > 0, count_ref[...], 0).astype(F32)
    zone = jnp.full((1, LANES), zone_ref[0].astype(F32))

    def idx_row(p, j):
        return idx_ref[p, :, pl.ds(j * LANES, LANES)].astype(F32)

    for ref, held in ((edge_ref, range(slots)), *zip(lean_refs, ((2, 3), (4, 5)))):
        ref[pl.ds(ref.shape[0] - 8, 8), :] = zeros_ref[...]
        at = scens
        for p in held:
            for j in range(pieces):
                ref[pl.ds(at, 1), :] = idx_row(p, j)
                at += 1
        ref[pl.ds(at, 1), :] = zone
    edge_ref[pl.ds(scens + slots * pieces + 1, 1), pl.ds(0, slots)] = numbers
    weight_ref[...] = line_tables(
        areas, regions, slots, pieces, near, idx_row, lambda p: numbers[:, p : p + 1], own_ref, weight_ref.shape[0]
    )
    high, low = halves(k_ref[0].T)
    kh_ref[...] = high
    kl_ref[...] = low
    lin_ref[...] = load_ref[0].T
    limits = cap_ref[...]

    def start(rows):
        return lin_ref[rows, :], jnp.zeros((CHAIN_ROWS, lin_ref.shape[1]), F32)

    def finish(rows, x, over):
        for ref in (edge_ref, *lean_refs):
            ref[rows, :] = x[:, :BOUNDARY]
        rest_ref[rows, :] = x[:, BOUNDARY:]
        v_ref[rows, :] = x + over

    run_sweeps(start, finish, lin_ref, over_ref, limits, kh_ref, kl_ref, INNER)


def share_kernel(areas, regions, near, zone_at, weight_ref, edge_ref, rest_ref, share_ref, *across_refs):
    scens = rest_ref.shape[0]
    x = jnp.concatenate([edge_ref[pl.ds(0, scens), :], rest_ref[...]], axis=1)
    sums = weighted_sums(weight_ref[...], x)
    if near:
        share_ref[...] = folded(sums[0:8, :])
        row_id = lax.broadcasted_iota(jnp.int32, (8, scens), 0)
        across = jnp.where(row_id == lax.axis_index("area"), sums[areas + 1 : areas + 2, :], 0.0)
        across_refs[0][...] = folded(jnp.where(row_id == areas, sums[areas : areas + 1, :], across))
        return
    if zone_at is not None:
        me = lax.axis_index("area") * regions + lax.axis_index("region")
        zone = edge_ref[pl.ds(zone_at, 1), pl.ds(0, 1)]
        row_id = lax.broadcasted_iota(jnp.int32, sums.shape, 0)
        sums = sums + jnp.where(row_id == areas * regions + 1 + me, zone, 0.0)
    share_ref[...] = sums[0 : share_ref.shape[0], :]


def append_kernel(scens, kept, zone_at, share_ref, across_ref, edge_ref, side_ref, pair_ref, full_ref, side_out_ref):
    pair = share_ref[...] + across_ref[...]
    rows = pair.shape[0]
    pair_ref[...] = pair
    full_ref[pl.ds(0, scens), :] = edge_ref[pl.ds(0, scens), :]
    full_ref[pl.ds(scens, rows), :] = pair
    if kept:
        full_ref[pl.ds(scens + rows, kept), :] = edge_ref[pl.ds(scens, kept), :]
        full_ref[pl.ds(scens + rows + kept, 1), :] = edge_ref[pl.ds(zone_at, 1), :]
    side_out_ref[...] = side_ref[...]


def live_lines(edge_ref, scens, slots, pieces, p):
    return edge_ref[pl.ds(scens + slots * pieces + 1, 1), pl.ds(p, 1)]


def by_area(values):
    me = lax.axis_index("area")
    out = []
    for k in range(4):
        mask = jnp.bitwise_xor(me, k)
        low = jnp.where(jnp.bitwise_and(mask, 1) == 0, values[0], values[1])
        high = jnp.where(jnp.bitwise_and(mask, 1) == 0, values[2], values[3])
        out.append(jnp.where(mask < 2, low, high))
    return out


def near_sums(scens, pair_ref, opposite_ref, far_ref, close_ref):
    rows = pl.ds(scens, pair_ref.shape[0])
    return unfolded((pair_ref[...] + close_ref[rows, :]) + (opposite_ref[...] + far_ref[rows, :]))


def near_prices(sums, zones, zone):
    price = sums[4:5, :] * SYSTEM_GAIN
    for k in range(4):
        price = price + jnp.where(zones[k] == zone, ZONE_GAIN, 0.0) * sums[k : k + 1, :]
    return price


def prices(shares, zones, total, regions, zone):
    ids = lax.broadcasted_iota(jnp.int32, zones.shape, 0)
    in_region = lax.rem(ids, regions) == lax.axis_index("region")
    gain = jnp.where(in_region & (zones == zone), ZONE_GAIN, 0.0) + SYSTEM_GAIN
    return jnp.sum(gain * shares[0:total, :], axis=0, keepdims=True)


class Mask(int):
    pass


class Plan:
    def __init__(self, areas, regions, scens, slots, pieces):
        self.near = (areas, regions) == (4, 2)
        self.scens, self.pieces = scens, pieces
        self.fold = 8 * (scens // LANES)
        if self.near:
            self.sources = [("area", Mask(2)), ("area", Mask(3)), ("area", Mask(1)), ("region", 1)]
            self.slots_of = [(2, 3), ((1, 0),), ((0, 1),), (4, 5)]
            self.buffer_of = [(2, 1), (1, 2), 0, 0, 3, 3]
            self.early = 1
            return
        self.sources, self.slots_of, self.buffer_of = [], [], [None] * slots
        for p in (2, 3, 0, 1, 4, 5):
            axis, move, _ = SLOTS[p]
            source = (axis, move % (areas if axis == "area" else regions))
            if source not in self.sources:
                self.sources.append(source)
                self.slots_of.append(())
            self.buffer_of[p] = self.sources.index(source)
            self.slots_of[self.buffer_of[p]] += (p,)
        self.early = max(self.buffer_of[2], self.buffer_of[3]) + 1

    def line_row(self, b, p, j):
        back = SLOTS[p][2]
        if self.near:
            back -= {0: 2, 3: 4}.get(b, 0)
        return self.scens + (self.fold if self.near and b in (1, 2) else 0) + back * self.pieces + j

    def zone_row(self, b):
        return self.scens + (self.fold if b in (1, 2) else 0) + 2 * self.pieces


def choice(entry, read):
    if isinstance(entry, int):
        return read(entry)
    even = lax.rem(lax.axis_index("area"), 2) == 0
    return jnp.where(even, read(entry[0]), read(entry[1]))


def coupling_kernel(plan, first, number, own_ref, *refs):
    got, before, coupling_ref = refs[:number], refs[number:-1], refs[-1]
    lines = plan.pieces * LANES
    bus_id = lax.broadcasted_iota(jnp.int32, (BOUNDARY, LANES), 0).astype(F32)
    counts = []
    for b, g in enumerate(got, first):
        met = None
        for entry in plan.slots_of[b]:
            mine = choice(entry, lambda p: own_ref[:, pl.ds(p * lines, lines)])
            there = []
            for j in range(plan.pieces):
                row = choice(entry, lambda p: g[pl.ds(plan.line_row(b, p, j), 1), :])
                there.append(jnp.where(bus_id == row, 1.0, 0.0).astype(BF16))
            pairs = dot_nt(mine, jnp.concatenate(there, axis=1))
            met = pairs if met is None else met + pairs
        counts.append(met)
    counts_high, counts_low = halves(jnp.concatenate(counts, axis=1))
    high, low = halves(jnp.concatenate([g[pl.ds(0, plan.scens), :] for g in got], axis=1))
    out = dot_nt(high, counts_high) + dot_nt(low, counts_high) + dot_nt(high, counts_low)
    for ref in before:
        out = out + ref[...]
    coupling_ref[...] = out


def second_kernel(
    areas, regions, plan, zone_at, lin_ref, coupling_ref, v_ref, kh_ref, kl_ref, cap_ref, edge1_ref, *refs
):
    edge_ref, rest_ref, sums_ref, lin2_ref, over_ref = refs[-5:]
    scens = lin_ref.shape[0]
    zone = edge1_ref[pl.ds(zone_at, 1), pl.ds(0, 1)]
    if plan.near:
        pair_ref, opposite_ref, *got = refs[:-5]
        sums = near_sums(scens, pair_ref, opposite_ref, got[1], got[2])
        zones = by_area([zone] + [got[b][pl.ds(plan.zone_row(b), 1), pl.ds(0, 1)] for b in (2, 0, 1)])
        price = near_prices(sums, zones, zone)
        sums_ref[pl.ds(0, 8), :] = sums
        sums_ref[pl.ds(8, 8), :] = jnp.zeros((8, scens), F32)
        for k in range(4):
            sums_ref[pl.ds(8 + k, 1), :] = jnp.broadcast_to(zones[k], (1, scens))
    else:
        total = areas * regions
        sums = refs[0][...]
        sums_ref[...] = sums
        price = prices(sums, sums[total + 1 : 2 * total + 1, :], total, regions, zone)
    price = jnp.broadcast_to(price, (8, scens)).T[:, 0:1]
    lin2_ref[:, pl.ds(0, BOUNDARY)] = lin_ref[:, pl.ds(0, BOUNDARY)] - price - coupling_ref[...]
    lin2_ref[:, pl.ds(BOUNDARY, BOUNDARY)] = lin_ref[:, pl.ds(BOUNDARY, BOUNDARY)] - price
    limits = cap_ref[...]

    def start(rows):
        clipped, over = clipping(v_ref[rows, :], limits)
        return lin2_ref[rows, :] + (clipped - over), over

    def finish(rows, x, over):
        edge_ref[rows, :] = x[:, :BOUNDARY]
        rest_ref[rows, :] = x[:, BOUNDARY:]

    run_sweeps(start, finish, lin2_ref, over_ref, limits, kh_ref, kl_ref, INNER)


def injection_kernel(edge_ref, rest_ref, injection_ref):
    scens = rest_ref.shape[0]
    injection_ref[0, pl.ds(0, BOUNDARY), :] = edge_ref[pl.ds(0, scens), :].T
    injection_ref[0, pl.ds(BOUNDARY, BOUNDARY), :] = rest_ref[...].T


def table_kernel(plan, own_ref, *refs):
    got = refs[:-2]
    mine_ref, theirs_ref = refs[-2:]
    slots, lines = mine_ref.shape[:2]
    pieces, scens = plan.pieces, plan.scens
    extra = own_ref.shape[0] - scens
    mine = own_ref[pl.ds(scens, extra), :].T
    rows = []
    for p in range(slots):
        rows += [choice(plan.buffer_of[p], lambda b: got[b][pl.ds(plan.line_row(b, p, j), 1), :]) for j in range(pieces)]
        rows.append(jnp.zeros((8 - pieces, LANES), F32))
    theirs = jnp.concatenate(rows, axis=0).T
    bus_id = lax.broadcasted_iota(jnp.int32, (LANES, BOUNDARY), 1).astype(F32)
    line_id = lax.broadcasted_iota(jnp.int32, (LANES, BOUNDARY), 0).astype(F32)
    for p in range(slots):
        number = live_lines(own_ref, scens, slots, pieces, p)
        half = 0.5 * SIGNS[p]
        for j in range(pieces):
            live = jnp.where(line_id + float(j * LANES) < number, half, 0.0)
            at = p * pieces + j
            there = p * 8 + j
            rows = pl.ds(j * LANES, LANES)
            mine_ref[p, rows, :] = jnp.where(bus_id == mine[:, at : at + 1], live, 0.0).astype(BF16)
            theirs_ref[p, rows, :] = jnp.where(bus_id == theirs[:, there : there + 1], -live, 0.0).astype(BF16)


def twice(x):
    return jnp.concatenate([x, x], axis=1)


def own_kernel(table_ref, edge_ref, flow_ref):
    scens = flow_ref.shape[2]
    parts = jnp.concatenate(halves(edge_ref[pl.ds(0, scens), :]), axis=1)
    for p in range(table_ref.shape[0]):
        flow_ref[p] = dot_nt(twice(table_ref[p]), parts)


def write_flows(plan, held, parts, table_ref, own_ref, flow_ref, flow_hbm, sems):
    copies = []
    for i, p in enumerate(held):
        part = choice(plan.buffer_of[p], lambda b: parts[b])
        flow_ref[i] = own_ref[p] + dot_nt(twice(table_ref[p]), part)
        copies.append(pltpu.make_async_copy(flow_ref.at[i], flow_hbm.at[0, p], sems.at[i]))
        copies[-1].start()
    return copies


def parts_of(plan, refs, first):
    return {b: jnp.concatenate(halves(ref[pl.ds(0, plan.scens), :]), axis=1) for b, ref in enumerate(refs, first)}


def early_kernel(plan, table_ref, own_ref, *refs):
    *got, flow_hbm, flow_ref, sems = refs
    parts = parts_of(plan, got, 0)
    for copy in write_flows(plan, (2, 3), parts, table_ref, own_ref, flow_ref, flow_hbm, sems):
        copy.wait()


def final_kernel(areas, regions, plan, number, table_ref, own_ref, sums_ref, *refs):
    got, rest = refs[:number], refs[number:-5]
    flow_hbm, price_ref, flow_ref, sems = refs[-4:]
    parts = parts_of(plan, got, plan.early)
    copies = write_flows(plan, (0, 1, 4, 5), parts, table_ref, own_ref, flow_ref, flow_hbm, sems)
    if plan.near:
        sums = sums_ref[pl.ds(0, 8), :] + near_sums(plan.scens, rest[0], rest[1], got[0], got[1])
        zones = [sums_ref[pl.ds(8 + k, 1), :] for k in range(4)]
        for z in range(ZONES):
            price_ref[pl.ds(z, 1), :] = near_prices(sums, zones, float(z))
    else:
        total = areas * regions
        first = sums_ref[...]
        zones = first[total + 1 : 2 * total + 1, :]
        for z in range(ZONES):
            price_ref[pl.ds(z, 1), :] = prices(first + rest[0][...], zones, total, regions, float(z))
    for copy in copies:
        copy.wait()


def moved(x, axis, by):
    length = lax.axis_size(axis)
    if isinstance(by, Mask):
        return lax.ppermute(x, axis, [(i, i ^ by) for i in range(length)])
    return lax.ppermute(x, axis, [((i + by) % length, i) for i in range(length)])


def body(kkt_inverse, scen_load, capacity, pair_active, tie_counts, line_index, area_zone):
    areas = lax.axis_size("area")
    regions = lax.axis_size("region")
    total = areas * regions
    _, buses, scens = scen_load.shape
    _, slots, lines = line_index.shape
    rest = buses - BOUNDARY
    pieces = lines // LANES
    plan = Plan(areas, regions, scens, slots, pieces)
    near, early = plan.near, plan.early
    zone_at = scens + slots * pieces
    share_rows = -(-(2 * total + 1) // 8) * 8
    weight_rows = 16 if near else -(-share_rows // 16) * 16

    def f32(*shape):
        return jax.ShapeDtypeStruct(shape, F32)

    def bf16(*shape):
        return jax.ShapeDtypeStruct(shape, BF16)

    def cost(flops):
        return pl.CostEstimate(flops=flops, bytes_accessed=0, transcendentals=0)

    def call(kernel, name, out_shape, operands, estimate=None, **more):
        return pl.pallas_call(
            kernel,
            out_shape=out_shape,
            in_specs=more.pop("in_specs", [VMEM] * len(operands)),
            out_specs=more.pop("out_specs", jax.tree.map(lambda _: VMEM, out_shape)),
            compiler_params=PARAMS,
            cost_estimate=estimate and cost(estimate),
            name=name,
            **more,
        )(*operands)

    def exchange(edge, rest, leans, weights, kept):
        held = edge.shape[0] > scens
        shapes = [f32(plan.fold, LANES)] * 2 if near else [f32(share_rows, scens)]
        share, *across = call(
            functools.partial(share_kernel, areas, regions, near, zone_at if held else None),
            "mismatch_shares",
            shapes,
            [weights, edge, rest],
        )
        if not near:
            return [moved(edge, axis, move) for axis, move in plan.sources], [lax.psum(share, ("area", "region"))]
        far, side = leans
        pair, full, side = call(
            functools.partial(append_kernel, scens, kept, zone_at),
            "pair_shares",
            [
                f32(plan.fold, LANES),
                f32(scens + plan.fold + -(-(kept and kept + 1) // 8) * 8, BOUNDARY),
                f32(*side.shape),
            ],
            [share, moved(across[0], "region", 1), edge, side],
        )
        got_side = moved(side, "region", 1)
        opposite = moved(pair, "area", Mask(2))
        got_near = moved(full, "area", Mask(1))
        got_other = moved(full, "area", Mask(3))
        return [moved(far, "area", Mask(2)), got_other, got_near, got_side], [pair, opposite]

    zeros = call(opening_kernel, "opening", f32(8, LANES), [], OPENING)
    lean_rows = -(-(scens + 2 * pieces + 1) // 8) * 8
    leans = [f32(lean_rows, BOUNDARY)] * 2 if near else []
    edge1, *more = call(
        functools.partial(first_kernel, areas, regions, near),
        "first_round",
        [
            f32(-(-(zone_at + 2) // 8) * 8, BOUNDARY),
            *leans,
            f32(scens, rest),
            f32(scens, buses),
            f32(scens, buses),
            bf16(buses, buses),
            bf16(buses, buses),
            bf16(BOUNDARY, slots * lines),
            f32(weight_rows, buses),
        ],
        [
            zeros,
            kkt_inverse,
            scen_load,
            capacity,
            line_index.reshape(slots, 1, lines),
            pair_active,
            tie_counts,
            area_zone,
        ],
        in_specs=[VMEM] * 7 + [SMEM],
        scratch_shapes=[pltpu.VMEM((scens, buses), F32)],
    )
    leans1, (rest1, state, lin, kh, kl, own, weights) = more[: len(leans)], more[len(leans) :]
    got1, sums1 = exchange(edge1, rest1, leans1, weights, 2 * pieces)
    coupling = call(
        functools.partial(coupling_kernel, plan, 0, early),
        "coupling",
        f32(scens, BOUNDARY),
        [own, *got1[:early]],
        BIG,
    )
    coupling = call(
        functools.partial(coupling_kernel, plan, early, len(got1) - early),
        "coupling",
        f32(scens, BOUNDARY),
        [own, *got1[early:], coupling],
        BIG,
    )
    edge2, rest2, first = call(
        functools.partial(second_kernel, areas, regions, plan, zone_at),
        "second_round",
        [f32(scens, BOUNDARY), f32(scens, rest), f32(16 if near else share_rows, scens)],
        [lin, coupling, state, kh, kl, capacity, edge1, *sums1, *(got1 if near else [])],
        scratch_shapes=[pltpu.VMEM((scens, buses), F32)] * 2,
    )
    got2, sums2 = exchange(edge2, rest2, [edge2] * 2, weights, 0)
    injection = call(injection_kernel, "injection", f32(1, buses, scens), [edge2, rest2])
    mine, theirs = call(
        functools.partial(table_kernel, plan),
        "line_table",
        [bf16(slots, lines, BOUNDARY)] * 2,
        [edge1, *got1],
    )
    own_flow = call(own_kernel, "own_flows", f32(slots, lines, scens), [mine, edge2])
    operands = [theirs, own_flow, *got2[:early]]
    flow = call(
        functools.partial(early_kernel, plan),
        "tie_flows_early",
        f32(1, slots, lines, scens),
        operands,
        BIG,
        out_specs=HBM,
        scratch_shapes=[pltpu.VMEM((2, lines, scens), F32), pltpu.SemaphoreType.DMA((2,))],
    )
    operands = [theirs, own_flow, first, *got2[early:], *sums2, flow]
    flow, price = call(
        functools.partial(final_kernel, areas, regions, plan, len(got2) - early),
        "tie_flows",
        (f32(1, slots, lines, scens), f32(ZONES, scens)),
        operands,
        BIG,
        in_specs=[VMEM] * (len(operands) - 1) + [HBM],
        out_specs=(HBM, VMEM),
        input_output_aliases={len(operands) - 1: 0},
        scratch_shapes=[pltpu.VMEM((slots - 2, lines, scens), F32), pltpu.SemaphoreType.DMA((slots - 2,))],
    )
    return injection, flow, price


def solution(mesh):
    placed = (
        P(("area", "region"), None, None),
        P(("area", "region"), None, ("group", "scen")),
        P(("area", "region"), None),
        P(("area", "region"), None),
        P(("area", "region"), None),
        P(("area", "region"), None, None),
        P(("area", "region")),
    )
    return jax.shard_map(
        body,
        mesh=mesh,
        in_specs=placed,
        out_specs=(
            P(("area", "region"), None, ("group", "scen")),
            P(("area", "region"), None, None, ("group", "scen")),
            P("region", ("group", "scen")),
        ),
        check_vma=False,
    )
```

time: 54.7 us -> 45.9 us (0.84)
  Pallas kernels: 19.6 us -> 15.4 us
  local copies, waits for them, and re-layouts: 2.71 us -> 0.31 us
  starting transfers between devices: 22.1 us -> 20 us
    pallas_call x11 -> x14, Pallas kernels: 19.6 us -> 15.4 us  [call(): pl.pallas_call(kernel, out_shape=out_shape, in_specs=more.pop('in_specs',...]
    ppermute x10 -> x8, starting transfers between devices: 16.7 us -> 14 us  [moved(): return lax.ppermute(x, axis, [(i, i ^ by) for i in range(length)])]
    unnamed x18 -> x12, local copies, waits for them, and re-layouts: 2.71 us -> 0.31 us
    ppermute x4, starting transfers between devices: 5.38 us -> 6.01 us  [moved(): lax.ppermute(x, axis, [((i + by) % length, i) for i in range(length)])]
    ppermute x10 -> x8, waiting for transfers between devices: 3.77 us -> 3.42 us  [moved(): return lax.ppermute(x, axis, [(i, i ^ by) for i in range(length)])]
  transfers between devices with their start and end apart: 14 -> 12, of which waited for: 5 -> 5; matrix products, arithmetic and copies ran while one was open for 0% -> 0% of each run, Pallas kernels for 11% -> 11%
where the time goes in v3:
time: 45.9 us; the launch traced here: 45.8 us
  starting transfers between devices  20 us (44%)
  Pallas kernels  15.4 us (34%)
  waiting for transfers between devices  8.59 us (19%)
  between operations  1.5 us (3%)
    pallas_call x14, Pallas kernels, call(): pl.pallas_call(kernel, out_shape=out_shape, in_specs=more.pop('in_specs',...  15.4 us
    ppermute x8, starting transfers between devices, moved(): return lax.ppermute(x, axis, [(i, i ^ by) for i in range(length)])  14 us
    ppermute x4, starting transfers between devices, moved(): lax.ppermute(x, axis, [((i + by) % length, i) for i in range(length)])  6.01 us
    ppermute x4, waiting for transfers between devices, moved(): lax.ppermute(x, axis, [((i + by) % length, i) for i in range(length)])  5.17 us
    ppermute x8, waiting for transfers between devices, moved(): return lax.ppermute(x, axis, [(i, i ^ by) for i in range(length)])  3.42 us
  transfers between devices with their start and end apart: 12, of which 5 were waited for; matrix products, arithmetic and copies ran while one was open for 0% of the time, Pallas kernels for 11%

profile of v3, /device:TPU:0, one launch (start us, length us, event | category | flops | bytes accessed | tf_op | source)
XLA Modules:
  0.0 45.8 jit_solution(17117516942116431076)
XLA Ops:
  1.7 4.3 %first_round.1 = (f32[280,128]{1,0:T(8,128)S(1)}, f32[264,128]{1,0:T(8,128)S(1)}, f32[264,128]{1,0:T(8,128)S(1)}, f32[256,128]{1,0:T(8,128)S(1)}, f32[256,256]{1...) custom-call(f32[8,128]{1,0:T(8,128)S(1)} %opening.1.zeros_ref, ...), custom_call_target="tpu_custom_call" | custom-call | tf_op jit(solution)/shard_map/first_round/pallas_call | solution.py:481
  6.0 4.1 %collective-permute-start.4 = (f32[264,128]{1,0:T(8,128)S(1)}, f32[264,128]{1,0:T(8,128)S(1)}, u32[]{:S(2)}, u32[]{:S(2)}) collective-permute-start(f32[264,128]{1,0:T(8,128)S(1)} %get-tuple-element.40), channel_id=1, source_target_pairs={{0,8},{4,12},{8,0},{12,4},{1,9},{5,13},{9,1},{13,5},{2,10},{6,14},... | collective-permute-start | bytes 405512 | tf_op jit(solution)/shard_map/ppermute | solution.py:453
  10.1 0.3 mismatch_shares.2
  10.4 1.6 %collective-permute-start = (f32[16,128]{1,0:T(8,128)S(1)}, f32[16,128]{1,0:T(8,128)S(1)}, u32[]{:S(2)}, u32[]{:S(2)}) collective-permute-start(f32[16,128]{1,0:T(8,128)S(1)} %get-tuple-element.36), channel_id=1, source_target_pairs={{2,0},{0,2},{3,1},{1,3},{6,4},{4,6},{7,5},{5,7},{10,8},{8,10},{11,... | collective-permute-start | bytes 24584 | tf_op jit(solution)/shard_map/ppermute | solution.py:454
  11.9 2.2 %collective-permute-done.across_ref = f32[16,128]{1,0:T(8,128)S(1)} collective-permute-done((f32[16,128]{1,0:T(8,128)S(1)}, f32[16,128]{1,0:T(8,128)S(1)}, u32[]{:S(2)}, u32[]{:S(2)}) %collective-permute-start) | collective-permute-done | bytes 8224 | tf_op jit(solution)/shard_map/ppermute | solution.py:454
  14.1 1.6 %collective-permute-start.2 = (f32[280,128]{1,0:T(8,128)S(1)}, f32[280,128]{1,0:T(8,128)S(1)}, u32[]{:S(2)}, u32[]{:S(2)}) collective-permute-start(f32[280,128]{1,0:T(8,128)S(1)} %get-tuple-element.38), channel_id=1, source_target_pairs={{0,4},{4,0},{8,12},{12,8},{1,5},{5,1},{9,13},{13,9},{2,6},{6,2},{1... | collective-permute-start | bytes 430088 | tf_op jit(solution)/shard_map/ppermute | solution.py:453
  15.8 1.9 %collective-permute-start.5 = (f32[16,128]{1,0:T(8,128)S(1)}, f32[16,128]{1,0:T(8,128)S(1)}, u32[]{:S(2)}, u32[]{:S(2)}) collective-permute-start(f32[16,128]{1,0:T(8,128)S(1)} %get-tuple-element.44.refs_0_), channel_id=1, source_target_pairs={{0,8},{4,12},{8,0},{12,4},{1,9},{5,13},{9,1},{13,5},{2,10},{6,14},... | collective-permute-start | bytes 24584 | tf_op jit(solution)/shard_map/ppermute | solution.py:453
  17.7 1.5 %collective-permute-start.3 = (f32[264,128]{1,0:T(8,128)S(1)}, f32[264,128]{1,0:T(8,128)S(1)}, u32[]{:S(2)}, u32[]{:S(2)}) collective-permute-start(f32[264,128]{1,0:T(8,128)S(1)} %get-tuple-element.39), channel_id=1, source_target_pairs={{2,0},{0,2},{3,1},{1,3},{6,4},{4,6},{7,5},{5,7},{10,8},{8,10},{11,... | collective-permute-start | bytes 405512 | tf_op jit(solution)/shard_map/ppermute | solution.py:454
  19.2 0.5 %coupling.2.refs_3_ = f32[256,128]{1,0:T(8,128)S(1)} custom-call(bf16[128,2304]{1,0:T(8,128)(2,1)S(1)} %get-tuple-element.31.own_ref, f32[264,128]{1,0:T(8,128)S(1)} %collective-permute-done.4.refs_0_.refs_2_), custom_call_target="tpu_custom_call" | custom-call | flops 4000000000 | tf_op jit(solution)/shard_map/coupling/pallas_call | solution.py:481
  19.7 3.0 %collective-permute-done.3.refs_2_.refs_5_.refs_3_ = f32[264,128]{1,0:T(8,128)S(1)} collective-permute-done((f32[264,128]{1,0:T(8,128)S(1)}, f32[264,128]{1,0:T(8,128)S(1)}, u32[]{:S(2)}, u32[]{:S(2)}) %collective-permute-start.3) | collective-permute-done | bytes 135200 | tf_op jit(solution)/shard_map/ppermute | solution.py:454
  22.8 0.6 %coupling.3.coupling_ref = f32[256,128]{1,0:T(8,128)S(1)} custom-call(bf16[128,2304]{1,0:T(8,128)(2,1)S(1)} %get-tuple-element.31.own_ref, f32[280,128]{1,0:T(8,128)S(1)} %collective-permute-done.1.refs_0_.refs_3_.refs_1_, f32[280,128]{1,0:T(8,128)S(1)} %collective-permute-done.2.refs_1_.refs_4_.refs_2_, ...), custom_call_target="tpu_custom_call" | custom-call | flops 4000000000 | tf_op jit(solution)/shard_map/coupling/pallas_call | solution.py:481
  23.6 3.9 %second_round.1 = (f32[256,128]{1,0:T(8,128)S(1)}, f32[256,128]{1,0:T(8,128)S(1)}, f32[16,256]{1,0:T(8,128)S(1)}) custom-call(f32[256,256]{1,0:T(8,128)S(1)} %get-tuple-element.30.lin_ref, f32[256,128]{1,0:T(8,128)S(1)} %coupling.3.coupling_ref, f32[256,256]{1,0:T(8,128)S(1)} %get-tuple-element.41.v_ref, bf16[256,256]{1,0:T(8,128)(2,1)S(1)} %get-tuple-element.42.kh_ref, ...), custom_call_target="tpu_custom_call" | custom-call | tf_op jit(solution)/shard_map/second_round/pallas_call | solution.py:481
  27.5 2.8 %collective-permute-start.11 = (f32[256,128]{1,0:T(8,128)S(1)}, f32[256,128]{1,0:T(8,128)S(1)}, u32[]{:S(2)}, u32[]{:S(2)}) collective-permute-start(f32[256,128]{1,0:T(8,128)S(1)} %get-tuple-element.45.edge_ref.side_ref), channel_id=1, source_target_pairs={{0,8},{4,12},{8,0},{12,4},{1,9},{5,13},{9,1},{13,5},{2,10},{6,14},... | collective-permute-start | bytes 393224 | tf_op jit(solution)/shard_map/ppermute | solution.py:453
  30.5 1.6 %collective-permute-start.6 = (f32[16,128]{1,0:T(8,128)S(1)}, f32[16,128]{1,0:T(8,128)S(1)}, u32[]{:S(2)}, u32[]{:S(2)}) collective-permute-start(f32[16,128]{1,0:T(8,128)S(1)} %get-tuple-element.51), channel_id=1, source_target_pairs={{2,0},{0,2},{3,1},{1,3},{6,4},{4,6},{7,5},{5,7},{10,8},{8,10},{11,... | collective-permute-start | bytes 24584 | tf_op jit(solution)/shard_map/ppermute | solution.py:454
  32.1 0.8 %injection.1 = f32[1,256,256]{2,1,0:T(8,128)} custom-call(f32[256,128]{1,0:T(8,128)S(1)} %get-tuple-element.45.edge_ref.side_ref, f32[256,128]{1,0:T(8,128)S(1)} %get-tuple-element.46.rest_ref), custom_call_target="tpu_custom_call" | custom-call | tf_op jit(solution)/shard_map/injection/pallas_call | solution.py:481
  32.9 0.9 %line_table.1 = (bf16[6,384,128]{2,1,0:T(8,128)(2,1)S(1)}, bf16[6,384,128]{2,1,0:T(8,128)(2,1)S(1)}) custom-call(f32[280,128]{1,0:T(8,128)S(1)} %get-tuple-element.33.edge_ref.edge1_ref.own_ref, f32[264,128]{1,0:T(8,128)S(1)} %collective-permute-done.4.refs_0_.refs_2_, f32[280,128]{1,0:T(8,128)S(1)} %collective-permute-done.1.refs_0_.refs_3_.refs_1_, ...), custom_call_target="tpu_custom_call" | custom-call | tf_op jit(solution)/shard_map/line_table/pallas_call | solution.py:481
  33.8 0.5 %own_flows.1.own_ref = f32[6,384,256]{2,1,0:T(8,128)S(1)} custom-call(bf16[6,384,128]{2,1,0:T(8,128)(2,1)S(1)} %get-tuple-element.48.table_ref, f32[256,128]{1,0:T(8,128)S(1)} %get-tuple-element.45.edge_ref.side_ref), custom_call_target="tpu_custom_call" | custom-call | tf_op jit(solution)/shard_map/own_flows/pallas_call | solution.py:481
  34.4 1.0 %collective-permute-start.8 = (f32[272,128]{1,0:T(8,128)S(1)}, f32[272,128]{1,0:T(8,128)S(1)}, u32[]{:S(2)}, u32[]{:S(2)}) collective-permute-start(f32[272,128]{1,0:T(8,128)S(1)} %get-tuple-element.52), channel_id=1, source_target_pairs={{0,4},{4,0},{8,12},{12,8},{1,5},{5,1},{9,13},{13,9},{2,6},{6,2},{1... | collective-permute-start | bytes 417800 | tf_op jit(solution)/shard_map/ppermute | solution.py:453
  35.4 1.0 %collective-permute-start.7 = (f32[272,128]{1,0:T(8,128)S(1)}, f32[272,128]{1,0:T(8,128)S(1)}, u32[]{:S(2)}, u32[]{:S(2)}) collective-permute-start(f32[272,128]{1,0:T(8,128)S(1)} %get-tuple-element.52), channel_id=1, source_target_pairs={{0,12},{4,8},{8,4},{12,0},{1,13},{5,9},{9,5},{13,1},{2,14},{6,10},... | collective-permute-start | bytes 417800 | tf_op jit(solution)/shard_map/ppermute | solution.py:453
  36.4 1.6 %collective-permute-start.10 = (f32[16,128]{1,0:T(8,128)S(1)}, f32[16,128]{1,0:T(8,128)S(1)}, u32[]{:S(2)}, u32[]{:S(2)}) collective-permute-start(f32[16,128]{1,0:T(8,128)S(1)} %get-tuple-element.54.refs_3_), channel_id=1, source_target_pairs={{0,8},{4,12},{8,0},{12,4},{1,9},{5,13},{9,1},{13,5},{2,10},{6,14},... | collective-permute-start | bytes 24584 | tf_op jit(solution)/shard_map/ppermute | solution.py:453
  37.9 1.4 %collective-permute-start.9 = (f32[256,128]{1,0:T(8,128)S(1)}, f32[256,128]{1,0:T(8,128)S(1)}, u32[]{:S(2)}, u32[]{:S(2)}) collective-permute-start(f32[256,128]{1,0:T(8,128)S(1)} %get-tuple-element.53), channel_id=1, source_target_pairs={{2,0},{0,2},{3,1},{1,3},{6,4},{4,6},{7,5},{5,7},{10,8},{8,10},{11,... | collective-permute-start | bytes 393224 | tf_op jit(solution)/shard_map/ppermute | solution.py:454
  39.3 1.2 %tie_flows_early.1.refs_5_ = f32[1,6,384,256]{3,2,1,0:T(8,128)} custom-call(bf16[6,384,128]{2,1,0:T(8,128)(2,1)S(1)} %get-tuple-element.47.table_ref, f32[6,384,256]{2,1,0:T(8,128)S(1)} %own_flows.1.own_ref, f32[256,128]{1,0:T(8,128)S(1)} %collective-permute-done.11.refs_0_), custom_call_target="tpu_custom_call" | custom-call | flops 4000000000 | tf_op jit(solution)/shard_map/tie_flows_early/pallas_call | solution.py:481
  40.6 3.1 %collective-permute-done.10.refs_4_ = f32[16,128]{1,0:T(8,128)S(1)} collective-permute-done((f32[16,128]{1,0:T(8,128)S(1)}, f32[16,128]{1,0:T(8,128)S(1)}, u32[]{:S(2)}, u32[]{:S(2)}) %collective-permute-start.10) | collective-permute-done | bytes 8224 | tf_op jit(solution)/shard_map/ppermute | solution.py:453
  43.6 2.1 %tie_flows.1 = (f32[1,6,384,256]{3,2,1,0:T(8,128)}, f32[4,256]{1,0:T(4,128)}) custom-call(bf16[6,384,128]{2,1,0:T(8,128)(2,1)S(1)} %get-tuple-element.47.table_ref, f32[6,384,256]{2,1,0:T(8,128)S(1)} %own_flows.1.own_ref, f32[16,256]{1,0:T(8,128)S(1)} %get-tuple-element.49.sums_ref, ...), custom_call_target="tpu_custom_call", output_to_operand_aliasing={{0}: (8, {})} | custom-call | flops 4000000000 | tf_op jit(solution)/shard_map/tie_flows/pallas_call | solution.py:481
  (26 shorter events, 1.0 us)
Async XLA Ops:
  0.6 0.8 %copy-start.3 = (f32[1,256]{1,0:T(1,128)S(1)}, f32[1,256]{1,0:T(1,128)}, u32[]{:S(2)}) copy-start(f32[1,256]{1,0:T(1,128)} %cap_ref.3) | copy-start | bytes 3076
  0.6 0.8 %copy-start.2 = (s32[1,6,384]{2,0,1:T(1,128)S(1)}, s32[1,6,384]{2,0,1:T(1,128)}, u32[]{:S(2)}) copy-start(s32[1,6,384]{2,0,1:T(1,128)} %param.12) | copy-start | bytes 27652
  0.7 0.8 %copy-start.5 = (s32[1,6]{1,0:T(1,128)S(1)}, s32[1,6]{1,0:T(1,128)}, u32[]{:S(2)}) copy-start(s32[1,6]{1,0:T(1,128)} %count_ref.1) | copy-start | bytes 76
  0.7 0.8 %copy-start.4 = (s32[1,6]{1,0:T(1,128)S(1)}, s32[1,6]{1,0:T(1,128)}, u32[]{:S(2)}) copy-start(s32[1,6]{1,0:T(1,128)} %active_ref.1) | copy-start | bytes 76
  0.7 1.0 %copy-start.1 = (f32[1,256,256]{2,1,0:T(8,128)S(1)}, f32[1,256,256]{2,1,0:T(8,128)}, u32[]{:S(2)}) copy-start(f32[1,256,256]{2,1,0:T(8,128)} %load_ref.1) | copy-start | bytes 786436
  0.7 1.1 %copy-start = (f32[1,256,256]{2,1,0:T(8,128)S(1)}, f32[1,256,256]{2,1,0:T(8,128)}, u32[]{:S(2)}) copy-start(f32[1,256,256]{2,1,0:T(8,128)} %k_ref.1) | copy-start | bytes 786436
  6.0 13.2 %collective-permute-start.4 = (f32[264,128]{1,0:T(8,128)S(1)}, f32[264,128]{1,0:T(8,128)S(1)}, u32[]{:S(2)}, u32[]{:S(2)}) collective-permute-start(f32[264,128]{1,0:T(8,128)S(1)} %get-tuple-element.40), channel_id=1, source_target_pairs={{0,8},{4,12},{8,0},{12,4},{1,9},{5,13},{9,1},{13,5},{2,10},{6,14},... | collective-permute-start | bytes 405512 | tf_op jit(solution)/shard_map/ppermute | solution.py:453
  10.4 3.7 %collective-permute-start = (f32[16,128]{1,0:T(8,128)S(1)}, f32[16,128]{1,0:T(8,128)S(1)}, u32[]{:S(2)}, u32[]{:S(2)}) collective-permute-start(f32[16,128]{1,0:T(8,128)S(1)} %get-tuple-element.36), channel_id=1, source_target_pairs={{2,0},{0,2},{3,1},{1,3},{6,4},{4,6},{7,5},{5,7},{10,8},{8,10},{11,... | collective-permute-start | bytes 24584 | tf_op jit(solution)/shard_map/ppermute | solution.py:454
  14.1 8.7 %collective-permute-start.2 = (f32[280,128]{1,0:T(8,128)S(1)}, f32[280,128]{1,0:T(8,128)S(1)}, u32[]{:S(2)}, u32[]{:S(2)}) collective-permute-start(f32[280,128]{1,0:T(8,128)S(1)} %get-tuple-element.38), channel_id=1, source_target_pairs={{0,4},{4,0},{8,12},{12,8},{1,5},{5,1},{9,13},{13,9},{2,6},{6,2},{1... | collective-permute-start | bytes 430088 | tf_op jit(solution)/shard_map/ppermute | solution.py:453
  15.8 7.1 %collective-permute-start.1 = (f32[280,128]{1,0:T(8,128)S(1)}, f32[280,128]{1,0:T(8,128)S(1)}, u32[]{:S(2)}, u32[]{:S(2)}) collective-permute-start(f32[280,128]{1,0:T(8,128)S(1)} %get-tuple-element.38), channel_id=1, source_target_pairs={{0,12},{4,8},{8,4},{12,0},{1,13},{5,9},{9,5},{13,1},{2,14},{6,10},... | collective-permute-start | bytes 430088 | tf_op jit(solution)/shard_map/ppermute | solution.py:453
  15.8 7.8 %collective-permute-start.5 = (f32[16,128]{1,0:T(8,128)S(1)}, f32[16,128]{1,0:T(8,128)S(1)}, u32[]{:S(2)}, u32[]{:S(2)}) collective-permute-start(f32[16,128]{1,0:T(8,128)S(1)} %get-tuple-element.44.refs_0_), channel_id=1, source_target_pairs={{0,8},{4,12},{8,0},{12,4},{1,9},{5,13},{9,1},{13,5},{2,10},{6,14},... | collective-permute-start | bytes 24584 | tf_op jit(solution)/shard_map/ppermute | solution.py:453
  17.7 5.0 %collective-permute-start.3 = (f32[264,128]{1,0:T(8,128)S(1)}, f32[264,128]{1,0:T(8,128)S(1)}, u32[]{:S(2)}, u32[]{:S(2)}) collective-permute-start(f32[264,128]{1,0:T(8,128)S(1)} %get-tuple-element.39), channel_id=1, source_target_pairs={{2,0},{0,2},{3,1},{1,3},{6,4},{4,6},{7,5},{5,7},{10,8},{8,10},{11,... | collective-permute-start | bytes 405512 | tf_op jit(solution)/shard_map/ppermute | solution.py:454
  27.5 11.8 %collective-permute-start.11 = (f32[256,128]{1,0:T(8,128)S(1)}, f32[256,128]{1,0:T(8,128)S(1)}, u32[]{:S(2)}, u32[]{:S(2)}) collective-permute-start(f32[256,128]{1,0:T(8,128)S(1)} %get-tuple-element.45.edge_ref.side_ref), channel_id=1, source_target_pairs={{0,8},{4,12},{8,0},{12,4},{1,9},{5,13},{9,1},{13,5},{2,10},{6,14},... | collective-permute-start | bytes 393224 | tf_op jit(solution)/shard_map/ppermute | solution.py:453
  30.5 3.8 %collective-permute-start.6 = (f32[16,128]{1,0:T(8,128)S(1)}, f32[16,128]{1,0:T(8,128)S(1)}, u32[]{:S(2)}, u32[]{:S(2)}) collective-permute-start(f32[16,128]{1,0:T(8,128)S(1)} %get-tuple-element.51), channel_id=1, source_target_pairs={{2,0},{0,2},{3,1},{1,3},{6,4},{4,6},{7,5},{5,7},{10,8},{8,10},{11,... | collective-permute-start | bytes 24584 | tf_op jit(solution)/shard_map/ppermute | solution.py:454
  34.4 9.3 %collective-permute-start.8 = (f32[272,128]{1,0:T(8,128)S(1)}, f32[272,128]{1,0:T(8,128)S(1)}, u32[]{:S(2)}, u32[]{:S(2)}) collective-permute-start(f32[272,128]{1,0:T(8,128)S(1)} %get-tuple-element.52), channel_id=1, source_target_pairs={{0,4},{4,0},{8,12},{12,8},{1,5},{5,1},{9,13},{13,9},{2,6},{6,2},{1... | collective-permute-start | bytes 417800 | tf_op jit(solution)/shard_map/ppermute | solution.py:453
  35.4 8.3 %collective-permute-start.7 = (f32[272,128]{1,0:T(8,128)S(1)}, f32[272,128]{1,0:T(8,128)S(1)}, u32[]{:S(2)}, u32[]{:S(2)}) collective-permute-start(f32[272,128]{1,0:T(8,128)S(1)} %get-tuple-element.52), channel_id=1, source_target_pairs={{0,12},{4,8},{8,4},{12,0},{1,13},{5,9},{9,5},{13,1},{2,14},{6,10},... | collective-permute-start | bytes 417800 | tf_op jit(solution)/shard_map/ppermute | solution.py:453
  36.4 7.3 %collective-permute-start.10 = (f32[16,128]{1,0:T(8,128)S(1)}, f32[16,128]{1,0:T(8,128)S(1)}, u32[]{:S(2)}, u32[]{:S(2)}) collective-permute-start(f32[16,128]{1,0:T(8,128)S(1)} %get-tuple-element.54.refs_3_), channel_id=1, source_target_pairs={{0,8},{4,12},{8,0},{12,4},{1,9},{5,13},{9,1},{13,5},{2,10},{6,14},... | collective-permute-start | bytes 24584 | tf_op jit(solution)/shard_map/ppermute | solution.py:453
  37.9 5.7 %collective-permute-start.9 = (f32[256,128]{1,0:T(8,128)S(1)}, f32[256,128]{1,0:T(8,128)S(1)}, u32[]{:S(2)}, u32[]{:S(2)}) collective-permute-start(f32[256,128]{1,0:T(8,128)S(1)} %get-tuple-element.53), channel_id=1, source_target_pairs={{2,0},{0,2},{3,1},{1,3},{6,4},{4,6},{7,5},{5,7},{10,8},{8,10},{11,... | collective-permute-start | bytes 393224 | tf_op jit(solution)/shard_map/ppermute | solution.py:454

commit v4 on v3

--- a/solution.py
+++ b/solution.py
@@ -273,7 +273,8 @@
             self.sources = [("area", Mask(2)), ("area", Mask(3)), ("area", Mask(1)), ("region", 1)]
             self.slots_of = [(2, 3), ((1, 0),), ((0, 1),), (4, 5)]
             self.buffer_of = [(2, 1), (1, 2), 0, 0, 3, 3]
-            self.early = 1
+            self.arrivals = [(0,), (1, 2, 3)]
+            self.last = (1, 2, 3)
             return
         self.sources, self.slots_of, self.buffer_of = [], [], [None] * slots
         for p in (2, 3, 0, 1, 4, 5):
@@ -284,7 +285,8 @@
                 self.slots_of.append(())
             self.buffer_of[p] = self.sources.index(source)
             self.slots_of[self.buffer_of[p]] += (p,)
-        self.early = max(self.buffer_of[2], self.buffer_of[3]) + 1
+        self.arrivals = [tuple(range(len(self.sources)))]
+        self.last = self.arrivals[0]
 
     def line_row(self, b, p, j):
         back = SLOTS[p][2]
@@ -303,12 +305,12 @@
     return jnp.where(even, read(entry[0]), read(entry[1]))
 
 
-def coupling_kernel(plan, first, number, own_ref, *refs):
-    got, before, coupling_ref = refs[:number], refs[number:-1], refs[-1]
+def coupling_kernel(plan, held, own_ref, *refs):
+    got, before, coupling_ref = refs[: len(held)], refs[len(held) : -1], refs[-1]
     lines = plan.pieces * LANES
     bus_id = lax.broadcasted_iota(jnp.int32, (BOUNDARY, LANES), 0).astype(F32)
     counts = []
-    for b, g in enumerate(got, first):
+    for b, g in zip(held, got):
         met = None
         for entry in plan.slots_of[b]:
             mine = choice(entry, lambda p: own_ref[:, pl.ds(p * lines, lines)])
@@ -328,13 +330,15 @@
 
 
 def second_kernel(
-    areas, regions, plan, zone_at, lin_ref, coupling_ref, v_ref, kh_ref, kl_ref, cap_ref, edge1_ref, *refs
+    areas, regions, plan, zone_at, *refs
 ):
+    *front, lin_ref, coupling_ref, v_ref, kh_ref, kl_ref, cap_ref, edge1_ref = refs[:-6]
+    refs = (*front, *refs[-6:])
     edge_ref, rest_ref, sums_ref, lin2_ref, over_ref = refs[-5:]
     scens = lin_ref.shape[0]
     zone = edge1_ref[pl.ds(zone_at, 1), pl.ds(0, 1)]
     if plan.near:
-        pair_ref, opposite_ref, *got = refs[:-5]
+        pair_ref, opposite_ref, *got = refs[:-6]
         sums = near_sums(scens, pair_ref, opposite_ref, got[1], got[2])
         zones = by_area([zone] + [got[b][pl.ds(plan.zone_row(b), 1), pl.ds(0, 1)] for b in (2, 0, 1)])
         price = near_prices(sums, zones, zone)
@@ -369,30 +373,33 @@
     injection_ref[0, pl.ds(BOUNDARY, BOUNDARY), :] = rest_ref[...].T
 
 
+def own_table_kernel(plan, own_ref, table_ref):
+    pieces, scens = plan.pieces, plan.scens
+    mine = own_ref[pl.ds(scens, own_ref.shape[0] - scens), :].T
+    fill_table(plan, own_ref, table_ref, 0.5, lambda p, j: mine[:, p * pieces + j : p * pieces + j + 1])
+
+
+def fill_table(plan, own_ref, table_ref, half, column):
+    slots, pieces, scens = table_ref.shape[0], plan.pieces, plan.scens
+    bus_id = lax.broadcasted_iota(jnp.int32, (LANES, BOUNDARY), 1).astype(F32)
+    line_id = lax.broadcasted_iota(jnp.int32, (LANES, BOUNDARY), 0).astype(F32)
+    for p in range(slots):
+        number = live_lines(own_ref, scens, slots, pieces, p)
+        for j in range(pieces):
+            live = jnp.where(line_id + float(j * LANES) < number, half * SIGNS[p], 0.0)
+            table_ref[p, pl.ds(j * LANES, LANES), :] = jnp.where(bus_id == column(p, j), live, 0.0).astype(BF16)
+
+
 def table_kernel(plan, own_ref, *refs):
-    got = refs[:-2]
-    mine_ref, theirs_ref = refs[-2:]
-    slots, lines = mine_ref.shape[:2]
-    pieces, scens = plan.pieces, plan.scens
-    extra = own_ref.shape[0] - scens
-    mine = own_ref[pl.ds(scens, extra), :].T
+    got = refs[:-1]
+    table_ref = refs[-1]
+    slots, pieces = table_ref.shape[0], plan.pieces
     rows = []
     for p in range(slots):
         rows += [choice(plan.buffer_of[p], lambda b: got[b][pl.ds(plan.line_row(b, p, j), 1), :]) for j in range(pieces)]
         rows.append(jnp.zeros((8 - pieces, LANES), F32))
     theirs = jnp.concatenate(rows, axis=0).T
-    bus_id = lax.broadcasted_iota(jnp.int32, (LANES, BOUNDARY), 1).astype(F32)
-    line_id = lax.broadcasted_iota(jnp.int32, (LANES, BOUNDARY), 0).astype(F32)
-    for p in range(slots):
-        number = live_lines(own_ref, scens, slots, pieces, p)
-        half = 0.5 * SIGNS[p]
-        for j in range(pieces):
-            live = jnp.where(line_id + float(j * LANES) < number, half, 0.0)
-            at = p * pieces + j
-            there = p * 8 + j
-            rows = pl.ds(j * LANES, LANES)
-            mine_ref[p, rows, :] = jnp.where(bus_id == mine[:, at : at + 1], live, 0.0).astype(BF16)
-            theirs_ref[p, rows, :] = jnp.where(bus_id == theirs[:, there : there + 1], -live, 0.0).astype(BF16)
+    fill_table(plan, own_ref, table_ref, -0.5, lambda p, j: theirs[:, p * 8 + j : p * 8 + j + 1])
 
 
 def twice(x):
@@ -416,35 +423,42 @@
     return copies
 
 
-def parts_of(plan, refs, first):
-    return {b: jnp.concatenate(halves(ref[pl.ds(0, plan.scens), :]), axis=1) for b, ref in enumerate(refs, first)}
-
-
-def early_kernel(plan, table_ref, own_ref, *refs):
-    *got, flow_hbm, flow_ref, sems = refs
-    parts = parts_of(plan, got, 0)
-    for copy in write_flows(plan, (2, 3), parts, table_ref, own_ref, flow_ref, flow_hbm, sems):
+def parts_of(plan, refs, held):
+    return {b: jnp.concatenate(halves(ref[pl.ds(0, plan.scens), :]), axis=1) for b, ref in zip(held, refs)}
+
+
+def parts_kernel(ref, part_ref):
+    part_ref[...] = jnp.concatenate(halves(ref[pl.ds(0, part_ref.shape[0]), :]), axis=1)
+
+
+def final_kernel(plan, table_ref, own_ref, *refs):
+    *got, flow_hbm, done_ref, flow_ref, sems = refs
+    if plan.near:
+        parts = {0: got[0][...]}
+        got = got[1:]
+    else:
+        parts = {}
+    parts.update(parts_of(plan, got, plan.last))
+    copies = write_flows(plan, (2, 3, 4, 5, 0, 1), parts, table_ref, own_ref, flow_ref, flow_hbm, sems)
+    done_ref[...] = jnp.zeros(done_ref.shape, F32)
+    for copy in copies:
         copy.wait()
 
 
-def final_kernel(areas, regions, plan, number, table_ref, own_ref, sums_ref, *refs):
-    got, rest = refs[:number], refs[number:-5]
-    flow_hbm, price_ref, flow_ref, sems = refs[-4:]
-    parts = parts_of(plan, got, plan.early)
-    copies = write_flows(plan, (0, 1, 4, 5), parts, table_ref, own_ref, flow_ref, flow_hbm, sems)
-    if plan.near:
-        sums = sums_ref[pl.ds(0, 8), :] + near_sums(plan.scens, rest[0], rest[1], got[0], got[1])
-        zones = [sums_ref[pl.ds(8 + k, 1), :] for k in range(4)]
+def price_kernel(areas, regions, near, first_ref, done_ref, *refs):
+    *rest, price_ref = refs
+    if near:
+        own, one, two, three = rest
+        sums = first_ref[pl.ds(0, 8), :] + unfolded((own[...] + one[...]) + (two[...] + three[...]))
+        zones = [first_ref[pl.ds(8 + k, 1), :] for k in range(4)]
         for z in range(ZONES):
             price_ref[pl.ds(z, 1), :] = near_prices(sums, zones, float(z))
-    else:
-        total = areas * regions
-        first = sums_ref[...]
-        zones = first[total + 1 : 2 * total + 1, :]
-        for z in range(ZONES):
-            price_ref[pl.ds(z, 1), :] = prices(first + rest[0][...], zones, total, regions, float(z))
-    for copy in copies:
-        copy.wait()
+        return
+    total = areas * regions
+    first = first_ref[...]
+    zones = first[total + 1 : 2 * total + 1, :]
+    for z in range(ZONES):
+        price_ref[pl.ds(z, 1), :] = prices(first + rest[0][...], zones, total, regions, float(z))
 
 
 def moved(x, axis, by):
@@ -463,7 +477,7 @@
     rest = buses - BOUNDARY
     pieces = lines // LANES
     plan = Plan(areas, regions, scens, slots, pieces)
-    near, early = plan.near, plan.early
+    near = plan.near
     zone_at = scens + slots * pieces
     share_rows = -(-(2 * total + 1) // 8) * 8
     weight_rows = 16 if near else -(-share_rows // 16) * 16
@@ -488,6 +502,17 @@
             name=name,
             **more,
         )(*operands)
+
+    def exchange_last(edge, rest, weights):
+        got = [moved(edge, axis, move) for axis, move in plan.sources[::-1]][::-1]
+        share, across = call(
+            functools.partial(share_kernel, areas, regions, near, None),
+            "mismatch_shares",
+            [f32(plan.fold, LANES)] * 2,
+            [weights, edge, rest],
+        )
+        pair = share + moved(across, "region", 1)
+        return got, [pair, *(moved(pair, "area", Mask(mask)) for mask in (1, 2, 3))]
 
     def exchange(edge, rest, leans, weights, kept):
         held = edge.shape[0] > scens
@@ -549,57 +574,50 @@
     )
     leans1, (rest1, state, lin, kh, kl, own, weights) = more[: len(leans)], more[len(leans) :]
     got1, sums1 = exchange(edge1, rest1, leans1, weights, 2 * pieces)
-    coupling = call(
-        functools.partial(coupling_kernel, plan, 0, early),
-        "coupling",
-        f32(scens, BOUNDARY),
-        [own, *got1[:early]],
-        BIG,
-    )
-    coupling = call(
-        functools.partial(coupling_kernel, plan, early, len(got1) - early),
-        "coupling",
-        f32(scens, BOUNDARY),
-        [own, *got1[early:], coupling],
-        BIG,
-    )
+    coupling = []
+    for held in plan.arrivals:
+        coupling = [
+            call(
+                functools.partial(coupling_kernel, plan, held),
+                "coupling",
+                f32(scens, BOUNDARY),
+                [own, *(got1[b] for b in held), *coupling],
+                BIG,
+            )
+        ]
+    mine = call(functools.partial(own_table_kernel, plan), "own_table", bf16(slots, lines, BOUNDARY), [edge1])
     edge2, rest2, first = call(
         functools.partial(second_kernel, areas, regions, plan, zone_at),
         "second_round",
         [f32(scens, BOUNDARY), f32(scens, rest), f32(16 if near else share_rows, scens)],
-        [lin, coupling, state, kh, kl, capacity, edge1, *sums1, *(got1 if near else [])],
+        [*sums1, *(got1 if near else []), lin, *coupling, state, kh, kl, capacity, edge1, mine],
         scratch_shapes=[pltpu.VMEM((scens, buses), F32)] * 2,
     )
-    got2, sums2 = exchange(edge2, rest2, [edge2] * 2, weights, 0)
+    if near:
+        got2, sums2 = exchange_last(edge2, rest2, weights)
+    else:
+        got2, sums2 = exchange(edge2, rest2, [], weights, 0)
     injection = call(injection_kernel, "injection", f32(1, buses, scens), [edge2, rest2])
-    mine, theirs = call(
-        functools.partial(table_kernel, plan),
-        "line_table",
-        [bf16(slots, lines, BOUNDARY)] * 2,
-        [edge1, *got1],
-    )
+    theirs = call(functools.partial(table_kernel, plan), "line_table", bf16(slots, lines, BOUNDARY), [edge1, *got1])
     own_flow = call(own_kernel, "own_flows", f32(slots, lines, scens), [mine, edge2])
-    operands = [theirs, own_flow, *got2[:early]]
-    flow = call(
-        functools.partial(early_kernel, plan),
-        "tie_flows_early",
-        f32(1, slots, lines, scens),
-        operands,
+    operands = got2
+    if near:
+        far = call(parts_kernel, "injection_parts", bf16(scens, 2 * BOUNDARY), got2[:1], BIG)
+        operands = [far, *(got2[b] for b in plan.last)]
+    flow, done = call(
+        functools.partial(final_kernel, plan),
+        "tie_flows",
+        (f32(1, slots, lines, scens), f32(8, LANES)),
+        [theirs, own_flow, *operands],
         BIG,
-        out_specs=HBM,
-        scratch_shapes=[pltpu.VMEM((2, lines, scens), F32), pltpu.SemaphoreType.DMA((2,))],
-    )
-    operands = [theirs, own_flow, first, *got2[early:], *sums2, flow]
-    flow, price = call(
-        functools.partial(final_kernel, areas, regions, plan, len(got2) - early),
-        "tie_flows",
-        (f32(1, slots, lines, scens), f32(ZONES, scens)),
-        operands,
-        BIG,
-        in_specs=[VMEM] * (len(operands) - 1) + [HBM],
         out_specs=(HBM, VMEM),
-        input_output_aliases={len(operands) - 1: 0},
-        scratch_shapes=[pltpu.VMEM((slots - 2, lines, scens), F32), pltpu.SemaphoreType.DMA((slots - 2,))],
+        scratch_shapes=[pltpu.VMEM((slots, lines, scens), F32), pltpu.SemaphoreType.DMA((slots,))],
+    )
+    price = call(
+        functools.partial(price_kernel, areas, regions, near),
+        "zone_prices",
+        f32(ZONES, scens),
+        [first, done, *sums2],
     )
     return injection, flow, price
 

time: 45.9 us -> 44.8 us (0.976)
  waiting for transfers between devices: 8.59 us -> 4.95 us
  starting transfers between devices: 20 us -> 23.2 us
  Pallas kernels: 15.4 us -> 14.7 us
    ppermute x8 -> x10, starting transfers between devices: 14 us -> 18 us  [moved(): return lax.ppermute(x, axis, [(i, i ^ by) for i in range(length)])]
    ppermute x8 -> x10, waiting for transfers between devices: 3.42 us -> 0.35 us  [moved(): return lax.ppermute(x, axis, [(i, i ^ by) for i in range(length)])]
    ppermute x4, starting transfers between devices: 6.01 us -> 5.14 us  [moved(): lax.ppermute(x, axis, [((i + by) % length, i) for i in range(length)])]
    pallas_call x14 -> x15, Pallas kernels: 15.4 us -> 14.7 us  [call(): pl.pallas_call(kernel, out_shape=out_shape, in_specs=more.pop('in_specs',...]
    ppermute x4, waiting for transfers between devices: 5.17 us -> 4.61 us  [moved(): lax.ppermute(x, axis, [((i + by) % length, i) for i in range(length)])]
  transfers between devices with their start and end apart: 12 -> 14, of which waited for: 5 -> 4; matrix products, arithmetic and copies ran while one was open for 0% -> 0% of each run, Pallas kernels for 11% -> 13%
where the time goes in v4:
time: 44.8 us; the launch traced here: 44.7 us
  starting transfers between devices  23.2 us (52%)
  Pallas kernels  14.7 us (33%)
  waiting for transfers between devices  4.95 us (11%)
  between operations  1.54 us (3%)
    ppermute x10, starting transfers between devices, moved(): return lax.ppermute(x, axis, [(i, i ^ by) for i in range(length)])  18 us
    pallas_call x15, Pallas kernels, call(): pl.pallas_call(kernel, out_shape=out_shape, in_specs=more.pop('in_specs',...  14.7 us
    ppermute x4, starting transfers between devices, moved(): lax.ppermute(x, axis, [((i + by) % length, i) for i in range(length)])  5.14 us
    ppermute x4, waiting for transfers between devices, moved(): lax.ppermute(x, axis, [((i + by) % length, i) for i in range(length)])  4.61 us
  transfers between devices with their start and end apart: 14, of which 4 were waited for; matrix products, arithmetic and copies ran while one was open for 0% of the time, Pallas kernels for 13%

profile of v4, /device:TPU:0, one launch (start us, length us, event | category | flops | bytes accessed | tf_op | source)
XLA Modules:
  0.0 44.7 jit_solution(12414323833288928689)
XLA Ops:
  1.7 4.3 %first_round.1 = (f32[280,128]{1,0:T(8,128)S(1)}, f32[264,128]{1,0:T(8,128)S(1)}, f32[264,128]{1,0:T(8,128)S(1)}, f32[256,128]{1,0:T(8,128)S(1)}, f32[256,256]{1...) custom-call(f32[8,128]{1,0:T(8,128)S(1)} %opening.1.zeros_ref, ...), custom_call_target="tpu_custom_call" | custom-call | tf_op jit(solution)/shard_map/first_round/pallas_call | solution.py:495
  6.0 4.1 %collective-permute-start.2 = (f32[264,128]{1,0:T(8,128)S(1)}, f32[264,128]{1,0:T(8,128)S(1)}, u32[]{:S(2)}, u32[]{:S(2)}) collective-permute-start(f32[264,128]{1,0:T(8,128)S(1)} %get-tuple-element.32), channel_id=1, source_target_pairs={{0,8},{4,12},{8,0},{12,4},{1,9},{5,13},{9,1},{13,5},{2,10},{6,14},... | collective-permute-start | bytes 405512 | tf_op jit(solution)/shard_map/ppermute | solution.py:467
  10.4 1.6 %collective-permute-start = (f32[16,128]{1,0:T(8,128)S(1)}, f32[16,128]{1,0:T(8,128)S(1)}, u32[]{:S(2)}, u32[]{:S(2)}) collective-permute-start(f32[16,128]{1,0:T(8,128)S(1)} %get-tuple-element.29), channel_id=1, source_target_pairs={{2,0},{0,2},{3,1},{1,3},{6,4},{4,6},{7,5},{5,7},{10,8},{8,10},{11,... | collective-permute-start | bytes 24584 | tf_op jit(solution)/shard_map/ppermute | solution.py:468
  11.9 0.6 %own_table.1.refs_13_.table_ref = bf16[6,384,128]{2,1,0:T(8,128)(2,1)S(1)} custom-call(f32[280,128]{1,0:T(8,128)S(1)} %get-tuple-element.26.edge_ref.own_ref.refs_12_), custom_call_target="tpu_custom_call" | custom-call | tf_op jit(solution)/shard_map/own_table/pallas_call | solution.py:495
  12.5 1.6 %collective-permute-done.across_ref = f32[16,128]{1,0:T(8,128)S(1)} collective-permute-done((f32[16,128]{1,0:T(8,128)S(1)}, f32[16,128]{1,0:T(8,128)S(1)}, u32[]{:S(2)}, u32[]{:S(2)}) %collective-permute-start) | collective-permute-done | bytes 8224 | tf_op jit(solution)/shard_map/ppermute | solution.py:468
  14.1 1.6 %collective-permute-start.4 = (f32[280,128]{1,0:T(8,128)S(1)}, f32[280,128]{1,0:T(8,128)S(1)}, u32[]{:S(2)}, u32[]{:S(2)}) collective-permute-start(f32[280,128]{1,0:T(8,128)S(1)} %get-tuple-element.33), channel_id=1, source_target_pairs={{0,4},{4,0},{8,12},{12,8},{1,5},{5,1},{9,13},{13,9},{2,6},{6,2},{1... | collective-permute-start | bytes 430088 | tf_op jit(solution)/shard_map/ppermute | solution.py:467
  15.8 1.9 %collective-permute-start.1 = (f32[16,128]{1,0:T(8,128)S(1)}, f32[16,128]{1,0:T(8,128)S(1)}, u32[]{:S(2)}, u32[]{:S(2)}) collective-permute-start(f32[16,128]{1,0:T(8,128)S(1)} %get-tuple-element.31.refs_0_), channel_id=1, source_target_pairs={{0,8},{4,12},{8,0},{12,4},{1,9},{5,13},{9,1},{13,5},{2,10},{6,14},... | collective-permute-start | bytes 24584 | tf_op jit(solution)/shard_map/ppermute | solution.py:467
  17.7 1.5 %collective-permute-start.5 = (f32[264,128]{1,0:T(8,128)S(1)}, f32[264,128]{1,0:T(8,128)S(1)}, u32[]{:S(2)}, u32[]{:S(2)}) collective-permute-start(f32[264,128]{1,0:T(8,128)S(1)} %get-tuple-element.34), channel_id=1, source_target_pairs={{2,0},{0,2},{3,1},{1,3},{6,4},{4,6},{7,5},{5,7},{10,8},{8,10},{11,... | collective-permute-start | bytes 405512 | tf_op jit(solution)/shard_map/ppermute | solution.py:468
  19.2 0.5 %coupling.2.refs_3_ = f32[256,128]{1,0:T(8,128)S(1)} custom-call(bf16[128,2304]{1,0:T(8,128)(2,1)S(1)} %get-tuple-element.36.own_ref, f32[264,128]{1,0:T(8,128)S(1)} %collective-permute-done.2.refs_0_.refs_2_), custom_call_target="tpu_custom_call" | custom-call | flops 4000000000 | tf_op jit(solution)/shard_map/coupling/pallas_call | solution.py:495
  19.7 3.0 %collective-permute-done.5.refs_2_.refs_5_.refs_3_ = f32[264,128]{1,0:T(8,128)S(1)} collective-permute-done((f32[264,128]{1,0:T(8,128)S(1)}, f32[264,128]{1,0:T(8,128)S(1)}, u32[]{:S(2)}, u32[]{:S(2)}) %collective-permute-start.5) | collective-permute-done | bytes 135200 | tf_op jit(solution)/shard_map/ppermute | solution.py:468
  22.8 0.6 %coupling.3.refs_7_ = f32[256,128]{1,0:T(8,128)S(1)} custom-call(bf16[128,2304]{1,0:T(8,128)(2,1)S(1)} %get-tuple-element.36.own_ref, f32[280,128]{1,0:T(8,128)S(1)} %collective-permute-done.3.refs_0_.refs_3_.refs_1_, f32[280,128]{1,0:T(8,128)S(1)} %collective-permute-done.4.refs_1_.refs_4_.refs_2_, ...), custom_call_target="tpu_custom_call" | custom-call | flops 4000000000 | tf_op jit(solution)/shard_map/coupling/pallas_call | solution.py:495
  23.6 3.9 %second_round.1 = (f32[256,128]{1,0:T(8,128)S(1)}, f32[256,128]{1,0:T(8,128)S(1)}, f32[16,256]{1,0:T(8,128)S(1)}) custom-call(f32[16,128]{1,0:T(8,128)S(1)} %get-tuple-element.31.refs_0_, f32[16,128]{1,0:T(8,128)S(1)} %collective-permute-done.1.refs_1_, f32[264,128]{1,0:T(8,128)S(1)} %collective-permute-done.2.refs_0_.refs_2_, ...), custom_call_target="tpu_custom_call" | custom-call | tf_op jit(solution)/shard_map/second_round/pallas_call | solution.py:495
  27.5 2.8 %collective-permute-start.6 = (f32[256,128]{1,0:T(8,128)S(1)}, f32[256,128]{1,0:T(8,128)S(1)}, u32[]{:S(2)}, u32[]{:S(2)}) collective-permute-start(f32[256,128]{1,0:T(8,128)S(1)} %get-tuple-element.40.edge_ref), channel_id=1, source_target_pairs={{0,8},{4,12},{8,0},{12,4},{1,9},{5,13},{9,1},{13,5},{2,10},{6,14},... | collective-permute-start | bytes 393224 | tf_op jit(solution)/shard_map/ppermute | solution.py:467
  30.5 1.6 %collective-permute-start.10 = (f32[16,128]{1,0:T(8,128)S(1)}, f32[16,128]{1,0:T(8,128)S(1)}, u32[]{:S(2)}, u32[]{:S(2)}) collective-permute-start(f32[16,128]{1,0:T(8,128)S(1)} %get-tuple-element.46), channel_id=1, source_target_pairs={{2,0},{0,2},{3,1},{1,3},{6,4},{4,6},{7,5},{5,7},{10,8},{8,10},{11,... | collective-permute-start | bytes 24584 | tf_op jit(solution)/shard_map/ppermute | solution.py:468
  32.1 0.8 %injection.1 = f32[1,256,256]{2,1,0:T(8,128)} custom-call(f32[256,128]{1,0:T(8,128)S(1)} %get-tuple-element.40.edge_ref, f32[256,128]{1,0:T(8,128)S(1)} %get-tuple-element.41.rest_ref), custom_call_target="tpu_custom_call" | custom-call | tf_op jit(solution)/shard_map/injection/pallas_call | solution.py:495
  32.9 0.5 %collective-permute-start.9 = (f32[256,128]{1,0:T(8,128)S(1)}, f32[256,128]{1,0:T(8,128)S(1)}, u32[]{:S(2)}, u32[]{:S(2)}) collective-permute-start(f32[256,128]{1,0:T(8,128)S(1)} %get-tuple-element.40.edge_ref), channel_id=1, source_target_pairs={{2,0},{0,2},{3,1},{1,3},{6,4},{4,6},{7,5},{5,7},{10,8},{8,10},{11,... | collective-permute-start | bytes 393224 | tf_op jit(solution)/shard_map/ppermute | solution.py:468
  33.5 0.9 %collective-permute-start.8 = (f32[256,128]{1,0:T(8,128)S(1)}, f32[256,128]{1,0:T(8,128)S(1)}, u32[]{:S(2)}, u32[]{:S(2)}) collective-permute-start(f32[256,128]{1,0:T(8,128)S(1)} %get-tuple-element.40.edge_ref), channel_id=1, source_target_pairs={{0,4},{4,0},{8,12},{12,8},{1,5},{5,1},{9,13},{13,9},{2,6},{6,2},{1... | collective-permute-start | bytes 393224 | tf_op jit(solution)/shard_map/ppermute | solution.py:467
  34.4 0.9 %collective-permute-start.7 = (f32[256,128]{1,0:T(8,128)S(1)}, f32[256,128]{1,0:T(8,128)S(1)}, u32[]{:S(2)}, u32[]{:S(2)}) collective-permute-start(f32[256,128]{1,0:T(8,128)S(1)} %get-tuple-element.40.edge_ref), channel_id=1, source_target_pairs={{0,12},{4,8},{8,4},{12,0},{1,13},{5,9},{9,5},{13,1},{2,14},{6,10},... | collective-permute-start | bytes 393224 | tf_op jit(solution)/shard_map/ppermute | solution.py:467
  35.3 0.5 %own_flows.1.own_ref = f32[6,384,256]{2,1,0:T(8,128)S(1)} custom-call(bf16[6,384,128]{2,1,0:T(8,128)(2,1)S(1)} %own_table.1.refs_13_.table_ref, f32[256,128]{1,0:T(8,128)S(1)} %get-tuple-element.40.edge_ref), custom_call_target="tpu_custom_call" | custom-call | tf_op jit(solution)/shard_map/own_flows/pallas_call | solution.py:495
  35.8 0.6 %line_table.1.table_ref = bf16[6,384,128]{2,1,0:T(8,128)(2,1)S(1)} custom-call(f32[280,128]{1,0:T(8,128)S(1)} %get-tuple-element.26.edge_ref.own_ref.refs_12_, f32[264,128]{1,0:T(8,128)S(1)} %collective-permute-done.2.refs_0_.refs_2_, f32[280,128]{1,0:T(8,128)S(1)} %collective-permute-done.3.refs_0_.refs_3_.refs_1_, ...), custom_call_target="tpu_custom_call" | custom-call | tf_op jit(solution)/shard_map/line_table/pallas_call | solution.py:495
  36.4 3.0 %collective-permute-start.13 = (f32[16,128]{1,0:T(8,128)S(1)}, f32[16,128]{1,0:T(8,128)S(1)}, u32[]{:S(2)}, u32[]{:S(2)}) collective-permute-start(f32[16,128]{1,0:T(8,128)S(1)} %add.3.refs_0_), channel_id=1, source_target_pairs={{0,12},{4,8},{8,4},{12,0},{1,13},{5,9},{9,5},{13,1},{2,14},{6,10},... | collective-permute-start | bytes 24584 | tf_op jit(solution)/shard_map/ppermute | solution.py:467
  39.5 2.8 %collective-permute-start.11 = (f32[16,128]{1,0:T(8,128)S(1)}, f32[16,128]{1,0:T(8,128)S(1)}, u32[]{:S(2)}, u32[]{:S(2)}) collective-permute-start(f32[16,128]{1,0:T(8,128)S(1)} %add.3.refs_0_), channel_id=1, source_target_pairs={{0,4},{4,0},{8,12},{12,8},{1,5},{5,1},{9,13},{13,9},{2,6},{6,2},{1... | collective-permute-start | bytes 24584 | tf_op jit(solution)/shard_map/ppermute | solution.py:467
  42.2 1.8 %tie_flows.1 = (f32[1,6,384,256]{3,2,1,0:T(8,128)}, f32[8,128]{1,0:T(8,128)S(1)}) custom-call(bf16[6,384,128]{2,1,0:T(8,128)(2,1)S(1)} %line_table.1.table_ref, f32[6,384,256]{2,1,0:T(8,128)S(1)} %own_flows.1.own_ref, bf16[256,256]{1,0:T(8,128)(2,1)S(1)} %injection_parts.1.refs_0_, f32[256,128]{1,0:T(8,128)S(1)} %collective-permute-done.7.refs_1_, ...), custom_call_target="tpu_custom_call" | custom-call | flops 4000000000 | tf_op jit(solution)/shard_map/tie_flows/pallas_call | solution.py:495
  44.0 0.6 %zone_prices.1 = f32[4,256]{1,0:T(4,128)} custom-call(f32[16,256]{1,0:T(8,128)S(1)} %get-tuple-element.43.first_ref, f32[8,128]{1,0:T(8,128)S(1)} %get-tuple-element.44.done_ref, f32[16,128]{1,0:T(8,128)S(1)} %add.3.refs_0_, f32[16,128]{1,0:T(8,128)S(1)} %collective-permute-done.11.refs_1_, f32[16,128]{1,0:T(8,128)S(1)} %collective-permute-done.12.refs_2_, ...), custom_call_target="tpu_custom_call" | custom-call | tf_op jit(solution)/shard_map/zone_prices/pallas_call | solution.py:495
  (32 shorter events, 1.2 us)
Async XLA Ops:
  0.6 0.8 %copy-start.3 = (f32[1,256]{1,0:T(1,128)S(1)}, f32[1,256]{1,0:T(1,128)}, u32[]{:S(2)}) copy-start(f32[1,256]{1,0:T(1,128)} %refs_11_.1) | copy-start | bytes 3076
  0.6 0.8 %copy-start.2 = (s32[1,6,384]{2,0,1:T(1,128)S(1)}, s32[1,6,384]{2,0,1:T(1,128)}, u32[]{:S(2)}) copy-start(s32[1,6,384]{2,0,1:T(1,128)} %param.12) | copy-start | bytes 27652
  0.7 0.8 %copy-start.5 = (s32[1,6]{1,0:T(1,128)S(1)}, s32[1,6]{1,0:T(1,128)}, u32[]{:S(2)}) copy-start(s32[1,6]{1,0:T(1,128)} %count_ref.1) | copy-start | bytes 76
  0.7 0.8 %copy-start.4 = (s32[1,6]{1,0:T(1,128)S(1)}, s32[1,6]{1,0:T(1,128)}, u32[]{:S(2)}) copy-start(s32[1,6]{1,0:T(1,128)} %active_ref.1) | copy-start | bytes 76
  0.7 1.0 %copy-start.1 = (f32[1,256,256]{2,1,0:T(8,128)S(1)}, f32[1,256,256]{2,1,0:T(8,128)}, u32[]{:S(2)}) copy-start(f32[1,256,256]{2,1,0:T(8,128)} %load_ref.1) | copy-start | bytes 786436
  0.7 1.1 %copy-start = (f32[1,256,256]{2,1,0:T(8,128)S(1)}, f32[1,256,256]{2,1,0:T(8,128)}, u32[]{:S(2)}) copy-start(f32[1,256,256]{2,1,0:T(8,128)} %k_ref.1) | copy-start | bytes 786436
  6.0 13.2 %collective-permute-start.2 = (f32[264,128]{1,0:T(8,128)S(1)}, f32[264,128]{1,0:T(8,128)S(1)}, u32[]{:S(2)}, u32[]{:S(2)}) collective-permute-start(f32[264,128]{1,0:T(8,128)S(1)} %get-tuple-element.32), channel_id=1, source_target_pairs={{0,8},{4,12},{8,0},{12,4},{1,9},{5,13},{9,1},{13,5},{2,10},{6,14},... | collective-permute-start | bytes 405512 | tf_op jit(solution)/shard_map/ppermute | solution.py:467
  10.4 3.7 %collective-permute-start = (f32[16,128]{1,0:T(8,128)S(1)}, f32[16,128]{1,0:T(8,128)S(1)}, u32[]{:S(2)}, u32[]{:S(2)}) collective-permute-start(f32[16,128]{1,0:T(8,128)S(1)} %get-tuple-element.29), channel_id=1, source_target_pairs={{2,0},{0,2},{3,1},{1,3},{6,4},{4,6},{7,5},{5,7},{10,8},{8,10},{11,... | collective-permute-start | bytes 24584 | tf_op jit(solution)/shard_map/ppermute | solution.py:468
  14.1 8.7 %collective-permute-start.4 = (f32[280,128]{1,0:T(8,128)S(1)}, f32[280,128]{1,0:T(8,128)S(1)}, u32[]{:S(2)}, u32[]{:S(2)}) collective-permute-start(f32[280,128]{1,0:T(8,128)S(1)} %get-tuple-element.33), channel_id=1, source_target_pairs={{0,4},{4,0},{8,12},{12,8},{1,5},{5,1},{9,13},{13,9},{2,6},{6,2},{1... | collective-permute-start | bytes 430088 | tf_op jit(solution)/shard_map/ppermute | solution.py:467
  15.8 7.1 %collective-permute-start.3 = (f32[280,128]{1,0:T(8,128)S(1)}, f32[280,128]{1,0:T(8,128)S(1)}, u32[]{:S(2)}, u32[]{:S(2)}) collective-permute-start(f32[280,128]{1,0:T(8,128)S(1)} %get-tuple-element.33), channel_id=1, source_target_pairs={{0,12},{4,8},{8,4},{12,0},{1,13},{5,9},{9,5},{13,1},{2,14},{6,10},... | collective-permute-start | bytes 430088 | tf_op jit(solution)/shard_map/ppermute | solution.py:467
  15.8 7.8 %collective-permute-start.1 = (f32[16,128]{1,0:T(8,128)S(1)}, f32[16,128]{1,0:T(8,128)S(1)}, u32[]{:S(2)}, u32[]{:S(2)}) collective-permute-start(f32[16,128]{1,0:T(8,128)S(1)} %get-tuple-element.31.refs_0_), channel_id=1, source_target_pairs={{0,8},{4,12},{8,0},{12,4},{1,9},{5,13},{9,1},{13,5},{2,10},{6,14},... | collective-permute-start | bytes 24584 | tf_op jit(solution)/shard_map/ppermute | solution.py:467
  17.7 5.0 %collective-permute-start.5 = (f32[264,128]{1,0:T(8,128)S(1)}, f32[264,128]{1,0:T(8,128)S(1)}, u32[]{:S(2)}, u32[]{:S(2)}) collective-permute-start(f32[264,128]{1,0:T(8,128)S(1)} %get-tuple-element.34), channel_id=1, source_target_pairs={{2,0},{0,2},{3,1},{1,3},{6,4},{4,6},{7,5},{5,7},{10,8},{8,10},{11,... | collective-permute-start | bytes 405512 | tf_op jit(solution)/shard_map/ppermute | solution.py:468
  27.5 11.9 %collective-permute-start.6 = (f32[256,128]{1,0:T(8,128)S(1)}, f32[256,128]{1,0:T(8,128)S(1)}, u32[]{:S(2)}, u32[]{:S(2)}) collective-permute-start(f32[256,128]{1,0:T(8,128)S(1)} %get-tuple-element.40.edge_ref), channel_id=1, source_target_pairs={{0,8},{4,12},{8,0},{12,4},{1,9},{5,13},{9,1},{13,5},{2,10},{6,14},... | collective-permute-start | bytes 393224 | tf_op jit(solution)/shard_map/ppermute | solution.py:467
  30.5 5.9 %collective-permute-start.10 = (f32[16,128]{1,0:T(8,128)S(1)}, f32[16,128]{1,0:T(8,128)S(1)}, u32[]{:S(2)}, u32[]{:S(2)}) collective-permute-start(f32[16,128]{1,0:T(8,128)S(1)} %get-tuple-element.46), channel_id=1, source_target_pairs={{2,0},{0,2},{3,1},{1,3},{6,4},{4,6},{7,5},{5,7},{10,8},{8,10},{11,... | collective-permute-start | bytes 24584 | tf_op jit(solution)/shard_map/ppermute | solution.py:468
  32.9 6.5 %collective-permute-start.9 = (f32[256,128]{1,0:T(8,128)S(1)}, f32[256,128]{1,0:T(8,128)S(1)}, u32[]{:S(2)}, u32[]{:S(2)}) collective-permute-start(f32[256,128]{1,0:T(8,128)S(1)} %get-tuple-element.40.edge_ref), channel_id=1, source_target_pairs={{2,0},{0,2},{3,1},{1,3},{6,4},{4,6},{7,5},{5,7},{10,8},{8,10},{11,... | collective-permute-start | bytes 393224 | tf_op jit(solution)/shard_map/ppermute | solution.py:468
  33.5 8.8 %collective-permute-start.8 = (f32[256,128]{1,0:T(8,128)S(1)}, f32[256,128]{1,0:T(8,128)S(1)}, u32[]{:S(2)}, u32[]{:S(2)}) collective-permute-start(f32[256,128]{1,0:T(8,128)S(1)} %get-tuple-element.40.edge_ref), channel_id=1, source_target_pairs={{0,4},{4,0},{8,12},{12,8},{1,5},{5,1},{9,13},{13,9},{2,6},{6,2},{1... | collective-permute-start | bytes 393224 | tf_op jit(solution)/shard_map/ppermute | solution.py:467
  34.4 7.8 %collective-permute-start.7 = (f32[256,128]{1,0:T(8,128)S(1)}, f32[256,128]{1,0:T(8,128)S(1)}, u32[]{:S(2)}, u32[]{:S(2)}) collective-permute-start(f32[256,128]{1,0:T(8,128)S(1)} %get-tuple-element.40.edge_ref), channel_id=1, source_target_pairs={{0,12},{4,8},{8,4},{12,0},{1,13},{5,9},{9,5},{13,1},{2,14},{6,10},... | collective-permute-start | bytes 393224 | tf_op jit(solution)/shard_map/ppermute | solution.py:467
  36.4 7.6 %collective-permute-start.13 = (f32[16,128]{1,0:T(8,128)S(1)}, f32[16,128]{1,0:T(8,128)S(1)}, u32[]{:S(2)}, u32[]{:S(2)}) collective-permute-start(f32[16,128]{1,0:T(8,128)S(1)} %add.3.refs_0_), channel_id=1, source_target_pairs={{0,12},{4,8},{8,4},{12,0},{1,13},{5,9},{9,5},{13,1},{2,14},{6,10},... | collective-permute-start | bytes 24584 | tf_op jit(solution)/shard_map/ppermute | solution.py:467
  39.4 4.6 %collective-permute-start.12 = (f32[16,128]{1,0:T(8,128)S(1)}, f32[16,128]{1,0:T(8,128)S(1)}, u32[]{:S(2)}, u32[]{:S(2)}) collective-permute-start(f32[16,128]{1,0:T(8,128)S(1)} %add.3.refs_0_), channel_id=1, source_target_pairs={{0,8},{4,12},{8,0},{12,4},{1,9},{5,13},{9,1},{13,5},{2,10},{6,14},... | collective-permute-start | bytes 24584 | tf_op jit(solution)/shard_map/ppermute | solution.py:467
  39.5 4.6 %collective-permute-start.11 = (f32[16,128]{1,0:T(8,128)S(1)}, f32[16,128]{1,0:T(8,128)S(1)}, u32[]{:S(2)}, u32[]{:S(2)}) collective-permute-start(f32[16,128]{1,0:T(8,128)S(1)} %add.3.refs_0_), channel_id=1, source_target_pairs={{0,4},{4,0},{8,12},{12,8},{1,5},{5,1},{9,13},{13,9},{2,6},{6,2},{1... | collective-permute-start | bytes 24584 | tf_op jit(solution)/shard_map/ppermute | solution.py:467

commit v5 on v4

--- a/solution.py
+++ b/solution.py
@@ -152,32 +152,35 @@
     zeros_ref[...] = jnp.zeros(zeros_ref.shape, F32)
 
 
-def first_kernel(
-    areas, regions, near, zeros_ref, k_ref, load_ref, cap_ref, idx_ref, active_ref, count_ref, zone_ref, *refs
-):
-    edge_ref, *lean_refs = refs[:-8]
-    rest_ref, v_ref, lin_ref, kh_ref, kl_ref, own_ref, weight_ref, over_ref = refs[-8:]
-    scens = lin_ref.shape[0]
+def lines_kernel(areas, regions, near, zeros_ref, idx_ref, active_ref, count_ref, zone_ref, block_ref, own_ref, weight_ref):
     slots, _, lines = idx_ref.shape
     pieces = lines // LANES
     numbers = jnp.where(active_ref[...] > 0, count_ref[...], 0).astype(F32)
-    zone = jnp.full((1, LANES), zone_ref[0].astype(F32))
 
     def idx_row(p, j):
         return idx_ref[p, :, pl.ds(j * LANES, LANES)].astype(F32)
 
-    for ref, held in ((edge_ref, range(slots)), *zip(lean_refs, ((2, 3), (4, 5)))):
-        ref[pl.ds(ref.shape[0] - 8, 8), :] = zeros_ref[...]
-        at = scens
-        for p in held:
-            for j in range(pieces):
-                ref[pl.ds(at, 1), :] = idx_row(p, j)
-                at += 1
-        ref[pl.ds(at, 1), :] = zone
-    edge_ref[pl.ds(scens + slots * pieces + 1, 1), pl.ds(0, slots)] = numbers
+    block_ref[pl.ds(block_ref.shape[0] - 8, 8), :] = zeros_ref[...]
+    for p in range(slots):
+        for j in range(pieces):
+            block_ref[pl.ds(p * pieces + j, 1), :] = idx_row(p, j)
+    block_ref[pl.ds(slots * pieces, 1), :] = jnp.full((1, LANES), zone_ref[0].astype(F32))
+    block_ref[pl.ds(slots * pieces + 1, 1), pl.ds(0, slots)] = numbers
     weight_ref[...] = line_tables(
         areas, regions, slots, pieces, near, idx_row, lambda p: numbers[:, p : p + 1], own_ref, weight_ref.shape[0]
     )
+
+
+def first_kernel(slots, pieces, k_ref, load_ref, cap_ref, block_ref, edge_ref, *refs):
+    *lean_refs, rest_ref, v_ref, lin_ref, kh_ref, kl_ref, over_ref = refs
+    scens = lin_ref.shape[0]
+    edge_ref[pl.ds(scens, block_ref.shape[0]), :] = block_ref[...]
+    for ref, p in zip(lean_refs, (2, 4)):
+        ref[pl.ds(scens, 2 * pieces), :] = block_ref[pl.ds(p * pieces, 2 * pieces), :]
+        rest = ref.shape[0] - scens - 2 * pieces
+        ref[pl.ds(scens + 2 * pieces, rest), :] = jnp.broadcast_to(
+            block_ref[pl.ds(slots * pieces, 1), :], (rest, LANES)
+        )
     high, low = halves(k_ref[0].T)
     kh_ref[...] = high
     kl_ref[...] = low
@@ -448,7 +451,7 @@
 def price_kernel(areas, regions, near, first_ref, done_ref, *refs):
     *rest, price_ref = refs
     if near:
-        own, one, two, three = rest
+        own, two, one, three = rest
         sums = first_ref[pl.ds(0, 8), :] + unfolded((own[...] + one[...]) + (two[...] + three[...]))
         zones = [first_ref[pl.ds(8 + k, 1), :] for k in range(4)]
         for z in range(ZONES):
@@ -512,7 +515,7 @@
             [weights, edge, rest],
         )
         pair = share + moved(across, "region", 1)
-        return got, [pair, *(moved(pair, "area", Mask(mask)) for mask in (1, 2, 3))]
+        return got, [pair, *(moved(pair, "area", Mask(mask)) for mask in (2, 1, 3))]
 
     def exchange(edge, rest, leans, weights, kept):
         held = edge.shape[0] > scens
@@ -545,34 +548,33 @@
     zeros = call(opening_kernel, "opening", f32(8, LANES), [], OPENING)
     lean_rows = -(-(scens + 2 * pieces + 1) // 8) * 8
     leans = [f32(lean_rows, BOUNDARY)] * 2 if near else []
+    block, own, weights = call(
+        functools.partial(lines_kernel, areas, regions, near),
+        "line_blocks",
+        [
+            f32(-(-(slots * pieces + 2) // 8) * 8, LANES),
+            bf16(BOUNDARY, slots * lines),
+            f32(weight_rows, buses),
+        ],
+        [zeros, line_index.reshape(slots, 1, lines), pair_active, tie_counts, area_zone],
+        in_specs=[VMEM] * 4 + [SMEM],
+    )
     edge1, *more = call(
-        functools.partial(first_kernel, areas, regions, near),
+        functools.partial(first_kernel, slots, pieces),
         "first_round",
         [
-            f32(-(-(zone_at + 2) // 8) * 8, BOUNDARY),
+            f32(scens + block.shape[0], BOUNDARY),
             *leans,
             f32(scens, rest),
             f32(scens, buses),
             f32(scens, buses),
             bf16(buses, buses),
             bf16(buses, buses),
-            bf16(BOUNDARY, slots * lines),
-            f32(weight_rows, buses),
         ],
-        [
-            zeros,
-            kkt_inverse,
-            scen_load,
-            capacity,
-            line_index.reshape(slots, 1, lines),
-            pair_active,
-            tie_counts,
-            area_zone,
-        ],
-        in_specs=[VMEM] * 7 + [SMEM],
+        [kkt_inverse, scen_load, capacity, block],
         scratch_shapes=[pltpu.VMEM((scens, buses), F32)],
     )
-    leans1, (rest1, state, lin, kh, kl, own, weights) = more[: len(leans)], more[len(leans) :]
+    leans1, (rest1, state, lin, kh, kl) = more[: len(leans)], more[len(leans) :]
     got1, sums1 = exchange(edge1, rest1, leans1, weights, 2 * pieces)
     coupling = []
     for held in plan.arrivals:

time: 44.8 us -> 44.5 us (level)
    pallas_call x15 -> x16, Pallas kernels: 14.7 us -> 14.6 us  [call(): pl.pallas_call(kernel, out_shape=out_shape, in_specs=more.pop('in_specs',...]
where the time goes in v5:
time: 44.5 us; the launch traced here: 44.4 us
  starting transfers between devices  23.1 us (52%)
  Pallas kernels  14.6 us (33%)
  waiting for transfers between devices  5 us (11%)
  between operations  1.53 us (3%)
    ppermute x10, starting transfers between devices, moved(): return lax.ppermute(x, axis, [(i, i ^ by) for i in range(length)])  18 us
    pallas_call x16, Pallas kernels, call(): pl.pallas_call(kernel, out_shape=out_shape, in_specs=more.pop('in_specs',...  14.6 us
    ppermute x4, starting transfers between devices, moved(): lax.ppermute(x, axis, [((i + by) % length, i) for i in range(length)])  5.14 us
    ppermute x4, waiting for transfers between devices, moved(): lax.ppermute(x, axis, [((i + by) % length, i) for i in range(length)])  4.61 us
  transfers between devices with their start and end apart: 14, of which 4 were waited for; matrix products, arithmetic and copies ran while one was open for 0% of the time, Pallas kernels for 13%

profile of v5, /device:TPU:0, one launch (start us, length us, event | category | flops | bytes accessed | tf_op | source)
XLA Modules:
  0.0 44.4 jit_solution(11027916982621514493)
XLA Ops:
  1.4 0.5 %line_blocks.1 = (f32[24,128]{1,0:T(8,128)S(1)}, bf16[128,2304]{1,0:T(8,128)(2,1)S(1)}, f32[16,256]{1,0:T(8,128)S(1)}) custom-call(f32[8,128]{1,0:T(8,128)S(1)} %opening.1.zeros_ref, s32[6,1,384]{2,1,0:T(1,128)S(1)} %bitcast.1, s32[1,6]{1,0:T(1,128)S(1)} %copy-done.4, s32[1,6]{1,0:T(1,128)S(1)} %copy-done.5, s32[1]{0:T(128)S(6)} %copy.10.zone_ref), custom_call_target="tpu_custom_call" | custom-call | tf_op jit(solution)/shard_map/line_blocks/pallas_call | solution.py:498
  2.0 3.7 %first_round.1 = (f32[280,128]{1,0:T(8,128)S(1)}, f32[264,128]{1,0:T(8,128)S(1)}, f32[264,128]{1,0:T(8,128)S(1)}, f32[256,128]{1,0:T(8,128)S(1)}, f32[256,256]{1...) custom-call(f32[1,256,256]{2,1,0:T(8,128)S(1)} %copy-done, ...), custom_call_target="tpu_custom_call" | custom-call | tf_op jit(solution)/shard_map/first_round/pallas_call | solution.py:498
  5.7 4.1 %collective-permute-start.2 = (f32[264,128]{1,0:T(8,128)S(1)}, f32[264,128]{1,0:T(8,128)S(1)}, u32[]{:S(2)}, u32[]{:S(2)}) collective-permute-start(f32[264,128]{1,0:T(8,128)S(1)} %get-tuple-element.34), channel_id=1, source_target_pairs={{0,8},{4,12},{8,0},{12,4},{1,9},{5,13},{9,1},{13,5},{2,10},{6,14},... | collective-permute-start | bytes 405512 | tf_op jit(solution)/shard_map/ppermute | solution.py:470
  10.0 1.6 %collective-permute-start = (f32[16,128]{1,0:T(8,128)S(1)}, f32[16,128]{1,0:T(8,128)S(1)}, u32[]{:S(2)}, u32[]{:S(2)}) collective-permute-start(f32[16,128]{1,0:T(8,128)S(1)} %get-tuple-element.31), channel_id=1, source_target_pairs={{2,0},{0,2},{3,1},{1,3},{6,4},{4,6},{7,5},{5,7},{10,8},{8,10},{11,... | collective-permute-start | bytes 24584 | tf_op jit(solution)/shard_map/ppermute | solution.py:471
  11.6 0.6 %own_table.1.refs_13_.table_ref = bf16[6,384,128]{2,1,0:T(8,128)(2,1)S(1)} custom-call(f32[280,128]{1,0:T(8,128)S(1)} %get-tuple-element.28.edge_ref.own_ref.refs_12_), custom_call_target="tpu_custom_call" | custom-call | tf_op jit(solution)/shard_map/own_table/pallas_call | solution.py:498
  12.2 1.6 %collective-permute-done.across_ref = f32[16,128]{1,0:T(8,128)S(1)} collective-permute-done((f32[16,128]{1,0:T(8,128)S(1)}, f32[16,128]{1,0:T(8,128)S(1)}, u32[]{:S(2)}, u32[]{:S(2)}) %collective-permute-start) | collective-permute-done | bytes 8224 | tf_op jit(solution)/shard_map/ppermute | solution.py:471
  13.8 1.6 %collective-permute-start.4 = (f32[280,128]{1,0:T(8,128)S(1)}, f32[280,128]{1,0:T(8,128)S(1)}, u32[]{:S(2)}, u32[]{:S(2)}) collective-permute-start(f32[280,128]{1,0:T(8,128)S(1)} %get-tuple-element.35), channel_id=1, source_target_pairs={{0,4},{4,0},{8,12},{12,8},{1,5},{5,1},{9,13},{13,9},{2,6},{6,2},{1... | collective-permute-start | bytes 430088 | tf_op jit(solution)/shard_map/ppermute | solution.py:470
  15.4 1.9 %collective-permute-start.1 = (f32[16,128]{1,0:T(8,128)S(1)}, f32[16,128]{1,0:T(8,128)S(1)}, u32[]{:S(2)}, u32[]{:S(2)}) collective-permute-start(f32[16,128]{1,0:T(8,128)S(1)} %get-tuple-element.33.refs_0_), channel_id=1, source_target_pairs={{0,8},{4,12},{8,0},{12,4},{1,9},{5,13},{9,1},{13,5},{2,10},{6,14},... | collective-permute-start | bytes 24584 | tf_op jit(solution)/shard_map/ppermute | solution.py:470
  17.3 1.5 %collective-permute-start.5 = (f32[264,128]{1,0:T(8,128)S(1)}, f32[264,128]{1,0:T(8,128)S(1)}, u32[]{:S(2)}, u32[]{:S(2)}) collective-permute-start(f32[264,128]{1,0:T(8,128)S(1)} %get-tuple-element.36), channel_id=1, source_target_pairs={{2,0},{0,2},{3,1},{1,3},{6,4},{4,6},{7,5},{5,7},{10,8},{8,10},{11,... | collective-permute-start | bytes 405512 | tf_op jit(solution)/shard_map/ppermute | solution.py:471
  18.8 0.5 %coupling.2.refs_3_ = f32[256,128]{1,0:T(8,128)S(1)} custom-call(bf16[128,2304]{1,0:T(8,128)(2,1)S(1)} %get-tuple-element.38.own_ref, f32[264,128]{1,0:T(8,128)S(1)} %collective-permute-done.2.refs_0_.refs_2_), custom_call_target="tpu_custom_call" | custom-call | flops 4000000000 | tf_op jit(solution)/shard_map/coupling/pallas_call | solution.py:498
  19.3 3.0 %collective-permute-done.5.refs_2_.refs_5_.refs_3_ = f32[264,128]{1,0:T(8,128)S(1)} collective-permute-done((f32[264,128]{1,0:T(8,128)S(1)}, f32[264,128]{1,0:T(8,128)S(1)}, u32[]{:S(2)}, u32[]{:S(2)}) %collective-permute-start.5) | collective-permute-done | bytes 135200 | tf_op jit(solution)/shard_map/ppermute | solution.py:471
  22.5 0.6 %coupling.3.refs_7_ = f32[256,128]{1,0:T(8,128)S(1)} custom-call(bf16[128,2304]{1,0:T(8,128)(2,1)S(1)} %get-tuple-element.38.own_ref, f32[280,128]{1,0:T(8,128)S(1)} %collective-permute-done.3.refs_0_.refs_3_.refs_1_, f32[280,128]{1,0:T(8,128)S(1)} %collective-permute-done.4.refs_1_.refs_4_.refs_2_, ...), custom_call_target="tpu_custom_call" | custom-call | flops 4000000000 | tf_op jit(solution)/shard_map/coupling/pallas_call | solution.py:498
  23.3 3.9 %second_round.1 = (f32[256,128]{1,0:T(8,128)S(1)}, f32[256,128]{1,0:T(8,128)S(1)}, f32[16,256]{1,0:T(8,128)S(1)}) custom-call(f32[16,128]{1,0:T(8,128)S(1)} %get-tuple-element.33.refs_0_, f32[16,128]{1,0:T(8,128)S(1)} %collective-permute-done.1.refs_1_, f32[264,128]{1,0:T(8,128)S(1)} %collective-permute-done.2.refs_0_.refs_2_, ...), custom_call_target="tpu_custom_call" | custom-call | tf_op jit(solution)/shard_map/second_round/pallas_call | solution.py:498
  27.2 2.8 %collective-permute-start.6 = (f32[256,128]{1,0:T(8,128)S(1)}, f32[256,128]{1,0:T(8,128)S(1)}, u32[]{:S(2)}, u32[]{:S(2)}) collective-permute-start(f32[256,128]{1,0:T(8,128)S(1)} %get-tuple-element.42.edge_ref), channel_id=1, source_target_pairs={{0,8},{4,12},{8,0},{12,4},{1,9},{5,13},{9,1},{13,5},{2,10},{6,14},... | collective-permute-start | bytes 393224 | tf_op jit(solution)/shard_map/ppermute | solution.py:470
  30.2 1.6 %collective-permute-start.10 = (f32[16,128]{1,0:T(8,128)S(1)}, f32[16,128]{1,0:T(8,128)S(1)}, u32[]{:S(2)}, u32[]{:S(2)}) collective-permute-start(f32[16,128]{1,0:T(8,128)S(1)} %get-tuple-element.48), channel_id=1, source_target_pairs={{2,0},{0,2},{3,1},{1,3},{6,4},{4,6},{7,5},{5,7},{10,8},{8,10},{11,... | collective-permute-start | bytes 24584 | tf_op jit(solution)/shard_map/ppermute | solution.py:471
  31.8 0.8 %injection.1 = f32[1,256,256]{2,1,0:T(8,128)} custom-call(f32[256,128]{1,0:T(8,128)S(1)} %get-tuple-element.42.edge_ref, f32[256,128]{1,0:T(8,128)S(1)} %get-tuple-element.43.rest_ref), custom_call_target="tpu_custom_call" | custom-call | tf_op jit(solution)/shard_map/injection/pallas_call | solution.py:498
  32.6 0.5 %collective-permute-start.9 = (f32[256,128]{1,0:T(8,128)S(1)}, f32[256,128]{1,0:T(8,128)S(1)}, u32[]{:S(2)}, u32[]{:S(2)}) collective-permute-start(f32[256,128]{1,0:T(8,128)S(1)} %get-tuple-element.42.edge_ref), channel_id=1, source_target_pairs={{2,0},{0,2},{3,1},{1,3},{6,4},{4,6},{7,5},{5,7},{10,8},{8,10},{11,... | collective-permute-start | bytes 393224 | tf_op jit(solution)/shard_map/ppermute | solution.py:471
  33.1 0.9 %collective-permute-start.8 = (f32[256,128]{1,0:T(8,128)S(1)}, f32[256,128]{1,0:T(8,128)S(1)}, u32[]{:S(2)}, u32[]{:S(2)}) collective-permute-start(f32[256,128]{1,0:T(8,128)S(1)} %get-tuple-element.42.edge_ref), channel_id=1, source_target_pairs={{0,4},{4,0},{8,12},{12,8},{1,5},{5,1},{9,13},{13,9},{2,6},{6,2},{1... | collective-permute-start | bytes 393224 | tf_op jit(solution)/shard_map/ppermute | solution.py:470
  34.1 0.9 %collective-permute-start.7 = (f32[256,128]{1,0:T(8,128)S(1)}, f32[256,128]{1,0:T(8,128)S(1)}, u32[]{:S(2)}, u32[]{:S(2)}) collective-permute-start(f32[256,128]{1,0:T(8,128)S(1)} %get-tuple-element.42.edge_ref), channel_id=1, source_target_pairs={{0,12},{4,8},{8,4},{12,0},{1,13},{5,9},{9,5},{13,1},{2,14},{6,10},... | collective-permute-start | bytes 393224 | tf_op jit(solution)/shard_map/ppermute | solution.py:470
  35.5 0.6 %line_table.1.table_ref = bf16[6,384,128]{2,1,0:T(8,128)(2,1)S(1)} custom-call(f32[280,128]{1,0:T(8,128)S(1)} %get-tuple-element.28.edge_ref.own_ref.refs_12_, f32[264,128]{1,0:T(8,128)S(1)} %collective-permute-done.2.refs_0_.refs_2_, f32[280,128]{1,0:T(8,128)S(1)} %collective-permute-done.3.refs_0_.refs_3_.refs_1_, ...), custom_call_target="tpu_custom_call" | custom-call | tf_op jit(solution)/shard_map/line_table/pallas_call | solution.py:498
  36.1 3.0 %collective-permute-start.13 = (f32[16,128]{1,0:T(8,128)S(1)}, f32[16,128]{1,0:T(8,128)S(1)}, u32[]{:S(2)}, u32[]{:S(2)}) collective-permute-start(f32[16,128]{1,0:T(8,128)S(1)} %add.3.refs_0_), channel_id=1, source_target_pairs={{0,12},{4,8},{8,4},{12,0},{1,13},{5,9},{9,5},{13,1},{2,14},{6,10},... | collective-permute-start | bytes 24584 | tf_op jit(solution)/shard_map/ppermute | solution.py:470
  39.1 2.8 %collective-permute-start.11 = (f32[16,128]{1,0:T(8,128)S(1)}, f32[16,128]{1,0:T(8,128)S(1)}, u32[]{:S(2)}, u32[]{:S(2)}) collective-permute-start(f32[16,128]{1,0:T(8,128)S(1)} %add.3.refs_0_), channel_id=1, source_target_pairs={{0,8},{4,12},{8,0},{12,4},{1,9},{5,13},{9,1},{13,5},{2,10},{6,14},... | collective-permute-start | bytes 24584 | tf_op jit(solution)/shard_map/ppermute | solution.py:470
  41.9 1.8 %tie_flows.1 = (f32[1,6,384,256]{3,2,1,0:T(8,128)}, f32[8,128]{1,0:T(8,128)S(1)}) custom-call(bf16[6,384,128]{2,1,0:T(8,128)(2,1)S(1)} %line_table.1.table_ref, f32[6,384,256]{2,1,0:T(8,128)S(1)} %own_flows.1.own_ref, bf16[256,256]{1,0:T(8,128)(2,1)S(1)} %injection_parts.1.refs_0_, f32[256,128]{1,0:T(8,128)S(1)} %collective-permute-done.7.refs_1_, ...), custom_call_target="tpu_custom_call" | custom-call | flops 4000000000 | tf_op jit(solution)/shard_map/tie_flows/pallas_call | solution.py:498
  43.7 0.6 %zone_prices.1 = f32[4,256]{1,0:T(4,128)} custom-call(f32[16,256]{1,0:T(8,128)S(1)} %get-tuple-element.45.first_ref, f32[8,128]{1,0:T(8,128)S(1)} %get-tuple-element.46.done_ref, f32[16,128]{1,0:T(8,128)S(1)} %add.3.refs_0_, f32[16,128]{1,0:T(8,128)S(1)} %collective-permute-done.11.refs_1_, f32[16,128]{1,0:T(8,128)S(1)} %collective-permute-done.12.refs_2_, ...), custom_call_target="tpu_custom_call" | custom-call | tf_op jit(solution)/shard_map/zone_prices/pallas_call | solution.py:498
  (33 shorter events, 1.5 us)
Async XLA Ops:
  0.6 0.8 %copy-start.2 = (s32[1,6,384]{2,0,1:T(1,128)S(1)}, s32[1,6,384]{2,0,1:T(1,128)}, u32[]{:S(2)}) copy-start(s32[1,6,384]{2,0,1:T(1,128)} %param.12) | copy-start | bytes 27652
  0.6 0.8 %copy-start.5 = (s32[1,6]{1,0:T(1,128)S(1)}, s32[1,6]{1,0:T(1,128)}, u32[]{:S(2)}) copy-start(s32[1,6]{1,0:T(1,128)} %count_ref.1) | copy-start | bytes 76
  0.7 0.8 %copy-start.4 = (s32[1,6]{1,0:T(1,128)S(1)}, s32[1,6]{1,0:T(1,128)}, u32[]{:S(2)}) copy-start(s32[1,6]{1,0:T(1,128)} %active_ref.1) | copy-start | bytes 76
  0.7 1.3 %copy-start.3 = (f32[1,256]{1,0:T(1,128)S(1)}, f32[1,256]{1,0:T(1,128)}, u32[]{:S(2)}) copy-start(f32[1,256]{1,0:T(1,128)} %refs_11_.1) | copy-start | bytes 3076
  0.7 1.3 %copy-start.1 = (f32[1,256,256]{2,1,0:T(8,128)S(1)}, f32[1,256,256]{2,1,0:T(8,128)}, u32[]{:S(2)}) copy-start(f32[1,256,256]{2,1,0:T(8,128)} %load_ref.1) | copy-start | bytes 786436
  0.7 1.3 %copy-start = (f32[1,256,256]{2,1,0:T(8,128)S(1)}, f32[1,256,256]{2,1,0:T(8,128)}, u32[]{:S(2)}) copy-start(f32[1,256,256]{2,1,0:T(8,128)} %k_ref.1) | copy-start | bytes 786436
  5.7 13.1 %collective-permute-start.2 = (f32[264,128]{1,0:T(8,128)S(1)}, f32[264,128]{1,0:T(8,128)S(1)}, u32[]{:S(2)}, u32[]{:S(2)}) collective-permute-start(f32[264,128]{1,0:T(8,128)S(1)} %get-tuple-element.34), channel_id=1, source_target_pairs={{0,8},{4,12},{8,0},{12,4},{1,9},{5,13},{9,1},{13,5},{2,10},{6,14},... | collective-permute-start | bytes 405512 | tf_op jit(solution)/shard_map/ppermute | solution.py:470
  10.0 3.7 %collective-permute-start = (f32[16,128]{1,0:T(8,128)S(1)}, f32[16,128]{1,0:T(8,128)S(1)}, u32[]{:S(2)}, u32[]{:S(2)}) collective-permute-start(f32[16,128]{1,0:T(8,128)S(1)} %get-tuple-element.31), channel_id=1, source_target_pairs={{2,0},{0,2},{3,1},{1,3},{6,4},{4,6},{7,5},{5,7},{10,8},{8,10},{11,... | collective-permute-start | bytes 24584 | tf_op jit(solution)/shard_map/ppermute | solution.py:471
  13.8 8.7 %collective-permute-start.4 = (f32[280,128]{1,0:T(8,128)S(1)}, f32[280,128]{1,0:T(8,128)S(1)}, u32[]{:S(2)}, u32[]{:S(2)}) collective-permute-start(f32[280,128]{1,0:T(8,128)S(1)} %get-tuple-element.35), channel_id=1, source_target_pairs={{0,4},{4,0},{8,12},{12,8},{1,5},{5,1},{9,13},{13,9},{2,6},{6,2},{1... | collective-permute-start | bytes 430088 | tf_op jit(solution)/shard_map/ppermute | solution.py:470
  15.4 7.1 %collective-permute-start.3 = (f32[280,128]{1,0:T(8,128)S(1)}, f32[280,128]{1,0:T(8,128)S(1)}, u32[]{:S(2)}, u32[]{:S(2)}) collective-permute-start(f32[280,128]{1,0:T(8,128)S(1)} %get-tuple-element.35), channel_id=1, source_target_pairs={{0,12},{4,8},{8,4},{12,0},{1,13},{5,9},{9,5},{13,1},{2,14},{6,10},... | collective-permute-start | bytes 430088 | tf_op jit(solution)/shard_map/ppermute | solution.py:470
  15.4 7.8 %collective-permute-start.1 = (f32[16,128]{1,0:T(8,128)S(1)}, f32[16,128]{1,0:T(8,128)S(1)}, u32[]{:S(2)}, u32[]{:S(2)}) collective-permute-start(f32[16,128]{1,0:T(8,128)S(1)} %get-tuple-element.33.refs_0_), channel_id=1, source_target_pairs={{0,8},{4,12},{8,0},{12,4},{1,9},{5,13},{9,1},{13,5},{2,10},{6,14},... | collective-permute-start | bytes 24584 | tf_op jit(solution)/shard_map/ppermute | solution.py:470
  17.3 5.0 %collective-permute-start.5 = (f32[264,128]{1,0:T(8,128)S(1)}, f32[264,128]{1,0:T(8,128)S(1)}, u32[]{:S(2)}, u32[]{:S(2)}) collective-permute-start(f32[264,128]{1,0:T(8,128)S(1)} %get-tuple-element.36), channel_id=1, source_target_pairs={{2,0},{0,2},{3,1},{1,3},{6,4},{4,6},{7,5},{5,7},{10,8},{8,10},{11,... | collective-permute-start | bytes 405512 | tf_op jit(solution)/shard_map/ppermute | solution.py:471
  27.2 11.9 %collective-permute-start.6 = (f32[256,128]{1,0:T(8,128)S(1)}, f32[256,128]{1,0:T(8,128)S(1)}, u32[]{:S(2)}, u32[]{:S(2)}) collective-permute-start(f32[256,128]{1,0:T(8,128)S(1)} %get-tuple-element.42.edge_ref), channel_id=1, source_target_pairs={{0,8},{4,12},{8,0},{12,4},{1,9},{5,13},{9,1},{13,5},{2,10},{6,14},... | collective-permute-start | bytes 393224 | tf_op jit(solution)/shard_map/ppermute | solution.py:470
  30.2 5.9 %collective-permute-start.10 = (f32[16,128]{1,0:T(8,128)S(1)}, f32[16,128]{1,0:T(8,128)S(1)}, u32[]{:S(2)}, u32[]{:S(2)}) collective-permute-start(f32[16,128]{1,0:T(8,128)S(1)} %get-tuple-element.48), channel_id=1, source_target_pairs={{2,0},{0,2},{3,1},{1,3},{6,4},{4,6},{7,5},{5,7},{10,8},{8,10},{11,... | collective-permute-start | bytes 24584 | tf_op jit(solution)/shard_map/ppermute | solution.py:471
  32.6 6.5 %collective-permute-start.9 = (f32[256,128]{1,0:T(8,128)S(1)}, f32[256,128]{1,0:T(8,128)S(1)}, u32[]{:S(2)}, u32[]{:S(2)}) collective-permute-start(f32[256,128]{1,0:T(8,128)S(1)} %get-tuple-element.42.edge_ref), channel_id=1, source_target_pairs={{2,0},{0,2},{3,1},{1,3},{6,4},{4,6},{7,5},{5,7},{10,8},{8,10},{11,... | collective-permute-start | bytes 393224 | tf_op jit(solution)/shard_map/ppermute | solution.py:471
  33.1 8.8 %collective-permute-start.8 = (f32[256,128]{1,0:T(8,128)S(1)}, f32[256,128]{1,0:T(8,128)S(1)}, u32[]{:S(2)}, u32[]{:S(2)}) collective-permute-start(f32[256,128]{1,0:T(8,128)S(1)} %get-tuple-element.42.edge_ref), channel_id=1, source_target_pairs={{0,4},{4,0},{8,12},{12,8},{1,5},{5,1},{9,13},{13,9},{2,6},{6,2},{1... | collective-permute-start | bytes 393224 | tf_op jit(solution)/shard_map/ppermute | solution.py:470
  34.1 7.8 %collective-permute-start.7 = (f32[256,128]{1,0:T(8,128)S(1)}, f32[256,128]{1,0:T(8,128)S(1)}, u32[]{:S(2)}, u32[]{:S(2)}) collective-permute-start(f32[256,128]{1,0:T(8,128)S(1)} %get-tuple-element.42.edge_ref), channel_id=1, source_target_pairs={{0,12},{4,8},{8,4},{12,0},{1,13},{5,9},{9,5},{13,1},{2,14},{6,10},... | collective-permute-start | bytes 393224 | tf_op jit(solution)/shard_map/ppermute | solution.py:470
  36.1 7.6 %collective-permute-start.13 = (f32[16,128]{1,0:T(8,128)S(1)}, f32[16,128]{1,0:T(8,128)S(1)}, u32[]{:S(2)}, u32[]{:S(2)}) collective-permute-start(f32[16,128]{1,0:T(8,128)S(1)} %add.3.refs_0_), channel_id=1, source_target_pairs={{0,12},{4,8},{8,4},{12,0},{1,13},{5,9},{9,5},{13,1},{2,14},{6,10},... | collective-permute-start | bytes 24584 | tf_op jit(solution)/shard_map/ppermute | solution.py:470
  39.1 4.6 %collective-permute-start.12 = (f32[16,128]{1,0:T(8,128)S(1)}, f32[16,128]{1,0:T(8,128)S(1)}, u32[]{:S(2)}, u32[]{:S(2)}) collective-permute-start(f32[16,128]{1,0:T(8,128)S(1)} %add.3.refs_0_), channel_id=1, source_target_pairs={{0,4},{4,0},{8,12},{12,8},{1,5},{5,1},{9,13},{13,9},{2,6},{6,2},{1... | collective-permute-start | bytes 24584 | tf_op jit(solution)/shard_map/ppermute | solution.py:470
  39.1 4.6 %collective-permute-start.11 = (f32[16,128]{1,0:T(8,128)S(1)}, f32[16,128]{1,0:T(8,128)S(1)}, u32[]{:S(2)}, u32[]{:S(2)}) collective-permute-start(f32[16,128]{1,0:T(8,128)S(1)} %add.3.refs_0_), channel_id=1, source_target_pairs={{0,8},{4,12},{8,0},{12,4},{1,9},{5,13},{9,1},{13,5},{2,10},{6,14},... | collective-permute-start | bytes 24584 | tf_op jit(solution)/shard_map/ppermute | solution.py:470

commit v6 on v5

--- a/solution.py
+++ b/solution.py
@@ -276,7 +276,7 @@
             self.sources = [("area", Mask(2)), ("area", Mask(3)), ("area", Mask(1)), ("region", 1)]
             self.slots_of = [(2, 3), ((1, 0),), ((0, 1),), (4, 5)]
             self.buffer_of = [(2, 1), (1, 2), 0, 0, 3, 3]
-            self.arrivals = [(0,), (1, 2, 3)]
+            self.arrivals = [(0,), (3,), (1, 2)]
             self.last = (1, 2, 3)
             return
         self.sources, self.slots_of, self.buffer_of = [], [], [None] * slots
@@ -354,14 +354,16 @@
         sums = refs[0][...]
         sums_ref[...] = sums
         price = prices(sums, sums[total + 1 : 2 * total + 1, :], total, regions, zone)
-    price = jnp.broadcast_to(price, (8, scens)).T[:, 0:1]
-    lin2_ref[:, pl.ds(0, BOUNDARY)] = lin_ref[:, pl.ds(0, BOUNDARY)] - price - coupling_ref[...]
-    lin2_ref[:, pl.ds(BOUNDARY, BOUNDARY)] = lin_ref[:, pl.ds(BOUNDARY, BOUNDARY)] - price
+    price_ref = over_ref
+    price_ref[...] = jnp.broadcast_to(jnp.broadcast_to(price, (8, scens)).T[:, 0:1], price_ref.shape)
     limits = cap_ref[...]
 
     def start(rows):
+        lin = lin_ref[rows, :] - price_ref[rows, :]
+        lin = jnp.concatenate([lin[:, :BOUNDARY] - coupling_ref[rows, :], lin[:, BOUNDARY:]], axis=1)
+        lin2_ref[rows, :] = lin
         clipped, over = clipping(v_ref[rows, :], limits)
-        return lin2_ref[rows, :] + (clipped - over), over
+        return lin + (clipped - over), over
 
     def finish(rows, x, over):
         edge_ref[rows, :] = x[:, :BOUNDARY]

time: 44.5 us -> 44.5 us (level)
  Pallas kernels: 14.6 us -> 15.1 us
    pallas_call x16 -> x17, Pallas kernels: 14.6 us -> 15.1 us  [call(): pl.pallas_call(kernel, out_shape=out_shape, in_specs=more.pop('in_specs',...]
  transfers between devices with their start and end apart: 14 -> 14, of which waited for: 4 -> 3; matrix products, arithmetic and copies ran while one was open for 0% -> 0% of each run, Pallas kernels for 13% -> 14%
where the time goes in v6:
time: 44.5 us; the launch traced here: 44.4 us
  starting transfers between devices  22.9 us (51%)
  Pallas kernels  15.1 us (34%)
  waiting for transfers between devices  4.76 us (11%)
  between operations  1.56 us (4%)
    ppermute x10, starting transfers between devices, moved(): return lax.ppermute(x, axis, [(i, i ^ by) for i in range(length)])  17.7 us
    pallas_call x17, Pallas kernels, call(): pl.pallas_call(kernel, out_shape=out_shape, in_specs=more.pop('in_specs',...  15.1 us
    ppermute x4, starting transfers between devices, moved(): lax.ppermute(x, axis, [((i + by) % length, i) for i in range(length)])  5.14 us
    ppermute x4, waiting for transfers between devices, moved(): lax.ppermute(x, axis, [((i + by) % length, i) for i in range(length)])  4.61 us
  transfers between devices with their start and end apart: 14, of which 3 were waited for; matrix products, arithmetic and copies ran while one was open for 0% of the time, Pallas kernels for 14%

profile of v6, /device:TPU:0, one launch (start us, length us, event | category | flops | bytes accessed | tf_op | source)
XLA Modules:
  0.0 44.4 jit_solution(8676616262869759769)
XLA Ops:
  1.4 0.5 %line_blocks.1 = (f32[24,128]{1,0:T(8,128)S(1)}, bf16[128,2304]{1,0:T(8,128)(2,1)S(1)}, f32[16,256]{1,0:T(8,128)S(1)}) custom-call(f32[8,128]{1,0:T(8,128)S(1)} %opening.1.zeros_ref, s32[6,1,384]{2,1,0:T(1,128)S(1)} %bitcast.1, s32[1,6]{1,0:T(1,128)S(1)} %copy-done.4, s32[1,6]{1,0:T(1,128)S(1)} %copy-done.5, s32[1]{0:T(128)S(6)} %copy.10.zone_ref), custom_call_target="tpu_custom_call" | custom-call | tf_op jit(solution)/shard_map/line_blocks/pallas_call | solution.py:500
  2.0 3.7 %first_round.1 = (f32[280,128]{1,0:T(8,128)S(1)}, f32[264,128]{1,0:T(8,128)S(1)}, f32[264,128]{1,0:T(8,128)S(1)}, f32[256,128]{1,0:T(8,128)S(1)}, f32[256,256]{1...) custom-call(f32[1,256,256]{2,1,0:T(8,128)S(1)} %copy-done, ...), custom_call_target="tpu_custom_call" | custom-call | tf_op jit(solution)/shard_map/first_round/pallas_call | solution.py:500
  5.7 4.1 %collective-permute-start.2 = (f32[264,128]{1,0:T(8,128)S(1)}, f32[264,128]{1,0:T(8,128)S(1)}, u32[]{:S(2)}, u32[]{:S(2)}) collective-permute-start(f32[264,128]{1,0:T(8,128)S(1)} %get-tuple-element.34), channel_id=1, source_target_pairs={{0,8},{4,12},{8,0},{12,4},{1,9},{5,13},{9,1},{13,5},{2,10},{6,14},... | collective-permute-start | bytes 405512 | tf_op jit(solution)/shard_map/ppermute | solution.py:472
  10.0 1.6 %collective-permute-start = (f32[16,128]{1,0:T(8,128)S(1)}, f32[16,128]{1,0:T(8,128)S(1)}, u32[]{:S(2)}, u32[]{:S(2)}) collective-permute-start(f32[16,128]{1,0:T(8,128)S(1)} %get-tuple-element.31), channel_id=1, source_target_pairs={{2,0},{0,2},{3,1},{1,3},{6,4},{4,6},{7,5},{5,7},{10,8},{8,10},{11,... | collective-permute-start | bytes 24584 | tf_op jit(solution)/shard_map/ppermute | solution.py:473
  11.6 0.6 %own_table.1.refs_13_.table_ref = bf16[6,384,128]{2,1,0:T(8,128)(2,1)S(1)} custom-call(f32[280,128]{1,0:T(8,128)S(1)} %get-tuple-element.28.edge_ref.own_ref.refs_12_), custom_call_target="tpu_custom_call" | custom-call | tf_op jit(solution)/shard_map/own_table/pallas_call | solution.py:500
  12.2 1.6 %collective-permute-done.across_ref = f32[16,128]{1,0:T(8,128)S(1)} collective-permute-done((f32[16,128]{1,0:T(8,128)S(1)}, f32[16,128]{1,0:T(8,128)S(1)}, u32[]{:S(2)}, u32[]{:S(2)}) %collective-permute-start) | collective-permute-done | bytes 8224 | tf_op jit(solution)/shard_map/ppermute | solution.py:473
  13.8 1.6 %collective-permute-start.4 = (f32[280,128]{1,0:T(8,128)S(1)}, f32[280,128]{1,0:T(8,128)S(1)}, u32[]{:S(2)}, u32[]{:S(2)}) collective-permute-start(f32[280,128]{1,0:T(8,128)S(1)} %get-tuple-element.35), channel_id=1, source_target_pairs={{0,4},{4,0},{8,12},{12,8},{1,5},{5,1},{9,13},{13,9},{2,6},{6,2},{1... | collective-permute-start | bytes 430088 | tf_op jit(solution)/shard_map/ppermute | solution.py:472
  15.4 1.9 %collective-permute-start.1 = (f32[16,128]{1,0:T(8,128)S(1)}, f32[16,128]{1,0:T(8,128)S(1)}, u32[]{:S(2)}, u32[]{:S(2)}) collective-permute-start(f32[16,128]{1,0:T(8,128)S(1)} %get-tuple-element.33.refs_0_), channel_id=1, source_target_pairs={{0,8},{4,12},{8,0},{12,4},{1,9},{5,13},{9,1},{13,5},{2,10},{6,14},... | collective-permute-start | bytes 24584 | tf_op jit(solution)/shard_map/ppermute | solution.py:472
  17.3 1.5 %collective-permute-start.5 = (f32[264,128]{1,0:T(8,128)S(1)}, f32[264,128]{1,0:T(8,128)S(1)}, u32[]{:S(2)}, u32[]{:S(2)}) collective-permute-start(f32[264,128]{1,0:T(8,128)S(1)} %get-tuple-element.36), channel_id=1, source_target_pairs={{2,0},{0,2},{3,1},{1,3},{6,4},{4,6},{7,5},{5,7},{10,8},{8,10},{11,... | collective-permute-start | bytes 405512 | tf_op jit(solution)/shard_map/ppermute | solution.py:473
  19.3 3.0 %collective-permute-done.5.refs_0_.refs_5_.refs_3_ = f32[264,128]{1,0:T(8,128)S(1)} collective-permute-done((f32[264,128]{1,0:T(8,128)S(1)}, f32[264,128]{1,0:T(8,128)S(1)}, u32[]{:S(2)}, u32[]{:S(2)}) %collective-permute-start.5) | collective-permute-done | bytes 135200 | tf_op jit(solution)/shard_map/ppermute | solution.py:473
  22.3 0.5 %coupling.4.refs_2_ = f32[256,128]{1,0:T(8,128)S(1)} custom-call(bf16[128,2304]{1,0:T(8,128)(2,1)S(1)} %get-tuple-element.38.own_ref, f32[264,128]{1,0:T(8,128)S(1)} %collective-permute-done.5.refs_0_.refs_5_.refs_3_, f32[256,128]{1,0:T(8,128)S(1)} %coupling.3.refs_1_), custom_call_target="tpu_custom_call" | custom-call | flops 4000000000 | tf_op jit(solution)/shard_map/coupling/pallas_call | solution.py:500
  22.9 0.6 %coupling.5.refs_7_ = f32[256,128]{1,0:T(8,128)S(1)} custom-call(bf16[128,2304]{1,0:T(8,128)(2,1)S(1)} %get-tuple-element.38.own_ref, f32[280,128]{1,0:T(8,128)S(1)} %collective-permute-done.3.refs_0_.refs_3_.refs_1_, f32[280,128]{1,0:T(8,128)S(1)} %collective-permute-done.4.refs_1_.refs_4_.refs_2_, f32[256,128]{1,0:T(8,128)S(1)} %coupling.4.refs_2_), custom_call_target="tpu_custom_call" | custom-call | flops 4000000000 | tf_op jit(solution)/shard_map/coupling/pallas_call | solution.py:500
  23.4 3.9 %second_round.1 = (f32[256,128]{1,0:T(8,128)S(1)}, f32[256,128]{1,0:T(8,128)S(1)}, f32[16,256]{1,0:T(8,128)S(1)}) custom-call(f32[16,128]{1,0:T(8,128)S(1)} %get-tuple-element.33.refs_0_, f32[16,128]{1,0:T(8,128)S(1)} %collective-permute-done.1.refs_1_, f32[264,128]{1,0:T(8,128)S(1)} %collective-permute-done.2.refs_0_.refs_2_, ...), custom_call_target="tpu_custom_call" | custom-call | tf_op jit(solution)/shard_map/second_round/pallas_call | solution.py:500
  27.4 2.5 %collective-permute-start.6 = (f32[256,128]{1,0:T(8,128)S(1)}, f32[256,128]{1,0:T(8,128)S(1)}, u32[]{:S(2)}, u32[]{:S(2)}) collective-permute-start(f32[256,128]{1,0:T(8,128)S(1)} %get-tuple-element.42.edge_ref), channel_id=1, source_target_pairs={{0,8},{4,12},{8,0},{12,4},{1,9},{5,13},{9,1},{13,5},{2,10},{6,14},... | collective-permute-start | bytes 393224 | tf_op jit(solution)/shard_map/ppermute | solution.py:472
  30.2 1.5 %collective-permute-start.10 = (f32[16,128]{1,0:T(8,128)S(1)}, f32[16,128]{1,0:T(8,128)S(1)}, u32[]{:S(2)}, u32[]{:S(2)}) collective-permute-start(f32[16,128]{1,0:T(8,128)S(1)} %get-tuple-element.48), channel_id=1, source_target_pairs={{2,0},{0,2},{3,1},{1,3},{6,4},{4,6},{7,5},{5,7},{10,8},{8,10},{11,... | collective-permute-start | bytes 24584 | tf_op jit(solution)/shard_map/ppermute | solution.py:473
  31.7 0.8 %injection.1 = f32[1,256,256]{2,1,0:T(8,128)} custom-call(f32[256,128]{1,0:T(8,128)S(1)} %get-tuple-element.42.edge_ref, f32[256,128]{1,0:T(8,128)S(1)} %get-tuple-element.43.rest_ref), custom_call_target="tpu_custom_call" | custom-call | tf_op jit(solution)/shard_map/injection/pallas_call | solution.py:500
  32.6 0.5 %collective-permute-start.9 = (f32[256,128]{1,0:T(8,128)S(1)}, f32[256,128]{1,0:T(8,128)S(1)}, u32[]{:S(2)}, u32[]{:S(2)}) collective-permute-start(f32[256,128]{1,0:T(8,128)S(1)} %get-tuple-element.42.edge_ref), channel_id=1, source_target_pairs={{2,0},{0,2},{3,1},{1,3},{6,4},{4,6},{7,5},{5,7},{10,8},{8,10},{11,... | collective-permute-start | bytes 393224 | tf_op jit(solution)/shard_map/ppermute | solution.py:473
  33.1 1.0 %collective-permute-start.8 = (f32[256,128]{1,0:T(8,128)S(1)}, f32[256,128]{1,0:T(8,128)S(1)}, u32[]{:S(2)}, u32[]{:S(2)}) collective-permute-start(f32[256,128]{1,0:T(8,128)S(1)} %get-tuple-element.42.edge_ref), channel_id=1, source_target_pairs={{0,4},{4,0},{8,12},{12,8},{1,5},{5,1},{9,13},{13,9},{2,6},{6,2},{1... | collective-permute-start | bytes 393224 | tf_op jit(solution)/shard_map/ppermute | solution.py:472
  34.1 1.4 %collective-permute-start.7 = (f32[256,128]{1,0:T(8,128)S(1)}, f32[256,128]{1,0:T(8,128)S(1)}, u32[]{:S(2)}, u32[]{:S(2)}) collective-permute-start(f32[256,128]{1,0:T(8,128)S(1)} %get-tuple-element.42.edge_ref), channel_id=1, source_target_pairs={{0,12},{4,8},{8,4},{12,0},{1,13},{5,9},{9,5},{13,1},{2,14},{6,10},... | collective-permute-start | bytes 393224 | tf_op jit(solution)/shard_map/ppermute | solution.py:472
  36.0 0.6 %line_table.1.table_ref = bf16[6,384,128]{2,1,0:T(8,128)(2,1)S(1)} custom-call(f32[280,128]{1,0:T(8,128)S(1)} %get-tuple-element.28.edge_ref.own_ref.refs_12_, f32[264,128]{1,0:T(8,128)S(1)} %collective-permute-done.2.refs_0_.refs_2_, f32[280,128]{1,0:T(8,128)S(1)} %collective-permute-done.3.refs_0_.refs_3_.refs_1_, ...), custom_call_target="tpu_custom_call" | custom-call | tf_op jit(solution)/shard_map/line_table/pallas_call | solution.py:500
  36.6 2.5 %collective-permute-start.13 = (f32[16,128]{1,0:T(8,128)S(1)}, f32[16,128]{1,0:T(8,128)S(1)}, u32[]{:S(2)}, u32[]{:S(2)}) collective-permute-start(f32[16,128]{1,0:T(8,128)S(1)} %add.3.refs_0_), channel_id=1, source_target_pairs={{0,12},{4,8},{8,4},{12,0},{1,13},{5,9},{9,5},{13,1},{2,14},{6,10},... | collective-permute-start | bytes 24584 | tf_op jit(solution)/shard_map/ppermute | solution.py:472
  39.1 2.7 %collective-permute-start.11 = (f32[16,128]{1,0:T(8,128)S(1)}, f32[16,128]{1,0:T(8,128)S(1)}, u32[]{:S(2)}, u32[]{:S(2)}) collective-permute-start(f32[16,128]{1,0:T(8,128)S(1)} %add.3.refs_0_), channel_id=1, source_target_pairs={{0,8},{4,12},{8,0},{12,4},{1,9},{5,13},{9,1},{13,5},{2,10},{6,14},... | collective-permute-start | bytes 24584 | tf_op jit(solution)/shard_map/ppermute | solution.py:472
  41.8 1.8 %tie_flows.1 = (f32[1,6,384,256]{3,2,1,0:T(8,128)}, f32[8,128]{1,0:T(8,128)S(1)}) custom-call(bf16[6,384,128]{2,1,0:T(8,128)(2,1)S(1)} %line_table.1.table_ref, f32[6,384,256]{2,1,0:T(8,128)S(1)} %own_flows.1.own_ref, bf16[256,256]{1,0:T(8,128)(2,1)S(1)} %injection_parts.1.refs_0_, f32[256,128]{1,0:T(8,128)S(1)} %collective-permute-done.7.refs_1_, ...), custom_call_target="tpu_custom_call" | custom-call | flops 4000000000 | tf_op jit(solution)/shard_map/tie_flows/pallas_call | solution.py:500
  43.8 0.6 %zone_prices.1 = f32[4,256]{1,0:T(4,128)} custom-call(f32[16,256]{1,0:T(8,128)S(1)} %get-tuple-element.45.first_ref, f32[8,128]{1,0:T(8,128)S(1)} %get-tuple-element.46.done_ref, f32[16,128]{1,0:T(8,128)S(1)} %add.3.refs_0_, f32[16,128]{1,0:T(8,128)S(1)} %collective-permute-done.11.refs_1_, f32[16,128]{1,0:T(8,128)S(1)} %collective-permute-done.12.refs_2_, ...), custom_call_target="tpu_custom_call" | custom-call | tf_op jit(solution)/shard_map/zone_prices/pallas_call | solution.py:500
  (34 shorter events, 1.8 us)
Async XLA Ops:
  0.6 0.8 %copy-start.2 = (s32[1,6,384]{2,0,1:T(1,128)S(1)}, s32[1,6,384]{2,0,1:T(1,128)}, u32[]{:S(2)}) copy-start(s32[1,6,384]{2,0,1:T(1,128)} %param.12) | copy-start | bytes 27652
  0.6 0.8 %copy-start.5 = (s32[1,6]{1,0:T(1,128)S(1)}, s32[1,6]{1,0:T(1,128)}, u32[]{:S(2)}) copy-start(s32[1,6]{1,0:T(1,128)} %count_ref.1) | copy-start | bytes 76
  0.7 0.8 %copy-start.4 = (s32[1,6]{1,0:T(1,128)S(1)}, s32[1,6]{1,0:T(1,128)}, u32[]{:S(2)}) copy-start(s32[1,6]{1,0:T(1,128)} %active_ref.1) | copy-start | bytes 76
  0.7 1.3 %copy-start.3 = (f32[1,256]{1,0:T(1,128)S(1)}, f32[1,256]{1,0:T(1,128)}, u32[]{:S(2)}) copy-start(f32[1,256]{1,0:T(1,128)} %refs_11_.1) | copy-start | bytes 3076
  0.7 1.3 %copy-start.1 = (f32[1,256,256]{2,1,0:T(8,128)S(1)}, f32[1,256,256]{2,1,0:T(8,128)}, u32[]{:S(2)}) copy-start(f32[1,256,256]{2,1,0:T(8,128)} %load_ref.1) | copy-start | bytes 786436
  0.7 1.3 %copy-start = (f32[1,256,256]{2,1,0:T(8,128)S(1)}, f32[1,256,256]{2,1,0:T(8,128)}, u32[]{:S(2)}) copy-start(f32[1,256,256]{2,1,0:T(8,128)} %k_ref.1) | copy-start | bytes 786436
  5.7 13.1 %collective-permute-start.2 = (f32[264,128]{1,0:T(8,128)S(1)}, f32[264,128]{1,0:T(8,128)S(1)}, u32[]{:S(2)}, u32[]{:S(2)}) collective-permute-start(f32[264,128]{1,0:T(8,128)S(1)} %get-tuple-element.34), channel_id=1, source_target_pairs={{0,8},{4,12},{8,0},{12,4},{1,9},{5,13},{9,1},{13,5},{2,10},{6,14},... | collective-permute-start | bytes 405512 | tf_op jit(solution)/shard_map/ppermute | solution.py:472
  10.0 3.7 %collective-permute-start = (f32[16,128]{1,0:T(8,128)S(1)}, f32[16,128]{1,0:T(8,128)S(1)}, u32[]{:S(2)}, u32[]{:S(2)}) collective-permute-start(f32[16,128]{1,0:T(8,128)S(1)} %get-tuple-element.31), channel_id=1, source_target_pairs={{2,0},{0,2},{3,1},{1,3},{6,4},{4,6},{7,5},{5,7},{10,8},{8,10},{11,... | collective-permute-start | bytes 24584 | tf_op jit(solution)/shard_map/ppermute | solution.py:473
  13.8 9.1 %collective-permute-start.4 = (f32[280,128]{1,0:T(8,128)S(1)}, f32[280,128]{1,0:T(8,128)S(1)}, u32[]{:S(2)}, u32[]{:S(2)}) collective-permute-start(f32[280,128]{1,0:T(8,128)S(1)} %get-tuple-element.35), channel_id=1, source_target_pairs={{0,4},{4,0},{8,12},{12,8},{1,5},{5,1},{9,13},{13,9},{2,6},{6,2},{1... | collective-permute-start | bytes 430088 | tf_op jit(solution)/shard_map/ppermute | solution.py:472
  15.4 7.5 %collective-permute-start.3 = (f32[280,128]{1,0:T(8,128)S(1)}, f32[280,128]{1,0:T(8,128)S(1)}, u32[]{:S(2)}, u32[]{:S(2)}) collective-permute-start(f32[280,128]{1,0:T(8,128)S(1)} %get-tuple-element.35), channel_id=1, source_target_pairs={{0,12},{4,8},{8,4},{12,0},{1,13},{5,9},{9,5},{13,1},{2,14},{6,10},... | collective-permute-start | bytes 430088 | tf_op jit(solution)/shard_map/ppermute | solution.py:472
  15.4 8.0 %collective-permute-start.1 = (f32[16,128]{1,0:T(8,128)S(1)}, f32[16,128]{1,0:T(8,128)S(1)}, u32[]{:S(2)}, u32[]{:S(2)}) collective-permute-start(f32[16,128]{1,0:T(8,128)S(1)} %get-tuple-element.33.refs_0_), channel_id=1, source_target_pairs={{0,8},{4,12},{8,0},{12,4},{1,9},{5,13},{9,1},{13,5},{2,10},{6,14},... | collective-permute-start | bytes 24584 | tf_op jit(solution)/shard_map/ppermute | solution.py:472
  17.3 5.0 %collective-permute-start.5 = (f32[264,128]{1,0:T(8,128)S(1)}, f32[264,128]{1,0:T(8,128)S(1)}, u32[]{:S(2)}, u32[]{:S(2)}) collective-permute-start(f32[264,128]{1,0:T(8,128)S(1)} %get-tuple-element.36), channel_id=1, source_target_pairs={{2,0},{0,2},{3,1},{1,3},{6,4},{4,6},{7,5},{5,7},{10,8},{8,10},{11,... | collective-permute-start | bytes 405512 | tf_op jit(solution)/shard_map/ppermute | solution.py:473
  27.4 11.7 %collective-permute-start.6 = (f32[256,128]{1,0:T(8,128)S(1)}, f32[256,128]{1,0:T(8,128)S(1)}, u32[]{:S(2)}, u32[]{:S(2)}) collective-permute-start(f32[256,128]{1,0:T(8,128)S(1)} %get-tuple-element.42.edge_ref), channel_id=1, source_target_pairs={{0,8},{4,12},{8,0},{12,4},{1,9},{5,13},{9,1},{13,5},{2,10},{6,14},... | collective-permute-start | bytes 393224 | tf_op jit(solution)/shard_map/ppermute | solution.py:472
  30.2 6.4 %collective-permute-start.10 = (f32[16,128]{1,0:T(8,128)S(1)}, f32[16,128]{1,0:T(8,128)S(1)}, u32[]{:S(2)}, u32[]{:S(2)}) collective-permute-start(f32[16,128]{1,0:T(8,128)S(1)} %get-tuple-element.48), channel_id=1, source_target_pairs={{2,0},{0,2},{3,1},{1,3},{6,4},{4,6},{7,5},{5,7},{10,8},{8,10},{11,... | collective-permute-start | bytes 24584 | tf_op jit(solution)/shard_map/ppermute | solution.py:473
  32.6 6.6 %collective-permute-start.9 = (f32[256,128]{1,0:T(8,128)S(1)}, f32[256,128]{1,0:T(8,128)S(1)}, u32[]{:S(2)}, u32[]{:S(2)}) collective-permute-start(f32[256,128]{1,0:T(8,128)S(1)} %get-tuple-element.42.edge_ref), channel_id=1, source_target_pairs={{2,0},{0,2},{3,1},{1,3},{6,4},{4,6},{7,5},{5,7},{10,8},{8,10},{11,... | collective-permute-start | bytes 393224 | tf_op jit(solution)/shard_map/ppermute | solution.py:473
  33.1 8.7 %collective-permute-start.8 = (f32[256,128]{1,0:T(8,128)S(1)}, f32[256,128]{1,0:T(8,128)S(1)}, u32[]{:S(2)}, u32[]{:S(2)}) collective-permute-start(f32[256,128]{1,0:T(8,128)S(1)} %get-tuple-element.42.edge_ref), channel_id=1, source_target_pairs={{0,4},{4,0},{8,12},{12,8},{1,5},{5,1},{9,13},{13,9},{2,6},{6,2},{1... | collective-permute-start | bytes 393224 | tf_op jit(solution)/shard_map/ppermute | solution.py:472
  34.1 7.7 %collective-permute-start.7 = (f32[256,128]{1,0:T(8,128)S(1)}, f32[256,128]{1,0:T(8,128)S(1)}, u32[]{:S(2)}, u32[]{:S(2)}) collective-permute-start(f32[256,128]{1,0:T(8,128)S(1)} %get-tuple-element.42.edge_ref), channel_id=1, source_target_pairs={{0,12},{4,8},{8,4},{12,0},{1,13},{5,9},{9,5},{13,1},{2,14},{6,10},... | collective-permute-start | bytes 393224 | tf_op jit(solution)/shard_map/ppermute | solution.py:472
  36.6 7.0 %collective-permute-start.13 = (f32[16,128]{1,0:T(8,128)S(1)}, f32[16,128]{1,0:T(8,128)S(1)}, u32[]{:S(2)}, u32[]{:S(2)}) collective-permute-start(f32[16,128]{1,0:T(8,128)S(1)} %add.3.refs_0_), channel_id=1, source_target_pairs={{0,12},{4,8},{8,4},{12,0},{1,13},{5,9},{9,5},{13,1},{2,14},{6,10},... | collective-permute-start | bytes 24584 | tf_op jit(solution)/shard_map/ppermute | solution.py:472
  39.1 4.5 %collective-permute-start.12 = (f32[16,128]{1,0:T(8,128)S(1)}, f32[16,128]{1,0:T(8,128)S(1)}, u32[]{:S(2)}, u32[]{:S(2)}) collective-permute-start(f32[16,128]{1,0:T(8,128)S(1)} %add.3.refs_0_), channel_id=1, source_target_pairs={{0,4},{4,0},{8,12},{12,8},{1,5},{5,1},{9,13},{13,9},{2,6},{6,2},{1... | collective-permute-start | bytes 24584 | tf_op jit(solution)/shard_map/ppermute | solution.py:472
  39.1 4.6 %collective-permute-start.11 = (f32[16,128]{1,0:T(8,128)S(1)}, f32[16,128]{1,0:T(8,128)S(1)}, u32[]{:S(2)}, u32[]{:S(2)}) collective-permute-start(f32[16,128]{1,0:T(8,128)S(1)} %add.3.refs_0_), channel_id=1, source_target_pairs={{0,8},{4,12},{8,0},{12,4},{1,9},{5,13},{9,1},{13,5},{2,10},{6,14},... | collective-permute-start | bytes 24584 | tf_op jit(solution)/shard_map/ppermute | solution.py:472

commit v7 on v5

--- a/solution.py
+++ b/solution.py
@@ -217,16 +217,14 @@
     share_ref[...] = sums[0 : share_ref.shape[0], :]
 
 
-def append_kernel(scens, kept, zone_at, share_ref, across_ref, edge_ref, side_ref, pair_ref, full_ref, side_out_ref):
+def append_kernel(scens, kept, zone_at, share_ref, across_ref, edge_ref, pair_ref, full_ref):
     pair = share_ref[...] + across_ref[...]
     rows = pair.shape[0]
     pair_ref[...] = pair
     full_ref[pl.ds(0, scens), :] = edge_ref[pl.ds(0, scens), :]
     full_ref[pl.ds(scens, rows), :] = pair
-    if kept:
-        full_ref[pl.ds(scens + rows, kept), :] = edge_ref[pl.ds(scens, kept), :]
-        full_ref[pl.ds(scens + rows + kept, 1), :] = edge_ref[pl.ds(zone_at, 1), :]
-    side_out_ref[...] = side_ref[...]
+    full_ref[pl.ds(scens + rows, kept), :] = edge_ref[pl.ds(scens, kept), :]
+    full_ref[pl.ds(scens + rows + kept, 1), :] = edge_ref[pl.ds(zone_at, 1), :]
 
 
 def live_lines(edge_ref, scens, slots, pieces, p):
@@ -276,7 +274,7 @@
             self.sources = [("area", Mask(2)), ("area", Mask(3)), ("area", Mask(1)), ("region", 1)]
             self.slots_of = [(2, 3), ((1, 0),), ((0, 1),), (4, 5)]
             self.buffer_of = [(2, 1), (1, 2), 0, 0, 3, 3]
-            self.arrivals = [(0,), (1, 2, 3)]
+            self.arrivals = [(0,), (3,), (1, 2)]
             self.last = (1, 2, 3)
             return
         self.sources, self.slots_of, self.buffer_of = [], [], [None] * slots
@@ -529,21 +527,14 @@
         if not near:
             return [moved(edge, axis, move) for axis, move in plan.sources], [lax.psum(share, ("area", "region"))]
         far, side = leans
-        pair, full, side = call(
+        pair, full = call(
             functools.partial(append_kernel, scens, kept, zone_at),
             "pair_shares",
-            [
-                f32(plan.fold, LANES),
-                f32(scens + plan.fold + -(-(kept and kept + 1) // 8) * 8, BOUNDARY),
-                f32(*side.shape),
-            ],
-            [share, moved(across[0], "region", 1), edge, side],
+            [f32(plan.fold, LANES), f32(scens + plan.fold + -(-(kept + 1) // 8) * 8, BOUNDARY)],
+            [share, moved(across[0], "region", 1), edge],
         )
-        got_side = moved(side, "region", 1)
-        opposite = moved(pair, "area", Mask(2))
-        got_near = moved(full, "area", Mask(1))
-        got_other = moved(full, "area", Mask(3))
-        return [moved(far, "area", Mask(2)), got_other, got_near, got_side], [pair, opposite]
+        got = [moved(x, *source) for x, source in zip((far, full, full, side), plan.sources)]
+        return got, [pair, moved(pair, "area", Mask(2))]
 
     zeros = call(opening_kernel, "opening", f32(8, LANES), [], OPENING)
     lean_rows = -(-(scens + 2 * pieces + 1) // 8) * 8

time: 44.5 us -> 44.6 us (level)
  starting transfers between devices: 23.1 us -> 22.1 us
  waiting for transfers between devices: 5 us -> 5.63 us
  Pallas kernels: 14.6 us -> 15.1 us
    ppermute x10, waiting for transfers between devices: 0.39 us -> 4.47 us  [moved(): return lax.ppermute(x, axis, [(i, i ^ by) for i in range(length)])]
    ppermute x4, waiting for transfers between devices: 4.61 us -> 1.16 us  [moved(): lax.ppermute(x, axis, [((i + by) % length, i) for i in range(length)])]
    ppermute x4, starting transfers between devices: 5.14 us -> 4.18 us  [moved(): lax.ppermute(x, axis, [((i + by) % length, i) for i in range(length)])]
    pallas_call x16 -> x17, Pallas kernels: 14.6 us -> 15.1 us  [call(): pl.pallas_call(kernel, out_shape=out_shape, in_specs=more.pop('in_specs',...]
  transfers between devices with their start and end apart: 14 -> 14, of which waited for: 4 -> 5; matrix products, arithmetic and copies ran while one was open for 0% -> 0% of each run, Pallas kernels for 13% -> 14%
where the time goes in v7:
time: 44.6 us; the launch traced here: 44.5 us
  starting transfers between devices  22.1 us (50%)
  Pallas kernels  15.1 us (34%)
  waiting for transfers between devices  5.63 us (13%)
  between operations  1.55 us (3%)
    ppermute x10, starting transfers between devices, moved(): return lax.ppermute(x, axis, [(i, i ^ by) for i in range(length)])  17.9 us
    pallas_call x17, Pallas kernels, call(): pl.pallas_call(kernel, out_shape=out_shape, in_specs=more.pop('in_specs',...  15.1 us
    ppermute x10, waiting for transfers between devices, moved(): return lax.ppermute(x, axis, [(i, i ^ by) for i in range(length)])  4.47 us
    ppermute x4, starting transfers between devices, moved(): lax.ppermute(x, axis, [((i + by) % length, i) for i in range(length)])  4.18 us
    ppermute x4, waiting for transfers between devices, moved(): lax.ppermute(x, axis, [((i + by) % length, i) for i in range(length)])  1.16 us
  transfers between devices with their start and end apart: 14, of which 5 were waited for; matrix products, arithmetic and copies ran while one was open for 0% of the time, Pallas kernels for 14%

profile of v7, /device:TPU:0, one launch (start us, length us, event | category | flops | bytes accessed | tf_op | source)
XLA Modules:
  0.0 44.5 jit_solution(4385760411511319145)
XLA Ops:
  1.4 0.5 %line_blocks.1 = (f32[24,128]{1,0:T(8,128)S(1)}, bf16[128,2304]{1,0:T(8,128)(2,1)S(1)}, f32[16,256]{1,0:T(8,128)S(1)}) custom-call(f32[8,128]{1,0:T(8,128)S(1)} %opening.1.zeros_ref, s32[6,1,384]{2,1,0:T(1,128)S(1)} %bitcast.1, s32[1,6]{1,0:T(1,128)S(1)} %copy-done.4, s32[1,6]{1,0:T(1,128)S(1)} %copy-done.5, s32[1]{0:T(128)S(6)} %copy.10.zone_ref), custom_call_target="tpu_custom_call" | custom-call | tf_op jit(solution)/shard_map/line_blocks/pallas_call | solution.py:496
  2.0 3.7 %first_round.1 = (f32[280,128]{1,0:T(8,128)S(1)}, f32[264,128]{1,0:T(8,128)S(1)}, f32[264,128]{1,0:T(8,128)S(1)}, f32[256,128]{1,0:T(8,128)S(1)}, f32[256,256]{1...) custom-call(f32[1,256,256]{2,1,0:T(8,128)S(1)} %copy-done, ...), custom_call_target="tpu_custom_call" | custom-call | tf_op jit(solution)/shard_map/first_round/pallas_call | solution.py:496
  5.7 4.1 %collective-permute-start.2 = (f32[264,128]{1,0:T(8,128)S(1)}, f32[264,128]{1,0:T(8,128)S(1)}, u32[]{:S(2)}, u32[]{:S(2)}) collective-permute-start(f32[264,128]{1,0:T(8,128)S(1)} %get-tuple-element.32), channel_id=1, source_target_pairs={{0,8},{4,12},{8,0},{12,4},{1,9},{5,13},{9,1},{13,5},{2,10},{6,14},... | collective-permute-start | bytes 405512 | tf_op jit(solution)/shard_map/ppermute | solution.py:468
  10.0 1.6 %collective-permute-start = (f32[16,128]{1,0:T(8,128)S(1)}, f32[16,128]{1,0:T(8,128)S(1)}, u32[]{:S(2)}, u32[]{:S(2)}) collective-permute-start(f32[16,128]{1,0:T(8,128)S(1)} %get-tuple-element.30), channel_id=1, source_target_pairs={{2,0},{0,2},{3,1},{1,3},{6,4},{4,6},{7,5},{5,7},{10,8},{8,10},{11,... | collective-permute-start | bytes 24584 | tf_op jit(solution)/shard_map/ppermute | solution.py:469
  11.6 0.5 %collective-permute-start.5 = (f32[264,128]{1,0:T(8,128)S(1)}, f32[264,128]{1,0:T(8,128)S(1)}, u32[]{:S(2)}, u32[]{:S(2)}) collective-permute-start(f32[264,128]{1,0:T(8,128)S(1)} %get-tuple-element.34), channel_id=1, source_target_pairs={{2,0},{0,2},{3,1},{1,3},{6,4},{4,6},{7,5},{5,7},{10,8},{8,10},{11,... | collective-permute-start | bytes 405512 | tf_op jit(solution)/shard_map/ppermute | solution.py:469
  12.1 0.6 %own_table.1.refs_13_.table_ref = bf16[6,384,128]{2,1,0:T(8,128)(2,1)S(1)} custom-call(f32[280,128]{1,0:T(8,128)S(1)} %get-tuple-element.27.edge_ref.own_ref.refs_12_), custom_call_target="tpu_custom_call" | custom-call | tf_op jit(solution)/shard_map/own_table/pallas_call | solution.py:496
  12.7 1.2 %collective-permute-done.across_ref = f32[16,128]{1,0:T(8,128)S(1)} collective-permute-done((f32[16,128]{1,0:T(8,128)S(1)}, f32[16,128]{1,0:T(8,128)S(1)}, u32[]{:S(2)}, u32[]{:S(2)}) %collective-permute-start) | collective-permute-done | bytes 8224 | tf_op jit(solution)/shard_map/ppermute | solution.py:469
  13.9 1.6 %collective-permute-start.4 = (f32[280,128]{1,0:T(8,128)S(1)}, f32[280,128]{1,0:T(8,128)S(1)}, u32[]{:S(2)}, u32[]{:S(2)}) collective-permute-start(f32[280,128]{1,0:T(8,128)S(1)} %get-tuple-element.33), channel_id=1, source_target_pairs={{0,4},{4,0},{8,12},{12,8},{1,5},{5,1},{9,13},{13,9},{2,6},{6,2},{1... | collective-permute-start | bytes 430088 | tf_op jit(solution)/shard_map/ppermute | solution.py:468
  15.5 1.9 %collective-permute-start.1 = (f32[16,128]{1,0:T(8,128)S(1)}, f32[16,128]{1,0:T(8,128)S(1)}, u32[]{:S(2)}, u32[]{:S(2)}) collective-permute-start(f32[16,128]{1,0:T(8,128)S(1)} %get-tuple-element.31.refs_0_), channel_id=1, source_target_pairs={{0,8},{4,12},{8,0},{12,4},{1,9},{5,13},{9,1},{13,5},{2,10},{6,14},... | collective-permute-start | bytes 24584 | tf_op jit(solution)/shard_map/ppermute | solution.py:468
  18.4 2.5 %collective-permute-done.4.refs_1_.refs_4_.refs_2_ = f32[280,128]{1,0:T(8,128)S(1)} collective-permute-done((f32[280,128]{1,0:T(8,128)S(1)}, f32[280,128]{1,0:T(8,128)S(1)}, u32[]{:S(2)}, u32[]{:S(2)}) %collective-permute-start.4) | collective-permute-done | bytes 143392 | tf_op jit(solution)/shard_map/ppermute | solution.py:468
  21.0 1.5 %collective-permute-done.3.refs_0_.refs_3_.refs_1_ = f32[280,128]{1,0:T(8,128)S(1)} collective-permute-done((f32[280,128]{1,0:T(8,128)S(1)}, f32[280,128]{1,0:T(8,128)S(1)}, u32[]{:S(2)}, u32[]{:S(2)}) %collective-permute-start.3) | collective-permute-done | bytes 143392 | tf_op jit(solution)/shard_map/ppermute | solution.py:468
  22.5 0.5 %coupling.5.refs_7_ = f32[256,128]{1,0:T(8,128)S(1)} custom-call(bf16[128,2304]{1,0:T(8,128)(2,1)S(1)} %get-tuple-element.36.own_ref, f32[280,128]{1,0:T(8,128)S(1)} %collective-permute-done.3.refs_0_.refs_3_.refs_1_, f32[280,128]{1,0:T(8,128)S(1)} %collective-permute-done.4.refs_1_.refs_4_.refs_2_, f32[256,128]{1,0:T(8,128)S(1)} %coupling.4.refs_2_), custom_call_target="tpu_custom_call" | custom-call | flops 4000000000 | tf_op jit(solution)/shard_map/coupling/pallas_call | solution.py:496
  23.3 3.9 %second_round.1 = (f32[256,128]{1,0:T(8,128)S(1)}, f32[256,128]{1,0:T(8,128)S(1)}, f32[16,256]{1,0:T(8,128)S(1)}) custom-call(f32[16,128]{1,0:T(8,128)S(1)} %get-tuple-element.31.refs_0_, f32[16,128]{1,0:T(8,128)S(1)} %collective-permute-done.1.refs_1_, f32[264,128]{1,0:T(8,128)S(1)} %collective-permute-done.2.refs_0_.refs_2_, ...), custom_call_target="tpu_custom_call" | custom-call | tf_op jit(solution)/shard_map/second_round/pallas_call | solution.py:496
  27.2 2.7 %collective-permute-start.6 = (f32[256,128]{1,0:T(8,128)S(1)}, f32[256,128]{1,0:T(8,128)S(1)}, u32[]{:S(2)}, u32[]{:S(2)}) collective-permute-start(f32[256,128]{1,0:T(8,128)S(1)} %get-tuple-element.40.edge_ref), channel_id=1, source_target_pairs={{0,8},{4,12},{8,0},{12,4},{1,9},{5,13},{9,1},{13,5},{2,10},{6,14},... | collective-permute-start | bytes 393224 | tf_op jit(solution)/shard_map/ppermute | solution.py:468
  30.2 1.6 %collective-permute-start.10 = (f32[16,128]{1,0:T(8,128)S(1)}, f32[16,128]{1,0:T(8,128)S(1)}, u32[]{:S(2)}, u32[]{:S(2)}) collective-permute-start(f32[16,128]{1,0:T(8,128)S(1)} %get-tuple-element.46), channel_id=1, source_target_pairs={{2,0},{0,2},{3,1},{1,3},{6,4},{4,6},{7,5},{5,7},{10,8},{8,10},{11,... | collective-permute-start | bytes 24584 | tf_op jit(solution)/shard_map/ppermute | solution.py:469
  31.7 0.8 %injection.1 = f32[1,256,256]{2,1,0:T(8,128)} custom-call(f32[256,128]{1,0:T(8,128)S(1)} %get-tuple-element.40.edge_ref, f32[256,128]{1,0:T(8,128)S(1)} %get-tuple-element.41.rest_ref), custom_call_target="tpu_custom_call" | custom-call | tf_op jit(solution)/shard_map/injection/pallas_call | solution.py:496
  32.6 0.5 %collective-permute-start.9 = (f32[256,128]{1,0:T(8,128)S(1)}, f32[256,128]{1,0:T(8,128)S(1)}, u32[]{:S(2)}, u32[]{:S(2)}) collective-permute-start(f32[256,128]{1,0:T(8,128)S(1)} %get-tuple-element.40.edge_ref), channel_id=1, source_target_pairs={{2,0},{0,2},{3,1},{1,3},{6,4},{4,6},{7,5},{5,7},{10,8},{8,10},{11,... | collective-permute-start | bytes 393224 | tf_op jit(solution)/shard_map/ppermute | solution.py:469
  33.1 1.0 %collective-permute-start.8 = (f32[256,128]{1,0:T(8,128)S(1)}, f32[256,128]{1,0:T(8,128)S(1)}, u32[]{:S(2)}, u32[]{:S(2)}) collective-permute-start(f32[256,128]{1,0:T(8,128)S(1)} %get-tuple-element.40.edge_ref), channel_id=1, source_target_pairs={{0,4},{4,0},{8,12},{12,8},{1,5},{5,1},{9,13},{13,9},{2,6},{6,2},{1... | collective-permute-start | bytes 393224 | tf_op jit(solution)/shard_map/ppermute | solution.py:468
  34.1 0.7 %collective-permute-start.7 = (f32[256,128]{1,0:T(8,128)S(1)}, f32[256,128]{1,0:T(8,128)S(1)}, u32[]{:S(2)}, u32[]{:S(2)}) collective-permute-start(f32[256,128]{1,0:T(8,128)S(1)} %get-tuple-element.40.edge_ref), channel_id=1, source_target_pairs={{0,12},{4,8},{8,4},{12,0},{1,13},{5,9},{9,5},{13,1},{2,14},{6,10},... | collective-permute-start | bytes 393224 | tf_op jit(solution)/shard_map/ppermute | solution.py:468
  35.3 0.6 %line_table.1.table_ref = bf16[6,384,128]{2,1,0:T(8,128)(2,1)S(1)} custom-call(f32[280,128]{1,0:T(8,128)S(1)} %get-tuple-element.27.edge_ref.own_ref.refs_12_, f32[264,128]{1,0:T(8,128)S(1)} %collective-permute-done.2.refs_0_.refs_2_, f32[280,128]{1,0:T(8,128)S(1)} %collective-permute-done.3.refs_0_.refs_3_.refs_1_, ...), custom_call_target="tpu_custom_call" | custom-call | tf_op jit(solution)/shard_map/line_table/pallas_call | solution.py:496
  35.9 3.1 %collective-permute-start.13 = (f32[16,128]{1,0:T(8,128)S(1)}, f32[16,128]{1,0:T(8,128)S(1)}, u32[]{:S(2)}, u32[]{:S(2)}) collective-permute-start(f32[16,128]{1,0:T(8,128)S(1)} %add.3.refs_0_), channel_id=1, source_target_pairs={{0,12},{4,8},{8,4},{12,0},{1,13},{5,9},{9,5},{13,1},{2,14},{6,10},... | collective-permute-start | bytes 24584 | tf_op jit(solution)/shard_map/ppermute | solution.py:468
  39.1 2.7 %collective-permute-start.11 = (f32[16,128]{1,0:T(8,128)S(1)}, f32[16,128]{1,0:T(8,128)S(1)}, u32[]{:S(2)}, u32[]{:S(2)}) collective-permute-start(f32[16,128]{1,0:T(8,128)S(1)} %add.3.refs_0_), channel_id=1, source_target_pairs={{0,8},{4,12},{8,0},{12,4},{1,9},{5,13},{9,1},{13,5},{2,10},{6,14},... | collective-permute-start | bytes 24584 | tf_op jit(solution)/shard_map/ppermute | solution.py:468
  42.0 1.8 %tie_flows.1 = (f32[1,6,384,256]{3,2,1,0:T(8,128)}, f32[8,128]{1,0:T(8,128)S(1)}) custom-call(bf16[6,384,128]{2,1,0:T(8,128)(2,1)S(1)} %line_table.1.table_ref, f32[6,384,256]{2,1,0:T(8,128)S(1)} %own_flows.1.own_ref, bf16[256,256]{1,0:T(8,128)(2,1)S(1)} %injection_parts.1.refs_0_, f32[256,128]{1,0:T(8,128)S(1)} %collective-permute-done.7.refs_1_, ...), custom_call_target="tpu_custom_call" | custom-call | flops 4000000000 | tf_op jit(solution)/shard_map/tie_flows/pallas_call | solution.py:496
  43.8 0.6 %zone_prices.1 = f32[4,256]{1,0:T(4,128)} custom-call(f32[16,256]{1,0:T(8,128)S(1)} %get-tuple-element.43.first_ref, f32[8,128]{1,0:T(8,128)S(1)} %get-tuple-element.44.done_ref, f32[16,128]{1,0:T(8,128)S(1)} %add.3.refs_0_, f32[16,128]{1,0:T(8,128)S(1)} %collective-permute-done.11.refs_1_, f32[16,128]{1,0:T(8,128)S(1)} %collective-permute-done.12.refs_2_, ...), custom_call_target="tpu_custom_call" | custom-call | tf_op jit(solution)/shard_map/zone_prices/pallas_call | solution.py:496
  (34 shorter events, 2.5 us)
Async XLA Ops:
  0.6 0.8 %copy-start.2 = (s32[1,6,384]{2,0,1:T(1,128)S(1)}, s32[1,6,384]{2,0,1:T(1,128)}, u32[]{:S(2)}) copy-start(s32[1,6,384]{2,0,1:T(1,128)} %param.12) | copy-start | bytes 27652
  0.6 0.8 %copy-start.5 = (s32[1,6]{1,0:T(1,128)S(1)}, s32[1,6]{1,0:T(1,128)}, u32[]{:S(2)}) copy-start(s32[1,6]{1,0:T(1,128)} %count_ref.1) | copy-start | bytes 76
  0.7 0.8 %copy-start.4 = (s32[1,6]{1,0:T(1,128)S(1)}, s32[1,6]{1,0:T(1,128)}, u32[]{:S(2)}) copy-start(s32[1,6]{1,0:T(1,128)} %active_ref.1) | copy-start | bytes 76
  0.7 1.3 %copy-start.3 = (f32[1,256]{1,0:T(1,128)S(1)}, f32[1,256]{1,0:T(1,128)}, u32[]{:S(2)}) copy-start(f32[1,256]{1,0:T(1,128)} %refs_11_.1) | copy-start | bytes 3076
  0.7 1.3 %copy-start.1 = (f32[1,256,256]{2,1,0:T(8,128)S(1)}, f32[1,256,256]{2,1,0:T(8,128)}, u32[]{:S(2)}) copy-start(f32[1,256,256]{2,1,0:T(8,128)} %load_ref.1) | copy-start | bytes 786436
  0.7 1.3 %copy-start = (f32[1,256,256]{2,1,0:T(8,128)S(1)}, f32[1,256,256]{2,1,0:T(8,128)}, u32[]{:S(2)}) copy-start(f32[1,256,256]{2,1,0:T(8,128)} %k_ref.1) | copy-start | bytes 786436
  5.7 11.7 %collective-permute-start.2 = (f32[264,128]{1,0:T(8,128)S(1)}, f32[264,128]{1,0:T(8,128)S(1)}, u32[]{:S(2)}, u32[]{:S(2)}) collective-permute-start(f32[264,128]{1,0:T(8,128)S(1)} %get-tuple-element.32), channel_id=1, source_target_pairs={{0,8},{4,12},{8,0},{12,4},{1,9},{5,13},{9,1},{13,5},{2,10},{6,14},... | collective-permute-start | bytes 405512 | tf_op jit(solution)/shard_map/ppermute | solution.py:468
  10.0 3.8 %collective-permute-start = (f32[16,128]{1,0:T(8,128)S(1)}, f32[16,128]{1,0:T(8,128)S(1)}, u32[]{:S(2)}, u32[]{:S(2)}) collective-permute-start(f32[16,128]{1,0:T(8,128)S(1)} %get-tuple-element.30), channel_id=1, source_target_pairs={{2,0},{0,2},{3,1},{1,3},{6,4},{4,6},{7,5},{5,7},{10,8},{8,10},{11,... | collective-permute-start | bytes 24584 | tf_op jit(solution)/shard_map/ppermute | solution.py:469
  11.6 6.3 %collective-permute-start.5 = (f32[264,128]{1,0:T(8,128)S(1)}, f32[264,128]{1,0:T(8,128)S(1)}, u32[]{:S(2)}, u32[]{:S(2)}) collective-permute-start(f32[264,128]{1,0:T(8,128)S(1)} %get-tuple-element.34), channel_id=1, source_target_pairs={{2,0},{0,2},{3,1},{1,3},{6,4},{4,6},{7,5},{5,7},{10,8},{8,10},{11,... | collective-permute-start | bytes 405512 | tf_op jit(solution)/shard_map/ppermute | solution.py:469
  13.9 7.1 %collective-permute-start.4 = (f32[280,128]{1,0:T(8,128)S(1)}, f32[280,128]{1,0:T(8,128)S(1)}, u32[]{:S(2)}, u32[]{:S(2)}) collective-permute-start(f32[280,128]{1,0:T(8,128)S(1)} %get-tuple-element.33), channel_id=1, source_target_pairs={{0,4},{4,0},{8,12},{12,8},{1,5},{5,1},{9,13},{13,9},{2,6},{6,2},{1... | collective-permute-start | bytes 430088 | tf_op jit(solution)/shard_map/ppermute | solution.py:468
  15.5 7.0 %collective-permute-start.3 = (f32[280,128]{1,0:T(8,128)S(1)}, f32[280,128]{1,0:T(8,128)S(1)}, u32[]{:S(2)}, u32[]{:S(2)}) collective-permute-start(f32[280,128]{1,0:T(8,128)S(1)} %get-tuple-element.33), channel_id=1, source_target_pairs={{0,12},{4,8},{8,4},{12,0},{1,13},{5,9},{9,5},{13,1},{2,14},{6,10},... | collective-permute-start | bytes 430088 | tf_op jit(solution)/shard_map/ppermute | solution.py:468
  15.5 7.8 %collective-permute-start.1 = (f32[16,128]{1,0:T(8,128)S(1)}, f32[16,128]{1,0:T(8,128)S(1)}, u32[]{:S(2)}, u32[]{:S(2)}) collective-permute-start(f32[16,128]{1,0:T(8,128)S(1)} %get-tuple-element.31.refs_0_), channel_id=1, source_target_pairs={{0,8},{4,12},{8,0},{12,4},{1,9},{5,13},{9,1},{13,5},{2,10},{6,14},... | collective-permute-start | bytes 24584 | tf_op jit(solution)/shard_map/ppermute | solution.py:468
  27.2 11.9 %collective-permute-start.6 = (f32[256,128]{1,0:T(8,128)S(1)}, f32[256,128]{1,0:T(8,128)S(1)}, u32[]{:S(2)}, u32[]{:S(2)}) collective-permute-start(f32[256,128]{1,0:T(8,128)S(1)} %get-tuple-element.40.edge_ref), channel_id=1, source_target_pairs={{0,8},{4,12},{8,0},{12,4},{1,9},{5,13},{9,1},{13,5},{2,10},{6,14},... | collective-permute-start | bytes 393224 | tf_op jit(solution)/shard_map/ppermute | solution.py:468
  30.2 5.8 %collective-permute-start.10 = (f32[16,128]{1,0:T(8,128)S(1)}, f32[16,128]{1,0:T(8,128)S(1)}, u32[]{:S(2)}, u32[]{:S(2)}) collective-permute-start(f32[16,128]{1,0:T(8,128)S(1)} %get-tuple-element.46), channel_id=1, source_target_pairs={{2,0},{0,2},{3,1},{1,3},{6,4},{4,6},{7,5},{5,7},{10,8},{8,10},{11,... | collective-permute-start | bytes 24584 | tf_op jit(solution)/shard_map/ppermute | solution.py:469
  32.6 6.6 %collective-permute-start.9 = (f32[256,128]{1,0:T(8,128)S(1)}, f32[256,128]{1,0:T(8,128)S(1)}, u32[]{:S(2)}, u32[]{:S(2)}) collective-permute-start(f32[256,128]{1,0:T(8,128)S(1)} %get-tuple-element.40.edge_ref), channel_id=1, source_target_pairs={{2,0},{0,2},{3,1},{1,3},{6,4},{4,6},{7,5},{5,7},{10,8},{8,10},{11,... | collective-permute-start | bytes 393224 | tf_op jit(solution)/shard_map/ppermute | solution.py:469
  33.1 8.9 %collective-permute-start.8 = (f32[256,128]{1,0:T(8,128)S(1)}, f32[256,128]{1,0:T(8,128)S(1)}, u32[]{:S(2)}, u32[]{:S(2)}) collective-permute-start(f32[256,128]{1,0:T(8,128)S(1)} %get-tuple-element.40.edge_ref), channel_id=1, source_target_pairs={{0,4},{4,0},{8,12},{12,8},{1,5},{5,1},{9,13},{13,9},{2,6},{6,2},{1... | collective-permute-start | bytes 393224 | tf_op jit(solution)/shard_map/ppermute | solution.py:468
  34.1 7.9 %collective-permute-start.7 = (f32[256,128]{1,0:T(8,128)S(1)}, f32[256,128]{1,0:T(8,128)S(1)}, u32[]{:S(2)}, u32[]{:S(2)}) collective-permute-start(f32[256,128]{1,0:T(8,128)S(1)} %get-tuple-element.40.edge_ref), channel_id=1, source_target_pairs={{0,12},{4,8},{8,4},{12,0},{1,13},{5,9},{9,5},{13,1},{2,14},{6,10},... | collective-permute-start | bytes 393224 | tf_op jit(solution)/shard_map/ppermute | solution.py:468
  35.9 7.9 %collective-permute-start.13 = (f32[16,128]{1,0:T(8,128)S(1)}, f32[16,128]{1,0:T(8,128)S(1)}, u32[]{:S(2)}, u32[]{:S(2)}) collective-permute-start(f32[16,128]{1,0:T(8,128)S(1)} %add.3.refs_0_), channel_id=1, source_target_pairs={{0,12},{4,8},{8,4},{12,0},{1,13},{5,9},{9,5},{13,1},{2,14},{6,10},... | collective-permute-start | bytes 24584 | tf_op jit(solution)/shard_map/ppermute | solution.py:468
  39.1 4.7 %collective-permute-start.12 = (f32[16,128]{1,0:T(8,128)S(1)}, f32[16,128]{1,0:T(8,128)S(1)}, u32[]{:S(2)}, u32[]{:S(2)}) collective-permute-start(f32[16,128]{1,0:T(8,128)S(1)} %add.3.refs_0_), channel_id=1, source_target_pairs={{0,4},{4,0},{8,12},{12,8},{1,5},{5,1},{9,13},{13,9},{2,6},{6,2},{1... | collective-permute-start | bytes 24584 | tf_op jit(solution)/shard_map/ppermute | solution.py:468
  39.1 4.7 %collective-permute-start.11 = (f32[16,128]{1,0:T(8,128)S(1)}, f32[16,128]{1,0:T(8,128)S(1)}, u32[]{:S(2)}, u32[]{:S(2)}) collective-permute-start(f32[16,128]{1,0:T(8,128)S(1)} %add.3.refs_0_), channel_id=1, source_target_pairs={{0,8},{4,12},{8,0},{12,4},{1,9},{5,13},{9,1},{13,5},{2,10},{6,14},... | collective-permute-start | bytes 24584 | tf_op jit(solution)/shard_map/ppermute | solution.py:468
